TPU v7x, 32 devices: a whole 2x2x4 slice. The times are simulated.
32 devices in a mesh: wide: 16 (over z, x, core), tensor: 2 (over y).
Axes of the slice: x: 2, y: 2, z: 4, core: 2. Of those that a mesh axis runs over, the one named last changes fastest.
Arguments:
- tokens: bfloat16 [4, 2, 1024, 1152], P(None, None, ('wide', 'tensor')), may hold values from -6 to 6
- out_grad: bfloat16 [4, 2, 1024, 1152], P(None, None, ('wide', 'tensor')), may hold values from -6 to 6
- doc_lengths: int32 [4, 2, 3], replicated, may hold values from 0 to 1024, as said below
- picture_starts: int32 [4, 2, 4], replicated, may hold values from 0 to 768, as said below
- q_weight: bfloat16 [1152, 1024], P('wide', 'tensor'), may hold values from -0.1875 to 0.1875
- k_weight: bfloat16 [1152, 256], P('wide'), may hold values from -0.1875 to 0.1875
- v_weight: bfloat16 [1152, 256], P('wide'), may hold values from -0.1875 to 0.1875
- out_weight: bfloat16 [1152, 1024], P('wide', 'tensor'), may hold values from -0.1875 to 0.1875
- gate_weight: bfloat16 [1152, 6912], P('wide', 'tensor'), may hold values from -0.1875 to 0.1875
- up_weight: bfloat16 [1152, 6912], P('wide', 'tensor'), may hold values from -0.1875 to 0.1875
- down_weight: bfloat16 [1152, 6912], P('wide', 'tensor'), may hold values from -0.078125 to 0.078125
- attn_in_gain: bfloat16 [1152], P('wide'), may hold values from 0.5 to 1.5
- attn_out_gain: bfloat16 [1152], P('wide'), may hold values from 0.5 to 1.5
- ffn_in_gain: bfloat16 [1152], P('wide'), may hold values from 0.5 to 1.5
- ffn_out_gain: bfloat16 [1152], P('wide'), may hold values from 0.5 to 1.5
- query_gain: bfloat16 [256], P('wide'), may hold values from 0.25 to 1.75
- key_gain: bfloat16 [256], P('wide'), may hold values from 0.25 to 1.75
Outputs:
- output: bfloat16 [4, 2, 1024, 1152], P(None, None, ('wide', 'tensor'))
- input_grad: bfloat16 [4, 2, 1024, 1152], P(None, None, ('wide', 'tensor'))
- q_weight_grad: float32 [1152, 1024], P('wide', 'tensor')
- k_weight_grad: float32 [1152, 256], P('wide')
- v_weight_grad: float32 [1152, 256], P('wide')
- out_weight_grad: float32 [1152, 1024], P('wide', 'tensor')
- gate_weight_grad: float32 [1152, 6912], P('wide', 'tensor')
- up_weight_grad: float32 [1152, 6912], P('wide', 'tensor')
- down_weight_grad: float32 [1152, 6912], P('wide', 'tensor')
- attn_in_gain_grad: float32 [1152], P('wide')
- attn_out_gain_grad: float32 [1152], P('wide')
- ffn_in_gain_grad: float32 [1152], P('wide')
- ffn_out_gain_grad: float32 [1152], P('wide')
- query_gain_grad: float32 [256], P('wide')
- key_gain_grad: float32 [256], P('wide')
Inputs may be any that keep to these rules, and one draw needn't show every extreme that they name: `doc_lengths`: each row sums to 1024; a zero is an empty document; in one sequence, chosen by the seed, the whole sequence is one document. `picture_starts`: picture block i starts within positions i * 256 to (i + 1) * 256 - 256, so blocks never intersect.
All inputs are finite; a program needn't handle non-finite values.
Results may differ from a plain program's by a relative error of at most 0.02.
Values may be sent and summed in bfloat16 or wider, within the bound.
No kernel may reach another device: no remote copies, remote signals or barrier semaphores. Data moves between devices by JAX's collectives and lax.ppermute only.
A program may use at most 256 MiB of HBM per device.

v0:
```python
import jax
import jax.numpy as jnp
from jax import lax
from jax.sharding import PartitionSpec as P

HD = 256
PIC = 256


EPSILON = 1e-06
ROPE_BASE = 1000000.0


def root_norm(values, factor):
    return values * lax.rsqrt(jnp.mean(values * values, axis=-1, keepdims=True) + EPSILON) * factor


def rotary(values, places):
    half_dim = values.shape[-1] // 2
    frequency = ROPE_BASE ** (-2.0 * jnp.arange(half_dim, dtype=jnp.float32) / values.shape[-1])
    angles = places.astype(jnp.float32)[..., None] * frequency
    cosine = jnp.cos(angles)
    sine_part = jnp.sin(angles)
    first_half = values[..., :half_dim]
    second_half = values[..., half_dim:]
    return jnp.concatenate(
        [
            first_half * cosine - second_half * sine_part,
            second_half * cosine + first_half * sine_part,
        ],
        axis=-1,
    )


def layout(lengths, starts, places):
    doc_ends = jnp.cumsum(lengths)
    before = places[:, None] >= doc_ends[None, :]
    doc_ids = jnp.sum(before.astype(jnp.int32), axis=1)
    opening = jnp.max(
        jnp.where(before, doc_ends[None, :], jnp.zeros_like(doc_ends)[None, :]), axis=1
    )
    within = places - opening
    inside = (places[:, None] >= starts[None, :]) & (places[:, None] < starts[None, :] + PIC)
    labels = jnp.arange(1, starts.shape[0] + 1, dtype=jnp.int32)
    pictures = (
        jnp.sum(jnp.where(inside, labels[None, :], jnp.zeros_like(labels)[None, :]), axis=1) - 1
    )
    return (doc_ids, within, pictures)


def allowed_mask(query_places, query_docs, query_pics, key_docs, key_pics):
    key_places = jnp.arange(key_docs.shape[0], dtype=jnp.int32)
    causal = key_places[None, :] <= query_places[:, None]
    shared = (query_pics[:, None] == key_pics[None, :]) & (query_pics[:, None] >= 0)
    return (query_docs[:, None] == key_docs[None, :]) & (causal | shared)


def query_piece(query_raw, factor, places):
    batch_count = query_raw.shape[0]
    count = query_raw.shape[1]
    query_heads = query_raw.reshape(batch_count, count, -1, HD).transpose(0, 2, 1, 3)
    return rotary(root_norm(query_heads, factor), places[:, None, :]) * HD ** (-0.5)


def key_piece(key_raw, factor, places):
    return rotary(root_norm(key_raw, factor), places)


def gated(gate_act, up_act):
    return jax.nn.gelu(gate_act, approximate=True) * up_act


def masked_scores(queries_low, all_keys, allowed):
    scores = jnp.einsum("shqd,skd->shqk", queries_low, all_keys, preferred_element_type=jnp.float32)
    return jnp.where(allowed[:, None], scores, -1e30)


def micro_step(micro_tokens, cotangent_in, lengths, starts, weights):
    (
        q_weight,
        k_weight,
        v_weight,
        out_weight,
        gate_weight,
        up_weight,
        down_weight,
        attn_in_gain,
        attn_out_gain,
        ffn_in_gain,
        ffn_out_gain,
        query_gain,
        key_gain,
    ) = weights
    batch_count = micro_tokens.shape[0]
    own_rows = micro_tokens.shape[1]
    span_len = own_rows * lax.axis_size("tensor")
    seq_len = span_len * lax.axis_size("wide")
    span_start = lax.axis_index("wide") * span_len
    own_start = span_start + lax.axis_index("tensor") * own_rows
    places = jnp.arange(seq_len, dtype=jnp.int32)
    doc_ids, within, pictures = jax.vmap(layout, in_axes=(0, 0, None))(lengths, starts, places)
    span_places = lax.dynamic_slice_in_dim(places, span_start, span_len)
    span_docs = lax.dynamic_slice_in_dim(doc_ids, span_start, span_len, axis=1)
    span_pics = lax.dynamic_slice_in_dim(pictures, span_start, span_len, axis=1)
    span_within = lax.dynamic_slice_in_dim(within, span_start, span_len, axis=1)
    own_within = lax.dynamic_slice_in_dim(within, own_start, own_rows, axis=1)
    allowed = jax.vmap(allowed_mask, in_axes=(None, 0, 0, 0, 0))(
        span_places, span_docs, span_pics, doc_ids, pictures
    )
    inputs = micro_tokens.astype(jnp.float32)
    normed, pull_in = jax.vjp(root_norm, inputs, attn_in_gain.astype(jnp.float32))
    normed_low = normed.astype(jnp.bfloat16)
    span_normed = lax.all_gather(normed_low, "tensor", axis=1, tiled=True)
    query_raw = jnp.einsum("scd,df->scf", span_normed, q_weight, preferred_element_type=jnp.float32)
    queries, pull_query = jax.vjp(
        lambda raw, factor: query_piece(raw, factor, span_within),
        query_raw,
        query_gain.astype(jnp.float32),
    )
    queries_low = queries.astype(jnp.bfloat16)
    key_raw = jnp.einsum("scd,df->scf", normed_low, k_weight, preferred_element_type=jnp.float32)
    key_rows, pull_key = jax.vjp(
        lambda raw, factor: key_piece(raw, factor, own_within),
        key_raw,
        key_gain.astype(jnp.float32),
    )
    key_low = key_rows.astype(jnp.bfloat16)
    value_low = jnp.einsum(
        "scd,df->scf", normed_low, v_weight, preferred_element_type=jnp.float32
    ).astype(jnp.bfloat16)
    all_keys, all_values = (
        lax.all_gather(key_low, ("wide", "tensor"), axis=1, tiled=True),
        lax.all_gather(value_low, ("wide", "tensor"), axis=1, tiled=True),
    )
    scores = masked_scores(queries_low, all_keys, allowed)
    row_top = jnp.max(scores, axis=-1, keepdims=True)
    row_total = jnp.sum(jnp.exp(scores - row_top), axis=-1, keepdims=True)
    log_total = row_top + jnp.log(row_total)
    attn_probs = jnp.exp(scores - log_total)
    mixed = jnp.einsum(
        "shqk,skd->shqd",
        attn_probs.astype(jnp.bfloat16),
        all_values,
        preferred_element_type=jnp.float32,
    )
    attended = mixed.astype(jnp.bfloat16).transpose(0, 2, 1, 3).reshape(batch_count, span_len, -1)
    branch_part = jnp.einsum(
        "scf,df->scd", attended, out_weight, preferred_element_type=jnp.float32
    )
    branch = lax.psum_scatter(branch_part, "tensor", scatter_dimension=1, tiled=True)
    lifted, pull_lift = jax.vjp(root_norm, branch, attn_out_gain.astype(jnp.float32))
    middle = inputs + lifted
    ffn_input, pull_ffn = jax.vjp(root_norm, middle, ffn_in_gain.astype(jnp.float32))
    span_ffn = lax.all_gather(ffn_input.astype(jnp.bfloat16), "tensor", axis=1, tiled=True)
    gate_act = jnp.einsum("scd,df->scf", span_ffn, gate_weight, preferred_element_type=jnp.float32)
    up_act = jnp.einsum("scd,df->scf", span_ffn, up_weight, preferred_element_type=jnp.float32)
    hidden, pull_hidden = jax.vjp(gated, gate_act, up_act)
    hidden_low = hidden.astype(jnp.bfloat16)
    second_part = jnp.einsum(
        "scf,df->scd", hidden_low, down_weight, preferred_element_type=jnp.float32
    )
    second = lax.psum_scatter(
        second_part.astype(jnp.bfloat16), "tensor", scatter_dimension=1, tiled=True
    ).astype(jnp.float32)
    closing, pull_close = jax.vjp(root_norm, second, ffn_out_gain.astype(jnp.float32))
    output = middle + closing
    cotangent = cotangent_in.astype(jnp.float32)
    grad_second, grad_ffn_out = pull_close(cotangent)
    span_grad_second = lax.all_gather(
        grad_second.astype(jnp.bfloat16), "tensor", axis=1, tiled=True
    )
    grad_down = jnp.einsum(
        "scd,scf->df", span_grad_second, hidden_low, preferred_element_type=jnp.float32
    )
    grad_hidden = jnp.einsum(
        "scd,df->scf", span_grad_second, down_weight, preferred_element_type=jnp.float32
    )
    grad_gate_act, grad_up_act = pull_hidden(grad_hidden)
    gate_grad_low = grad_gate_act.astype(jnp.bfloat16)
    up_grad_low = grad_up_act.astype(jnp.bfloat16)
    grad_gate = jnp.einsum(
        "scd,scf->df", span_ffn, gate_grad_low, preferred_element_type=jnp.float32
    )
    grad_up = jnp.einsum("scd,scf->df", span_ffn, up_grad_low, preferred_element_type=jnp.float32)
    ffn_part = jnp.einsum(
        "scf,df->scd", gate_grad_low, gate_weight, preferred_element_type=jnp.float32
    ) + jnp.einsum("scf,df->scd", up_grad_low, up_weight, preferred_element_type=jnp.float32)
    grad_ffn_input = lax.psum_scatter(
        ffn_part.astype(jnp.bfloat16), "tensor", scatter_dimension=1, tiled=True
    ).astype(jnp.float32)
    grad_middle_norm, grad_ffn_in = pull_ffn(grad_ffn_input)
    grad_middle = cotangent + grad_middle_norm
    grad_branch, grad_attn_out = pull_lift(grad_middle)
    span_grad_branch = lax.all_gather(
        grad_branch.astype(jnp.bfloat16), "tensor", axis=1, tiled=True
    )
    grad_out = jnp.einsum(
        "scd,scf->df", span_grad_branch, attended, preferred_element_type=jnp.float32
    )
    grad_attended = jnp.einsum(
        "scd,df->scf", span_grad_branch, out_weight, preferred_element_type=jnp.float32
    )
    grad_mixed = (
        grad_attended.reshape(batch_count, span_len, -1, HD)
        .transpose(0, 2, 1, 3)
        .astype(jnp.bfloat16)
    )
    again_scores = masked_scores(queries_low, all_keys, allowed)
    again_probs = jnp.exp(again_scores - log_total)
    grad_probs = jnp.einsum(
        "shqd,skd->shqk", grad_mixed, all_values, preferred_element_type=jnp.float32
    )
    grad_scores = again_probs * (
        grad_probs - jnp.sum(again_probs * grad_probs, axis=-1, keepdims=True)
    )
    grad_scores_low = grad_scores.astype(jnp.bfloat16)
    grad_queries = jnp.einsum(
        "shqk,skd->shqd", grad_scores_low, all_keys, preferred_element_type=jnp.float32
    )
    grad_keys_all = jnp.einsum(
        "shqk,shqd->skd", grad_scores_low, queries_low, preferred_element_type=jnp.float32
    )
    grad_values_all = jnp.einsum(
        "shqk,shqd->skd",
        again_probs.astype(jnp.bfloat16),
        grad_mixed,
        preferred_element_type=jnp.float32,
    )
    grad_keys, grad_values = (
        lax.psum_scatter(grad_keys_all, ("wide", "tensor"), scatter_dimension=1, tiled=True),
        lax.psum_scatter(grad_values_all, ("wide", "tensor"), scatter_dimension=1, tiled=True),
    )
    grad_key_raw, grad_key_gain = pull_key(grad_keys)
    key_grad_low = grad_key_raw.astype(jnp.bfloat16)
    value_grad_low = grad_values.astype(jnp.bfloat16)
    grad_query_raw, grad_query_gain = pull_query(grad_queries)
    query_grad_low = grad_query_raw.astype(jnp.bfloat16)
    grad_query = jnp.einsum(
        "scd,scf->df", span_normed, query_grad_low, preferred_element_type=jnp.float32
    )
    grad_key = jnp.einsum(
        "scd,scf->df", normed_low, key_grad_low, preferred_element_type=jnp.float32
    )
    grad_value = jnp.einsum(
        "scd,scf->df", normed_low, value_grad_low, preferred_element_type=jnp.float32
    )
    query_part = jnp.einsum(
        "scf,df->scd", query_grad_low, q_weight, preferred_element_type=jnp.float32
    )
    grad_normed = (
        lax.psum_scatter(
            query_part.astype(jnp.bfloat16), "tensor", scatter_dimension=1, tiled=True
        ).astype(jnp.float32)
        + jnp.einsum("scf,df->scd", key_grad_low, k_weight, preferred_element_type=jnp.float32)
        + jnp.einsum("scf,df->scd", value_grad_low, v_weight, preferred_element_type=jnp.float32)
    )
    grad_inputs_norm, grad_attn_in = pull_in(grad_normed)
    grad_inputs = grad_middle + grad_inputs_norm
    grad_terms = (
        grad_query,
        grad_key,
        grad_value,
        grad_out,
        grad_gate,
        grad_up,
        grad_down,
        grad_attn_in,
        grad_attn_out,
        grad_ffn_in,
        grad_ffn_out,
        grad_query_gain,
        grad_key_gain,
    )
    return (output, grad_inputs, grad_terms)


def body(
    tokens,
    out_grad,
    doc_lengths,
    picture_starts,
    q_weight,
    k_weight,
    v_weight,
    out_weight,
    gate_weight,
    up_weight,
    down_weight,
    attn_in_gain,
    attn_out_gain,
    ffn_in_gain,
    ffn_out_gain,
    query_gain,
    key_gain,
):
    shards = (
        q_weight,
        k_weight,
        v_weight,
        out_weight,
        gate_weight,
        up_weight,
        down_weight,
        attn_in_gain,
        attn_out_gain,
        ffn_in_gain,
        ffn_out_gain,
        query_gain,
        key_gain,
    )
    micro_count = tokens.shape[0]
    per_pass = micro_count // micro_count
    outputs = []
    input_grads = []
    totals = None
    for turn_index in range(micro_count):
        gathered = (
            lax.all_gather(shards[0], "wide", axis=0, tiled=True),
            lax.all_gather(shards[1], "wide", axis=0, tiled=True),
            lax.all_gather(shards[2], "wide", axis=0, tiled=True),
            lax.all_gather(shards[3], "wide", axis=0, tiled=True),
            lax.all_gather(shards[4], "wide", axis=0, tiled=True),
            lax.all_gather(shards[5], "wide", axis=0, tiled=True),
            lax.all_gather(shards[6], "wide", axis=0, tiled=True),
            lax.all_gather(shards[7], "wide", axis=0, tiled=True),
            lax.all_gather(shards[8], "wide", axis=0, tiled=True),
            lax.all_gather(shards[9], "wide", axis=0, tiled=True),
            lax.all_gather(shards[10], "wide", axis=0, tiled=True),
            lax.all_gather(shards[11], "wide", axis=0, tiled=True),
            lax.all_gather(shards[12], "wide", axis=0, tiled=True),
        )
        grad_sums = tuple((jnp.zeros(item_array.shape, jnp.float32) for item_array in gathered))
        index_micro = turn_index * per_pass
        produced, backed, grad_terms = micro_step(
            tokens[index_micro],
            out_grad[index_micro],
            doc_lengths[index_micro],
            picture_starts[index_micro],
            gathered,
        )
        outputs.append(produced)
        input_grads.append(backed)
        grad_sums = tuple((right_side for right_side in grad_terms))
        reduced = lax.psum_scatter(grad_sums, "wide", scatter_dimension=0, tiled=True)
        totals = (
            reduced
            if totals is None
            else tuple((left_side + right_side for left_side, right_side in zip(totals, reduced)))
        )
    shared = (
        lax.psum(totals[1].astype(jnp.bfloat16), "tensor").astype(jnp.float32),
        lax.psum(totals[2].astype(jnp.bfloat16), "tensor").astype(jnp.float32),
        lax.psum(totals[7].astype(jnp.bfloat16), "tensor").astype(jnp.float32),
        lax.psum(totals[8].astype(jnp.bfloat16), "tensor").astype(jnp.float32),
        lax.psum(totals[9].astype(jnp.bfloat16), "tensor").astype(jnp.float32),
        lax.psum(totals[10].astype(jnp.bfloat16), "tensor").astype(jnp.float32),
        lax.psum(totals[11].astype(jnp.bfloat16), "tensor").astype(jnp.float32),
        lax.psum(totals[12].astype(jnp.bfloat16), "tensor").astype(jnp.float32),
    )
    return (
        jnp.stack(outputs).astype(jnp.bfloat16),
        jnp.stack(input_grads).astype(jnp.bfloat16),
        totals[0],
        shared[0],
        shared[1],
        totals[3],
        totals[4],
        totals[5],
        totals[6],
        shared[2],
        shared[3],
        shared[4],
        shared[5],
        shared[6],
        shared[7],
    )


def solution(mesh):
    placed = (
        P(None, None, ("wide", "tensor"), None),
        P(None, None, ("wide", "tensor"), None),
        P(),
        P(),
        P("wide", "tensor"),
        P("wide", None),
        P("wide", None),
        P("wide", "tensor"),
        P("wide", "tensor"),
        P("wide", "tensor"),
        P("wide", "tensor"),
        P("wide"),
        P("wide"),
        P("wide"),
        P("wide"),
        P("wide"),
        P("wide"),
    )
    return jax.shard_map(
        body,
        mesh=mesh,
        in_specs=placed,
        out_specs=(
            P(None, None, ("wide", "tensor"), None),
            P(None, None, ("wide", "tensor"), None),
            P("wide", "tensor"),
            P("wide", None),
            P("wide", None),
            P("wide", "tensor"),
            P("wide", "tensor"),
            P("wide", "tensor"),
            P("wide", "tensor"),
            P("wide"),
            P("wide"),
            P("wide"),
            P("wide"),
            P("wide"),
            P("wide"),
        ),
        check_vma=False,
    )
```

profile of v0, /device:TPU:0, one launch (start us, length us, event | category | flops | bytes accessed | tf_op | source)
XLA Modules:
  0.0 3034.8 jit_solution(16705043628471772892)
XLA Ops:
  15.7 63.3 %all-reduce.32 = (bf16[1152]{0:T(1024)(128)(2,1)S(1)}, bf16[256]{0:T(256)(128)(2,1)S(1)}, bf16[256]{0:T(256)(128)(2,1)S(1)}, bf16[1152]{0:T(1024)(128)(2,1)}, bf...) all-reduce(bf16[1152]{0:T(1024)(128)(2,1)S(1)} %dynamic-update-slice, ...), channel_id=1, replica_groups=mesh['wide'=16,'tensor'=2] {'wide'}, use_global_device_ids=true, to_apply=%add.16 | all-reduce | flops 5120 | bytes 20480
  80.9 19.3 all_gather.154
  105.3 20.6 all_gather.157
  134.6 6.8 all_gather.75
  141.4 7.7 all_gather.167
  173.0 41.7 %all-gather.34.cloned.1.call-done = bf16[2,1024,256]{2,1,0:T(8,128)(2,1)} async-done(((bf16[2,32,256]{2,1,0:T(8,128)(2,1)}), bf16[2,1024,256]{2,1,0:T(8,128)(2,1)}) %all-gather.34.cloned.1.call-update) | async-done | bytes 1048592 | tf_op jit(solution)/shard_map/all_gather | solution.py:133
  216.4 37.8 %all-gather.20.cloned.1.call-done = bf16[1152,512]{1,0:T(8,128)(2,1)} async-done(((bf16[72,512]{1,0:T(8,128)(2,1)}), bf16[1152,512]{1,0:T(8,128)(2,1)}) %all-gather.20.cloned.1.call-update) | async-done | bytes 1179664 | tf_op jit(solution)/shard_map/all_gather | solution.py:321
  256.9 52.9 %all-gather.16.cloned.1.call-done = bf16[2,1024,256]{2,1,0:T(8,128)(2,1)} async-done(((bf16[2,32,256]{2,1,0:T(8,128)(2,1)}), bf16[2,1024,256]{2,1,0:T(8,128)(2,1)}) %all-gather.16.cloned.1.call-update) | async-done | bytes 1048592 | tf_op jit(solution)/shard_map/all_gather | solution.py:132
  313.4 52.0 %all-gather.18.cloned.1.call-done = bf16[2,1024,256]{2,1,0:T(8,128)(2,1)} async-done(((bf16[2,32,256]{2,1,0:T(8,128)(2,1)}), bf16[2,1024,256]{2,1,0:T(8,128)(2,1)}) %all-gather.18.cloned.1.call-update) | async-done | bytes 1048592 | tf_op jit(solution)/shard_map/all_gather | solution.py:133
  371.4 49.8 %all-gather.28.cloned.1.call-done = bf16[2,1024,256]{2,1,0:T(8,128)(2,1)} async-done(((bf16[2,32,256]{2,1,0:T(8,128)(2,1)}), bf16[2,1024,256]{2,1,0:T(8,128)(2,1)}) %all-gather.28.cloned.1.call-update) | async-done | bytes 1048592 | tf_op jit(solution)/shard_map/all_gather | solution.py:132
  425.0 52.0 %all-gather.30.cloned.1.call-done = bf16[2,1024,256]{2,1,0:T(8,128)(2,1)} async-done(((bf16[2,32,256]{2,1,0:T(8,128)(2,1)}), bf16[2,1024,256]{2,1,0:T(8,128)(2,1)}) %all-gather.30.cloned.1.call-update) | async-done | bytes 1048592 | tf_op jit(solution)/shard_map/all_gather | solution.py:133
  482.7 50.0 %all-gather.36.cloned.1.call-done = bf16[2,1024,256]{2,1,0:T(8,128)(2,1)} async-done(((bf16[2,32,256]{2,1,0:T(8,128)(2,1)}), bf16[2,1024,256]{2,1,0:T(8,128)(2,1)}) %all-gather.36.cloned.1.call-update) | async-done | bytes 1048592 | tf_op jit(solution)/shard_map/all_gather | solution.py:132
  536.6 51.7 %all-gather.38.cloned.1.call-done = bf16[2,1024,256]{2,1,0:T(8,128)(2,1)} async-done(((bf16[2,32,256]{2,1,0:T(8,128)(2,1)}), bf16[2,1024,256]{2,1,0:T(8,128)(2,1)}) %all-gather.38.cloned.1.call-update) | async-done | bytes 1048592 | tf_op jit(solution)/shard_map/all_gather | solution.py:133
  597.9 7.5 reduce-scatter.46.cloned.1.call-done
  607.1 16.4 reduce-scatter.38.cloned.1.call-done
  625.2 16.6 reduce-scatter.42.cloned.1.call-done
  643.3 16.5 reduce-scatter.50.cloned.1.call-done
  689.9 44.1 %all-gather.22.cloned.1.call-done = bf16[1152,3456]{1,0:T(8,128)(2,1)} async-done(((bf16[72,3456]{1,0:T(8,128)(2,1)}), bf16[1152,3456]{1,0:T(8,128)(2,1)}) %all-gather.22.cloned.1.call-update) | async-done | bytes 7962640 | tf_op jit(solution)/shard_map/all_gather | solution.py:322
  740.0 66.6 %all-gather.24.cloned.1.call-done = bf16[1152,3456]{1,0:T(8,128)(2,1)} async-done(((bf16[72,3456]{1,0:T(8,128)(2,1)}), bf16[1152,3456]{1,0:T(8,128)(2,1)}) %all-gather.24.cloned.1.call-update) | async-done | bytes 7962640 | tf_op jit(solution)/shard_map/all_gather | solution.py:323
  806.6 6.9 multiply_convert_fusion.4
  813.5 65.7 %all-gather.26.cloned.1.call-done = bf16[1152,3456]{1,0:T(8,128)(2,1)} async-done(((bf16[72,3456]{1,0:T(8,128)(2,1)}), bf16[1152,3456]{1,0:T(8,128)(2,1)}) %all-gather.26.cloned.1.call-update) | async-done | bytes 7962640 | tf_op jit(solution)/shard_map/all_gather | solution.py:324
  879.2 6.7 fusion.90
  905.8 6.8 multiply_convert_fusion.7
  921.7 6.8 multiply_convert_fusion.5
  975.9 6.6 fusion.125
  995.0 6.5 fusion.96
  1001.8 6.6 fusion.118
  1020.8 6.6 fusion.99
  1027.5 6.6 fusion.132
  1040.5 6.5 fusion.93
  1047.2 12.2 reduce-scatter.78.cloned.1.call-done
  1067.9 6.7 all_gather.184
  1090.5 7.2 all_gather.186
  1103.3 6.8 all_gather.180
  1144.8 71.0 %reduce-scatter.74.cloned.1.call-done = f32[2,32,256]{2,1,0:T(8,128)} async-done(((f32[2,1024,256]{2,1,0:T(8,128)}), f32[2,32,256]{2,1,0:T(8,128)}) %reduce-scatter.74.cloned.1.call-update) | async-done | bytes 65552 | tf_op jit(solution)/shard_map/reduce_scatter | solution.py:230
  1215.8 135.7 %reduce-scatter.66.cloned.1.call-done = f32[2,32,256]{2,1,0:T(8,128)} async-done(((f32[2,1024,256]{2,1,0:T(8,128)}), f32[2,32,256]{2,1,0:T(8,128)}) %reduce-scatter.66.cloned.1.call-update) | async-done | bytes 65552 | tf_op jit(solution)/shard_map/reduce_scatter | solution.py:230
  1351.5 135.9 %reduce-scatter.82.cloned.1.call-done = f32[2,32,256]{2,1,0:T(8,128)} async-done(((f32[2,1024,256]{2,1,0:T(8,128)}), f32[2,32,256]{2,1,0:T(8,128)}) %reduce-scatter.82.cloned.1.call-update) | async-done | bytes 65552 | tf_op jit(solution)/shard_map/reduce_scatter | solution.py:230
  1489.4 133.5 %reduce-scatter.58.cloned.1.call-done = f32[2,32,256]{2,1,0:T(8,128)} async-done(((f32[2,1024,256]{2,1,0:T(8,128)}), f32[2,32,256]{2,1,0:T(8,128)}) %reduce-scatter.58.cloned.1.call-update) | async-done | bytes 65552 | tf_op jit(solution)/shard_map/reduce_scatter | solution.py:230
  1630.1 128.5 %reduce-scatter.60.cloned.1.call-done = f32[2,32,256]{2,1,0:T(8,128)} async-done(((f32[2,1024,256]{2,1,0:T(8,128)}), f32[2,32,256]{2,1,0:T(8,128)}) %reduce-scatter.60.cloned.1.call-update) | async-done | bytes 65552 | tf_op jit(solution)/shard_map/reduce_scatter | solution.py:231
  1760.8 133.4 %reduce-scatter.68.cloned.1.call-done = f32[2,32,256]{2,1,0:T(8,128)} async-done(((f32[2,1024,256]{2,1,0:T(8,128)}), f32[2,32,256]{2,1,0:T(8,128)}) %reduce-scatter.68.cloned.1.call-update) | async-done | bytes 65552 | tf_op jit(solution)/shard_map/reduce_scatter | solution.py:231
  1896.9 133.0 %reduce-scatter.76.cloned.1.call-done = f32[2,32,256]{2,1,0:T(8,128)} async-done(((f32[2,1024,256]{2,1,0:T(8,128)}), f32[2,32,256]{2,1,0:T(8,128)}) %reduce-scatter.76.cloned.1.call-update) | async-done | bytes 65552 | tf_op jit(solution)/shard_map/reduce_scatter | solution.py:231
  2032.7 132.9 %reduce-scatter.84.cloned.1.call-done = f32[2,32,256]{2,1,0:T(8,128)} async-done(((f32[2,1024,256]{2,1,0:T(8,128)}), f32[2,32,256]{2,1,0:T(8,128)}) %reduce-scatter.84.cloned.1.call-update) | async-done | bytes 65552 | tf_op jit(solution)/shard_map/reduce_scatter | solution.py:231
  2169.0 8.0 reduce-scatter.64.cloned.1.call-done
  2178.9 12.9 reduce-scatter.56.cloned.1.call-done
  2193.8 12.2 reduce-scatter.72.cloned.1.call-done
  2208.0 12.2 reduce-scatter.80.cloned.1.call-done
  2226.7 62.1 %all-reduce.31 = (bf16[1152]{0:T(1024)(128)(2,1)S(1)}, bf16[1152]{0:T(1024)(128)(2,1)S(1)}, bf16[1152]{0:T(1024)(128)(2,1)S(1)}, bf16[1152]{0:T(1024)(128)(2,1)S...) all-reduce(f32[1152]{0:T(1024)S(1)} %add_add_fusion.27, ...), channel_id=72, replica_groups=mesh['wide'=16,'tensor'=2] {'wide'}, use_global_device_ids=true, to_apply=%region_131.132.clone | all-reduce | flops 5120 | bytes 30720
  2293.8 48.7 %reduce-scatter.90.cloned.1.call-done = f32[72,256]{1,0:T(8,128)} async-done(((f32[1152,256]{1,0:T(8,128)}), f32[72,256]{1,0:T(8,128)}) %reduce-scatter.90.cloned.1.call-update) | async-done | bytes 73744 | tf_op jit(solution)/shard_map/reduce_scatter | solution.py:344
  2353.6 7.8 convolution_bitcast_fusion.11
  2361.4 7.9 fusion.8
  2369.4 7.8 fusion.7
  2377.3 14.0 fusion.6
  2392.4 7.8 convolution_bitcast_fusion.7
  2400.2 7.9 fusion.5
  2408.1 7.7 fusion.4
  2415.9 13.3 fusion.3
  2430.4 7.8 convolution_bitcast_fusion.3
  2438.2 7.9 fusion.2
  2446.2 8.1 fusion.1
  2454.3 13.6 fusion
  2481.2 20.0 reduce-scatter.92.cloned.1.call-done
  2501.2 175.5 %reduce-scatter.94.cloned.1.call-done = f32[72,3456]{1,0:T(8,128)} async-done(((f32[1152,3456]{1,0:T(8,128)}), f32[72,3456]{1,0:T(8,128)}) %reduce-scatter.94.cloned.1.call-update) | async-done | bytes 995344
  2676.7 175.6 %reduce-scatter.96.cloned.1.call-done = f32[72,3456]{1,0:T(8,128)} async-done(((f32[1152,3456]{1,0:T(8,128)}), f32[72,3456]{1,0:T(8,128)}) %reduce-scatter.96.cloned.1.call-update) | async-done | bytes 995344
  2852.3 175.5 %reduce-scatter.98.cloned.1.call-done = f32[72,3456]{1,0:T(8,128)} async-done(((f32[1152,3456]{1,0:T(8,128)}), f32[72,3456]{1,0:T(8,128)}) %reduce-scatter.98.cloned.1.call-update) | async-done | bytes 995344
  (1139 shorter events, 355.9 us)
Async XLA Ops:
  7.2 158.7 %all-gather.14.cloned.1.call-start = ((), (), s32[]{:S(2)}) async-start(), calls=%async_computation.31 | async-start | bytes 1253376 | tf_op jit(solution)/shard_map/all_gather | solution.py:318
  7.9 162.8 %all-gather.32.cloned.1.call-start = ((), (), s32[]{:S(2)}) async-start(), calls=%async_computation.44 | async-start | bytes 1081344 | tf_op jit(solution)/shard_map/all_gather | solution.py:132
  101.9 1524.3 %copy-start.45 = (bf16[2,32,1152]{2,1,0:T(8,128)(2,1)}, bf16[2,32,1152]{2,1,0:T(8,128)(2,1)S(1)}, u32[]{:S(2)}) copy-start(bf16[2,32,1152]{2,1,0:T(8,128)(2,1)S(1)} %get-tuple-element.159) | copy-start | bytes 442372
  105.3 109.4 %all-gather.34.cloned.1.call-start = ((), (), s32[]{:S(2)}) async-start(), calls=%async_computation.45 | async-start | bytes 1081344 | tf_op jit(solution)/shard_map/all_gather | solution.py:133
  126.8 127.3 %all-gather.20.cloned.1.call-start = ((), (), s32[]{:S(2)}) async-start(), calls=%async_computation.34 | async-start | bytes 1253376 | tf_op jit(solution)/shard_map/all_gather | solution.py:321
  127.4 182.3 %all-gather.16.cloned.1.call-start = ((), (), s32[]{:S(2)}) async-start(), calls=%async_computation.32 | async-start | bytes 1081344 | tf_op jit(solution)/shard_map/all_gather | solution.py:132
  130.3 235.1 %all-gather.18.cloned.1.call-start = ((), (), s32[]{:S(2)}) async-start(), calls=%async_computation.33 | async-start | bytes 1081344 | tf_op jit(solution)/shard_map/all_gather | solution.py:133
  131.2 290.0 %all-gather.28.cloned.1.call-start = ((), (), s32[]{:S(2)}) async-start(), calls=%async_computation.40 | async-start | bytes 1081344 | tf_op jit(solution)/shard_map/all_gather | solution.py:132
  131.9 345.0 %all-gather.30.cloned.1.call-start = ((), (), s32[]{:S(2)}) async-start(), calls=%async_computation.41 | async-start | bytes 1081344 | tf_op jit(solution)/shard_map/all_gather | solution.py:133
  132.9 399.9 %all-gather.36.cloned.1.call-start = ((), (), s32[]{:S(2)}) async-start(), calls=%async_computation.48 | async-start | bytes 1081344 | tf_op jit(solution)/shard_map/all_gather | solution.py:132
  133.6 454.8 %all-gather.38.cloned.1.call-start = ((), (), s32[]{:S(2)}) async-start(), calls=%async_computation.49 | async-start | bytes 1081344 | tf_op jit(solution)/shard_map/all_gather | solution.py:133
  134.5 471.0 %reduce-scatter.46.cloned.1.call-start = ((), (), s32[]{:S(2)}) async-start(), calls=%async_computation.46 | async-start | bytes 884736 | tf_op jit(solution)/shard_map/reduce_scatter | solution.py:150
  256.8 366.8 %reduce-scatter.38.cloned.1.call-start = ((), (), s32[]{:S(2)}) async-start(), calls=%async_computation.35 | async-start | bytes 884736 | tf_op jit(solution)/shard_map/reduce_scatter | solution.py:150
  369.3 272.4 %reduce-scatter.42.cloned.1.call-start = ((), (), s32[]{:S(2)}) async-start(), calls=%async_computation.42 | async-start | bytes 884736 | tf_op jit(solution)/shard_map/reduce_scatter | solution.py:150
  480.9 178.9 %reduce-scatter.50.cloned.1.call-start = ((), (), s32[]{:S(2)}) async-start(), calls=%async_computation.50 | async-start | bytes 884736 | tf_op jit(solution)/shard_map/reduce_scatter | solution.py:150
  592.3 141.7 %all-gather.22.cloned.1.call-start = ((), (), s32[]{:S(2)}) async-start(), calls=%async_computation.36 | async-start | bytes 8460288 | tf_op jit(solution)/shard_map/all_gather | solution.py:322
  592.9 213.7 %all-gather.24.cloned.1.call-start = ((), (), s32[]{:S(2)}) async-start(), calls=%async_computation.37 | async-start | bytes 8460288 | tf_op jit(solution)/shard_map/all_gather | solution.py:323
  593.5 285.7 %all-gather.26.cloned.1.call-start = ((), (), s32[]{:S(2)}) async-start(), calls=%async_computation.38 | async-start | bytes 8460288 | tf_op jit(solution)/shard_map/all_gather | solution.py:324
  594.0 338.9 %reduce-scatter.52.cloned.1.call-start = ((), (), s32[]{:S(2)}) async-start(), calls=%async_computation.51 | async-start | bytes 442368 | tf_op jit(solution)/shard_map/reduce_scatter | solution.py:162
  886.0 49.1 %reduce-scatter.44.cloned.1.call-start = ((), (), s32[]{:S(2)}) async-start(), calls=%async_computation.43 | async-start | bytes 442368 | tf_op jit(solution)/shard_map/reduce_scatter | solution.py:162
  900.9 35.7 %reduce-scatter.40.cloned.1.call-start = ((), (), s32[]{:S(2)}) async-start(), calls=%async_computation.39 | async-start | bytes 442368 | tf_op jit(solution)/shard_map/reduce_scatter | solution.py:162
  916.8 26.5 reduce-scatter.48.cloned.1.call-start
  932.7 114.4 %reduce-scatter.54.cloned.1.call-start = ((), (), s32[]{:S(2)}) async-start(), calls=%async_computation.52 | async-start | bytes 442368 | tf_op jit(solution)/shard_map/reduce_scatter | solution.py:188
  969.9 77.3 %reduce-scatter.70.cloned.1.call-start = ((), (), s32[]{:S(2)}) async-start(), calls=%async_computation.60 | async-start | bytes 442368 | tf_op jit(solution)/shard_map/reduce_scatter | solution.py:188
  1001.6 45.6 %reduce-scatter.62.cloned.1.call-start = ((), (), s32[]{:S(2)}) async-start(), calls=%async_computation.56 | async-start | bytes 442368 | tf_op jit(solution)/shard_map/reduce_scatter | solution.py:188
  1027.4 31.9 %reduce-scatter.78.cloned.1.call-start = ((), (), s32[]{:S(2)}) async-start(), calls=%async_computation.64 | async-start | bytes 442368 | tf_op jit(solution)/shard_map/reduce_scatter | solution.py:188
  1047.0 168.8 %reduce-scatter.74.cloned.1.call-start = ((), (), s32[]{:S(2)}) async-start(), calls=%async_computation.62 | async-start | bytes 2162688 | tf_op jit(solution)/shard_map/reduce_scatter | solution.py:230
  1078.7 272.8 %reduce-scatter.66.cloned.1.call-start = ((), (), s32[]{:S(2)}) async-start(), calls=%async_computation.58 | async-start | bytes 2162688 | tf_op jit(solution)/shard_map/reduce_scatter | solution.py:230
  1090.4 397.0 %reduce-scatter.82.cloned.1.call-start = ((), (), s32[]{:S(2)}) async-start(), calls=%async_computation.66 | async-start | bytes 2162688 | tf_op jit(solution)/shard_map/reduce_scatter | solution.py:230
  1103.3 519.7 %reduce-scatter.58.cloned.1.call-start = ((), (), s32[]{:S(2)}) async-start(), calls=%async_computation.54 | async-start | bytes 2162688 | tf_op jit(solution)/shard_map/reduce_scatter | solution.py:230
  1115.6 643.0 %reduce-scatter.60.cloned.1.call-start = ((), (), s32[]{:S(2)}) async-start(), calls=%async_computation.55 | async-start | bytes 2162688 | tf_op jit(solution)/shard_map/reduce_scatter | solution.py:231
  1119.4 774.8 %reduce-scatter.68.cloned.1.call-start = ((), (), s32[]{:S(2)}) async-start(), calls=%async_computation.59 | async-start | bytes 2162688 | tf_op jit(solution)/shard_map/reduce_scatter | solution.py:231
  1123.2 906.7 %reduce-scatter.76.cloned.1.call-start = ((), (), s32[]{:S(2)}) async-start(), calls=%async_computation.63 | async-start | bytes 2162688 | tf_op jit(solution)/shard_map/reduce_scatter | solution.py:231
  1126.1 1039.5 %reduce-scatter.84.cloned.1.call-start = ((), (), s32[]{:S(2)}) async-start(), calls=%async_computation.67 | async-start | bytes 2162688 | tf_op jit(solution)/shard_map/reduce_scatter | solution.py:231
  1129.3 1047.7 %reduce-scatter.64.cloned.1.call-start = ((), (), s32[]{:S(2)}) async-start(), calls=%async_computation.57 | async-start | bytes 442368 | tf_op jit(solution)/shard_map/reduce_scatter | solution.py:251
  1137.6 1054.2 %reduce-scatter.56.cloned.1.call-start = ((), (), s32[]{:S(2)}) async-start(), calls=%async_computation.53 | async-start | bytes 442368 | tf_op jit(solution)/shard_map/reduce_scatter | solution.py:251
  1139.0 1067.0 %reduce-scatter.72.cloned.1.call-start = ((), (), s32[]{:S(2)}) async-start(), calls=%async_computation.61 | async-start | bytes 442368 | tf_op jit(solution)/shard_map/reduce_scatter | solution.py:251
  1139.2 348.2 %copy-start.290 = (f32[128]{0:T(128)S(1)}, f32[128]{0:T(128)}, u32[]{:S(2)}) copy-start(f32[128]{0:T(128)} %copy-done.289) | copy-start | bytes 1540
  1140.5 348.2 %copy-start.176 = (f32[2,32,256]{2,1,0:T(8,128)S(1)}, f32[2,32,256]{2,1,0:T(8,128)}, u32[]{:S(2)}) copy-start(f32[2,32,256]{2,1,0:T(8,128)} %copy-done.175) | copy-start | bytes 196612
  1140.5 348.3 %copy-start.279 = (f32[256]{0:T(256)S(1)}, f32[256]{0:T(256)}, u32[]{:S(2)}) copy-start(f32[256]{0:T(256)} %copy-done.278) | copy-start | bytes 3076
  1140.5 348.3 %copy-start.287 = (f32[2,32]{1,0:T(2,128)S(1)}, f32[2,32]{1,0:T(2,128)}, u32[]{:S(2)}) copy-start(f32[2,32]{1,0:T(2,128)} %copy-done.286) | copy-start | bytes 772
  1140.5 348.9 %copy-start.318 = (f32[2,32]{1,0:T(2,128)S(1)}, f32[2,32]{1,0:T(2,128)}, u32[]{:S(2)}) copy-start(f32[2,32]{1,0:T(2,128)} %copy-done.317) | copy-start | bytes 772
  1140.5 482.5 %copy-start.306 = (f32[2,32]{1,0:T(2,128)S(1)}, f32[2,32]{1,0:T(2,128)}, u32[]{:S(2)}) copy-start(f32[2,32]{1,0:T(2,128)} %copy-done.305) | copy-start | bytes 772
  1140.5 483.4 %copy-start.170 = (f32[2,32,256]{2,1,0:T(8,128)S(1)}, f32[2,32,256]{2,1,0:T(8,128)}, u32[]{:S(2)}) copy-start(f32[2,32,256]{2,1,0:T(8,128)} %copy-done.169) | copy-start | bytes 196612
  1140.5 483.4 %copy-start.172 = (f32[2,32,256]{2,1,0:T(8,128)S(1)}, f32[2,32,256]{2,1,0:T(8,128)}, u32[]{:S(2)}) copy-start(f32[2,32,256]{2,1,0:T(8,128)} %copy-done.171) | copy-start | bytes 196612
  1140.5 483.4 %copy-start.174 = (f32[2,32,256]{2,1,0:T(8,128)S(1)}, f32[2,32,256]{2,1,0:T(8,128)}, u32[]{:S(2)}) copy-start(f32[2,32,256]{2,1,0:T(8,128)} %copy-done.173) | copy-start | bytes 196612
  1140.5 483.4 %copy-start.281 = (f32[2,32]{1,0:T(2,128)S(1)}, f32[2,32]{1,0:T(2,128)}, u32[]{:S(2)}) copy-start(f32[2,32]{1,0:T(2,128)} %copy-done.280) | copy-start | bytes 772
  1140.5 483.4 %copy-start.283 = (f32[2,32]{1,0:T(2,128)S(1)}, f32[2,32]{1,0:T(2,128)}, u32[]{:S(2)}) copy-start(f32[2,32]{1,0:T(2,128)} %copy-done.282) | copy-start | bytes 772
  1140.6 483.4 %copy-start.285 = (f32[2,32]{1,0:T(2,128)S(1)}, f32[2,32]{1,0:T(2,128)}, u32[]{:S(2)}) copy-start(f32[2,32]{1,0:T(2,128)} %copy-done.284) | copy-start | bytes 772
  1140.6 1079.6 %reduce-scatter.80.cloned.1.call-start = ((), (), s32[]{:S(2)}) async-start(), calls=%async_computation.65 | async-start | bytes 442368 | tf_op jit(solution)/shard_map/reduce_scatter | solution.py:251
  1141.9 482.8 %copy-start.316 = (f32[2,32]{1,0:T(2,128)S(1)}, f32[2,32]{1,0:T(2,128)}, u32[]{:S(2)}) copy-start(f32[2,32]{1,0:T(2,128)} %copy-done.315) | copy-start | bytes 772
  1141.9 482.8 %copy-start.312 = (f32[2,32]{1,0:T(2,128)S(1)}, f32[2,32]{1,0:T(2,128)}, u32[]{:S(2)}) copy-start(f32[2,32]{1,0:T(2,128)} %copy-done.311) | copy-start | bytes 772
  1142.0 482.8 %copy-start.314 = (f32[2,32]{1,0:T(2,128)S(1)}, f32[2,32]{1,0:T(2,128)}, u32[]{:S(2)}) copy-start(f32[2,32]{1,0:T(2,128)} %copy-done.313) | copy-start | bytes 772
  1142.0 482.9 %copy-start.152 = (bf16[2,2,8,8,256]{4,3,1,2,0:T(8,128)(2,1)}, bf16[2,2,8,8,256]{4,3,1,2,0:T(8,128)(2,1)S(1)}, u32[]{:S(2)}) copy-start(bf16[2,2,8,8,256]{4,3,1,2,0:T(8,128)(2,1)S(1)} %copy.136) | copy-start | bytes 393220
  1142.0 482.9 %copy-start.52 = (bf16[2,32,1152]{2,1,0:T(8,128)(2,1)S(1)}, bf16[2,32,1152]{2,1,0:T(8,128)(2,1)}, u32[]{:S(2)}) copy-start(bf16[2,32,1152]{2,1,0:T(8,128)(2,1)} %copy-done.51) | copy-start | bytes 442372
  1143.2 482.1 %copy-start.50 = (bf16[2,32,1152]{2,1,0:T(8,128)(2,1)S(1)}, bf16[2,32,1152]{2,1,0:T(8,128)(2,1)}, u32[]{:S(2)}) copy-start(bf16[2,32,1152]{2,1,0:T(8,128)(2,1)} %copy-done.49) | copy-start | bytes 442372
  1143.3 1149.0 %reduce-scatter.88.cloned.1.call-start = ((), (), s32[]{:S(2)}) async-start(), calls=%async_computation.69 | async-start | bytes 1253376 | tf_op jit(solution)/shard_map/reduce_scatter | solution.py:344
  1627.7 714.9 %reduce-scatter.90.cloned.1.call-start = ((), (), s32[]{:S(2)}) async-start(), calls=%async_computation.70 | async-start | bytes 1253376 | tf_op jit(solution)/shard_map/reduce_scatter | solution.py:344
  2168.3 303.2 %all-reduce.36.cloned.1.call-start = ((), (), s32[]{:S(2)}) async-start(), calls=%async_computation.75 | async-start | bytes 153600 | tf_op jit(solution)/shard_map/psum | solution.py:351
  2344.1 137.2 %reduce-scatter.86.cloned.1.call-start = ((), (), s32[]{:S(2)}) async-start(), calls=%async_computation.68 | async-start | bytes 2506752 | tf_op jit(solution)/shard_map/reduce_scatter | solution.py:344
  2347.0 154.3 %reduce-scatter.92.cloned.1.call-start = ((), (), s32[]{:S(2)}) async-start(), calls=%async_computation.71 | async-start | bytes 2506752 | tf_op jit(solution)/shard_map/reduce_scatter | solution.py:344
  2352.4 324.3 %reduce-scatter.94.cloned.1.call-start = ((), (), s32[]{:S(2)}) async-start(), calls=%async_computation.72 | async-start | bytes 16920576
  2391.3 461.0 %reduce-scatter.96.cloned.1.call-start = ((), (), s32[]{:S(2)}) async-start(), calls=%async_computation.73 | async-start | bytes 16920576
  2429.3 598.6 %reduce-scatter.98.cloned.1.call-start = ((), (), s32[]{:S(2)}) async-start(), calls=%async_computation.74 | async-start | bytes 16920576
  (345 other events, 5168.3 us)
Sparse Core Ops, SparseCore 0:
  10.3 41.2 all-gather.13
  105.4 52.7 all-gather.31
  161.8 52.8 all-gather.33
  216.8 37.2 all-gather.19
  257.0 52.6 all-gather.15
  312.7 52.6 all-gather.17
  368.4 52.6 all-gather.27
  424.2 52.6 all-gather.29
  480.0 52.6 all-gather.35
  535.6 52.6 all-gather.37
  591.2 14.2 reduce-scatter.45
  608.2 15.2 reduce-scatter.37
  626.4 15.2 reduce-scatter.41
  644.5 15.2 reduce-scatter.49
  661.8 72.1 all-gather.21
  736.1 70.5 all-gather.23
  808.6 70.5 all-gather.25
  886.1 10.3 reduce-scatter.51
  901.0 10.4 reduce-scatter.43
  916.9 10.4 reduce-scatter.39
  932.8 10.4 reduce-scatter.47
  970.0 12.0 reduce-scatter.53
  1001.7 12.1 reduce-scatter.69
  1027.5 12.1 reduce-scatter.61
  1047.2 12.1 reduce-scatter.77
  1078.8 136.9 reduce-scatter.73
  1218.0 133.4 reduce-scatter.65
  1353.8 133.6 reduce-scatter.81
  1489.8 133.1 reduce-scatter.57
  1625.1 133.5 reduce-scatter.59
  1761.0 133.1 reduce-scatter.67
  1896.5 133.3 reduce-scatter.75
  2032.1 133.4 reduce-scatter.83
  2168.4 8.5 reduce-scatter.63
  2179.8 12.0 reduce-scatter.55
  2193.9 12.0 reduce-scatter.71
  2208.1 12.0 reduce-scatter.79
  2223.8 58.1 reduce-scatter.87
  2285.4 57.0 reduce-scatter.89
  2346.3 20.6 all-reduce.35
  2371.3 63.1 reduce-scatter.85
  2439.3 61.8 reduce-scatter.91
  2505.8 170.8 reduce-scatter.93
  2681.4 170.8 reduce-scatter.95
  2856.9 170.8 reduce-scatter.97
where the time goes:
time: 3050 us; the launch traced here: 3030 us
  waiting for transfers between devices  2290 us (75%)
  matrix products  337 us (11%)
  blocking collectives  267 us (9%)
  other arithmetic  78.7 us (3%)
  local copies, waits for them, and re-layouts  41.5 us (1%)
    unnamed x48, waiting for transfers between devices  530 us
    reduce_scatter x4, waiting for transfers between devices, micro_step(): lax.psum_scatter(grad_values_all, ('wide', 'tensor'), scatter_dimension=1...  528 us
    reduce_scatter x4, waiting for transfers between devices, micro_step(): lax.psum_scatter(grad_keys_all, ('wide', 'tensor'), scatter_dimension=1,...  476 us
    all_gather x4, waiting for transfers between devices, micro_step(): lax.all_gather(value_low, ('wide', 'tensor'), axis=1, tiled=True)  197 us
    all_gather x4, waiting for transfers between devices, micro_step(): lax.all_gather(key_low, ('wide', 'tensor'), axis=1, tiled=True)  153 us
    unnamed x2, blocking collectives  125 us
    reduce_scatter x4, waiting for transfers between devices, body(): lax.psum_scatter(grad_sums, 'wide', scatter_dimension=0, tiled=True)  68.7 us
    all_gather x1, waiting for transfers between devices, body(): lax.all_gather(shards[5], 'wide', axis=0, tiled=True)  66.6 us
  transfers between devices with their start and end apart: 45, of which 34 were waited for; matrix products, arithmetic and copies ran while one was open for 13% of the time, Pallas kernels for 0%

commit v1 on v0

v1 whole, which is shorter than its diff:
```python
import jax
import jax.numpy as jnp
from jax import lax
from jax.sharding import Mesh
from jax.sharding import PartitionSpec as P

HD = 256
PIC = 256
EPSILON = 1e-06
ROPE_BASE = 1000000.0
F32 = jnp.float32
BF16 = jnp.bfloat16


def dot(left, right, dims):
    return lax.dot_general(left, right, ((dims[0], dims[1]), ((), ())), preferred_element_type=F32)


def mm(left, right):
    return dot(left, right, ((1,), (0,)))


def mm_nt(left, right):
    return dot(left, right, ((1,), (1,)))


def mm_tn(left, right):
    return dot(left, right, ((0,), (0,)))


def inverse_root(values):
    return lax.rsqrt(jnp.mean(values * values, axis=-1, keepdims=True) + EPSILON)


def norm_back(values, factor, grad):
    root = inverse_root(values)
    scaled = grad * factor
    inner = jnp.mean(values * scaled, axis=-1, keepdims=True)
    grad_values = root * (scaled - values * (root * root * inner))
    return grad_values, jnp.sum(grad * values * root, axis=0)


def turn(values, cosine, sine):
    half = values.shape[-1] // 2
    first = values[..., :half]
    second = values[..., half:]
    return jnp.concatenate([first * cosine - second * sine, second * cosine + first * sine], axis=-1)


def layout(lengths, starts, places):
    doc_ends = jnp.cumsum(lengths)
    before = places[:, None] >= doc_ends[None, :]
    doc_ids = jnp.sum(before.astype(jnp.int32), axis=1)
    opening = jnp.max(jnp.where(before, doc_ends[None, :], 0), axis=1)
    inside = (places[:, None] >= starts[None, :]) & (places[:, None] < starts[None, :] + PIC)
    labels = jnp.arange(1, starts.shape[0] + 1, dtype=jnp.int32)
    pictures = jnp.sum(jnp.where(inside, labels[None, :], 0), axis=1) - 1
    return doc_ids, places - opening, pictures


def shift(values, axis, step):
    size = lax.axis_size(axis)
    return lax.ppermute(values, axis, [(i, (i + step) % size) for i in range(size)])


def gather_rows(own):
    near = [own] + [shift(own, "tensor", k) for k in range(1, lax.axis_size("tensor"))]
    row = jnp.concatenate(near, axis=0)
    rest = [row] + [shift(row, "core", k) for k in range(1, lax.axis_size("core"))]
    return jnp.concatenate(rest, axis=0)


def scatter_rows(parts):
    cores = lax.axis_size("core")
    tensors = lax.axis_size("tensor")
    rows = parts.shape[0] // cores
    total = parts[:rows]
    for k in range(1, cores):
        total = total + shift(parts[k * rows : (k + 1) * rows].astype(BF16), "core", -k).astype(F32)
    rows = rows // tensors
    result = total[:rows]
    for k in range(1, tensors):
        result = result + shift(total[k * rows : (k + 1) * rows].astype(BF16), "tensor", -k).astype(F32)
    return result


def ring_order(count):
    return list(range(0, count, 2)) + list(range(1, count, 2))[::-1]


def ring_pairs(count, way):
    ring = ring_order(count)
    return [(ring[i], ring[(i + way) % count]) for i in range(count)]


def ring_place(place, offset):
    count = lax.axis_size("seq")
    return jnp.array(ring_order(count), jnp.int32)[(place + offset) % count]


def ring_gather(chains, place):
    count = lax.axis_size("seq")
    moving = [block for block, _ in chains]
    spot = ring_place(place, 0)
    full = [
        lax.dynamic_update_slice(
            jnp.zeros((count * b.shape[0],) + b.shape[1:], b.dtype), b, (spot * b.shape[0], 0)
        )
        for b in moving
    ]
    for step in range(1, count):
        for i, (_, way) in enumerate(chains):
            moving[i] = lax.ppermute(moving[i], "seq", ring_pairs(count, way))
            spot = ring_place(place, -way * step)
            full[i] = lax.dynamic_update_slice(full[i], moving[i], (spot * moving[i].shape[0], 0))
    return full


def ring_scatter(chains, place):
    count = lax.axis_size("seq")
    sums = [make(ring_place(place, -way)) for make, way in chains]
    for step in range(1, count):
        for i, (make, way) in enumerate(chains):
            arrived = lax.ppermute(sums[i].astype(BF16), "seq", ring_pairs(count, way))
            sums[i] = arrived.astype(F32) + make(ring_place(place, -way * (step + 1)))
    return sums


def sum_all(values):
    for axis in ("core", "tensor", "seq"):
        size = lax.axis_size(axis)
        hop = 1
        while hop < size:
            values = values + lax.ppermute(values, axis, [(i, i ^ hop) for i in range(size)])
            hop *= 2
    return values


def sum_tensor(values):
    if lax.axis_size("tensor") == 2:
        return values + shift(values, "tensor", 1)
    return lax.psum(values, "tensor")


def body(
    tokens,
    out_grad,
    doc_lengths,
    picture_starts,
    q_weight,
    k_weight,
    v_weight,
    out_weight,
    gate_weight,
    up_weight,
    down_weight,
    attn_in_gain,
    attn_out_gain,
    ffn_in_gain,
    ffn_out_gain,
    query_gain,
    key_gain,
):
    seqs = lax.axis_size("seq")
    cores = lax.axis_size("core")
    tensors = lax.axis_size("tensor")
    s_index = lax.axis_index("seq")
    c_index = lax.axis_index("core")
    t_index = lax.axis_index("tensor")
    micro, per_micro, span, width = tokens.shape
    place = jnp.array([ring_order(seqs).index(i) for i in range(seqs)], jnp.int32)[s_index]
    heads_here = q_weight.shape[1] // HD
    split_heads = heads_here > 1
    assert heads_here == (cores if split_heads else 1)
    own_feats = k_weight.shape[0]

    if split_heads:
        q_block, out_block = (
            lax.all_to_all(w, "core", split_axis=1, concat_axis=0, tiled=True) for w in (q_weight, out_weight)
        )
    else:
        q_block, out_block = (lax.all_gather(w, "core", axis=0, tiled=True) for w in (q_weight, out_weight))
    gains = jnp.concatenate([attn_in_gain, attn_out_gain, ffn_in_gain, ffn_out_gain, query_gain, key_gain])
    gain_row = jnp.pad(gains[None, :], ((0, 7), (0, 2 * HD - gains.shape[0])))
    kv_block = jnp.concatenate([jnp.concatenate([k_weight, v_weight], axis=1), gain_row], axis=0)
    q_out, kv_mine = ring_gather([(jnp.concatenate([q_block, out_block], axis=1), 1), (kv_block, -1)], place)
    q_full = q_out[:, :HD]
    out_full = q_out[:, HD:]
    kv_all = lax.all_gather(kv_mine.reshape(seqs, -1, 2 * HD), "core", axis=1)
    kv_full = kv_all[:, :, :own_feats].reshape(width, 2 * HD)
    gain_all = kv_all[:, :, own_feats].astype(F32)
    gain_sizes = [own_feats] * 4 + [query_gain.shape[0]] * 2
    gain_ends = [sum(gain_sizes[: i + 1]) for i in range(6)]
    g_in, g_ao, g_fi, g_fo, g_q, g_k = (
        gain_all[:, :, end - size : end].reshape(1, -1) for end, size in zip(gain_ends, gain_sizes)
    )
    qkv_full = jnp.concatenate([q_full, kv_full], axis=1)

    gate_block, up_block, down_block = (
        lax.all_to_all(w, "core", split_axis=1, concat_axis=0, tiled=True)
        for w in (gate_weight, up_weight, down_weight)
    )
    gate_full, up_full = ring_gather([(gate_block, 1), (up_block, -1)], place)
    half = down_block.shape[0] // 2
    down_low, down_high = ring_gather([(down_block[:half], 1), (down_block[half:], -1)], place)
    hidden_here = gate_block.shape[1]
    down_full = jnp.concatenate(
        [down_low.reshape(seqs, half, hidden_here), down_high.reshape(seqs, half, hidden_here)], axis=1
    ).reshape(width, hidden_here)

    def to_rows(values):
        moved = lax.all_to_all(values.reshape(seqs, span, width), "seq", split_axis=0, concat_axis=0, tiled=True)
        return moved.reshape(seqs * span, width)

    def from_rows(values):
        moved = lax.all_to_all(values.reshape(seqs, span, width), "seq", split_axis=0, concat_axis=0, tiled=True)
        return moved.reshape(micro, per_micro, span, width)

    x = to_rows(tokens).astype(F32)
    cotangent = to_rows(out_grad).astype(F32)

    steps = jnp.arange(cores, dtype=jnp.int32)
    owner_core = ((c_index - steps) % cores)[:, None, None, None]
    owner_tensor = ((t_index - jnp.arange(tensors, dtype=jnp.int32)) % tensors)[None, :, None, None]
    block_index = jnp.arange(seqs, dtype=jnp.int32)[None, None, :, None]
    inner = jnp.arange(span, dtype=jnp.int32)[None, None, None, :]
    places = (((block_index * cores + owner_core) * tensors + owner_tensor) * span + inner).reshape(-1)
    docs, within, pics = layout(
        doc_lengths.reshape(seqs, -1)[s_index], picture_starts.reshape(seqs, -1)[s_index], places
    )
    frequency = ROPE_BASE ** (-2.0 * jnp.arange(HD // 2, dtype=F32) / HD)
    angles = within.astype(F32)[:, None] * frequency[None, :]
    cosine = jnp.cos(angles)
    sine = jnp.sin(angles)
    rows = places.shape[0]
    q_rows = rows if split_heads else rows // cores

    a_own = (x * inverse_root(x) * g_in).astype(BF16)
    a_all = gather_rows(a_own)
    raw = mm(a_all, qkv_full)
    q_raw = raw[:q_rows, :HD]
    k_raw = raw[:, HD : 2 * HD]
    value = raw[:, 2 * HD :].astype(BF16)
    scale = HD ** (-0.5)
    query = (turn(q_raw * inverse_root(q_raw) * g_q, cosine[:q_rows], sine[:q_rows]) * scale).astype(BF16)
    key = turn(k_raw * inverse_root(k_raw) * g_k, cosine, sine).astype(BF16)
    allowed = (docs[:q_rows, None] == docs[None, :]) & (
        (places[None, :] <= places[:q_rows, None])
        | ((pics[:q_rows, None] == pics[None, :]) & (pics[:q_rows, None] >= 0))
    )
    scores = jnp.where(allowed, mm_nt(query, key), -1e30)
    top = jnp.max(scores, axis=-1, keepdims=True)
    log_total = top + jnp.log(jnp.sum(jnp.exp(scores - top), axis=-1, keepdims=True))
    prob = jnp.exp(scores - log_total)
    attended = mm(prob.astype(BF16), value).astype(BF16)
    branch_part = mm_nt(attended, out_full)
    if q_rows != rows:
        branch_part = jnp.pad(branch_part, ((0, rows - q_rows), (0, 0)))
    branch = scatter_rows(branch_part)

    middle = x + branch * inverse_root(branch) * g_ao
    f_own = (middle * inverse_root(middle) * g_fi).astype(BF16)
    f_all = gather_rows(f_own)
    gate_act = mm(f_all, gate_full)
    up_act = mm(f_all, up_full)
    gelu, pull_gelu = jax.vjp(lambda v: jax.nn.gelu(v, approximate=True), gate_act)
    hidden = (gelu * up_act).astype(BF16)
    second = scatter_rows(mm_nt(hidden, down_full))
    output = middle + second * inverse_root(second) * g_fo

    grad_second, grad_fo = norm_back(second, g_fo, cotangent)
    de_all = gather_rows(grad_second.astype(BF16))
    grad_hidden = mm(de_all, down_full)
    up_grad = (grad_hidden * gelu).astype(BF16)
    gate_grad = pull_gelu(grad_hidden * up_act)[0].astype(BF16)

    def blocks(left, right, first, count):
        left_t = left.T

        def make(spot):
            start = spot * (left_t.shape[0] // seqs) + first
            return mm(lax.dynamic_slice_in_dim(left_t, start, count, 0), right)

        return make

    feats = width // seqs
    down_low, down_high = ring_scatter(
        [(blocks(de_all, hidden, 0, half), 1), (blocks(de_all, hidden, half, half), -1)], place
    )
    down_sum = jnp.concatenate([down_low, down_high], axis=0)
    gate_sum, up_sum = ring_scatter(
        [(blocks(f_all, gate_grad, 0, feats), 1), (blocks(f_all, up_grad, 0, feats), -1)], place
    )
    grad_f = scatter_rows(mm_nt(gate_grad, gate_full) + mm_nt(up_grad, up_full))
    back_middle, grad_fi = norm_back(middle, g_fi, grad_f)
    grad_middle = cotangent + back_middle

    grad_branch, grad_ao = norm_back(branch, g_ao, grad_middle)
    dr_all = gather_rows(grad_branch.astype(BF16))
    grad_attended = mm(dr_all[:q_rows], out_full).astype(BF16)
    grad_prob = mm_nt(grad_attended, value)
    grad_scores = (prob * (grad_prob - jnp.sum(prob * grad_prob, axis=-1, keepdims=True))).astype(BF16)
    grad_query = mm(grad_scores, key)
    grad_key = mm_tn(grad_scores, query)
    grad_value = mm_tn(prob.astype(BF16), grad_attended)
    back_query, grad_gq = norm_back(q_raw, g_q, turn(grad_query * scale, cosine[:q_rows], -sine[:q_rows]))
    back_key, grad_gk = norm_back(k_raw, g_k, turn(grad_key, cosine, -sine))
    query_low = back_query.astype(BF16)
    kv_low = jnp.concatenate([back_key, grad_value], axis=1).astype(BF16)

    out_sum, q_sum = ring_scatter(
        [
            (blocks(dr_all[:q_rows], attended, 0, feats), 1),
            (blocks(a_all[:q_rows], query_low, 0, feats), -1),
        ],
        place,
    )
    kv_parts = mm_tn(a_all, kv_low).reshape(seqs, cores, own_feats, 2 * HD)
    kv_core = lax.dynamic_index_in_dim(kv_parts, c_index, 1, keepdims=False)
    for k in range(1, cores):
        going = lax.dynamic_index_in_dim(kv_parts, (c_index + k) % cores, 1, keepdims=False)
        kv_core = kv_core + shift(going.astype(BF16), "core", k).astype(F32)
    kv_sum = ring_scatter(
        [(lambda spot: lax.dynamic_index_in_dim(kv_core, spot, 0, keepdims=False), 1)], place
    )[0]
    kv_sum = sum_tensor(kv_sum)

    query_part = mm_nt(query_low, q_full)
    if q_rows != rows:
        query_part = jnp.pad(query_part, ((0, rows - q_rows), (0, 0)))
    grad_a = scatter_rows(query_part + mm_nt(kv_low, kv_full))
    back_x, grad_in = norm_back(x, g_in, grad_a)
    input_grad = grad_middle + back_x

    def to_owner(values):
        return lax.all_to_all(values, "core", split_axis=0, concat_axis=1, tiled=True)

    if split_heads:
        q_grad, out_grad_w = to_owner(q_sum), to_owner(out_sum)
    else:
        q_grad, out_grad_w = (
            lax.psum_scatter(v, "core", scatter_dimension=0, tiled=True) for v in (q_sum, out_sum)
        )
    gain_grads = (grad_in, grad_ao, grad_fi, grad_fo, grad_gq, grad_gk)
    packed = jnp.concatenate([g.reshape(seqs * cores, -1) for g in gain_grads], axis=1)
    shape = packed.shape
    packed = sum_all(packed.reshape(-1, 128)).reshape(shape)
    mine = lax.dynamic_index_in_dim(packed, s_index * cores + c_index, 0, keepdims=False)
    gain_out = tuple(mine[end - size : end] for end, size in zip(gain_ends, gain_sizes))
    return (
        from_rows(output.astype(BF16)),
        from_rows(input_grad.astype(BF16)),
        q_grad,
        kv_sum[:, :HD],
        kv_sum[:, HD:],
        out_grad_w,
        to_owner(gate_sum),
        to_owner(up_sum),
        to_owner(down_sum),
    ) + gain_out


def solution(mesh):
    def run(tokens, *rest):
        seqs = tokens.shape[0] * tokens.shape[1]
        wide, tensor = mesh.shape["wide"], mesh.shape["tensor"]
        fine = Mesh(mesh.devices.reshape(seqs, wide // seqs, tensor), ("seq", "core", "tensor"))
        acts = P(None, None, ("seq", "core", "tensor"), None)
        both = P(("seq", "core"), "tensor")
        rows = P(("seq", "core"), None)
        vector = P(("seq", "core"))
        weights = (both, rows, rows, both, both, both, both) + (vector,) * 6
        return jax.shard_map(
            body,
            mesh=fine,
            in_specs=(acts, acts, P(), P()) + weights,
            out_specs=(acts, acts) + weights,
            check_vma=False,
        )(tokens, *rest)

    return run
```

time: 3050 us -> 744 us (0.24)
  waiting for transfers between devices: 2290 us -> 192 us
  blocking collectives: 267 us -> 43 us
  matrix products: 337 us -> 138 us
  starting transfers between devices: 3.79 us -> 138 us
  local copies, waits for them, and re-layouts: 41.5 us -> 104 us
  between operations: 22.2 us -> 69.9 us
  other arithmetic: 78.7 us -> 47.9 us
    reduce_scatter x28 -> x0, waiting for transfers between devices: 1190 us -> none  [the longest x4 528 us: micro_step(): lax.psum_scatter(grad_values_all, ('wide', 'tensor'), scatter_dimension=1...]
    all_gather x13 -> x1, waiting for transfers between devices: 564 us -> 0.01 us  [body(): kv_all = lax.all_gather(kv_mine.reshape(seqs, -1, 2 * HD), 'core', axis=1)]
    unnamed x48 -> x1, waiting for transfers between devices: 530 us -> 0.02 us
    dot_general x108 -> x66, matrix products: 337 us -> 138 us  [dot(): lax.dot_general(left, right, ((dims[0], dims[1]), ((), ())), preferred_el...]
    ppermute x0 -> x114, waiting for transfers between devices: none -> 191 us  [the longest x49 93.9 us: ring_scatter(): arrived = lax.ppermute(sums[i].astype(BF16), 'seq', ring_pairs(count, way))]
    all_gather x18 -> x0, blocking collectives: 141 us -> none  [the longest x4 26.8 us: micro_step(): lax.all_gather(grad_branch.astype(jnp.bfloat16), 'tensor', axis=1, tiled=...]
    unnamed x2 -> x0, blocking collectives: 125 us -> none
    ppermute x0 -> x114, starting transfers between devices: none -> 115 us  [the longest x49 52.1 us: ring_scatter(): arrived = lax.ppermute(sums[i].astype(BF16), 'seq', ring_pairs(count, way))]
  transfers between devices with their start and end apart: 45 -> 120, of which waited for: 34 -> 51; matrix products, arithmetic and copies ran while one was open for 13% -> 30% of each run, Pallas kernels for 0% -> 0%
where the time goes in v1:
time: 744 us; the launch traced here: 733 us
  waiting for transfers between devices  192 us (26%)
  starting transfers between devices  138 us (19%)
  matrix products  138 us (19%)
  local copies, waits for them, and re-layouts  104 us (14%)
  between operations  69.9 us (9%)
  other arithmetic  47.9 us (6%)
  blocking collectives  43 us (6%)
    dot_general x66, matrix products, dot(): lax.dot_general(left, right, ((dims[0], dims[1]), ((), ())), preferred_el...  138 us
    ppermute x49, waiting for transfers between devices, ring_scatter(): arrived = lax.ppermute(sums[i].astype(BF16), 'seq', ring_pairs(count, way))  93.9 us
    ppermute x42, waiting for transfers between devices, ring_gather(): moving[i] = lax.ppermute(moving[i], 'seq', ring_pairs(count, way))  56.3 us
    ppermute x49, starting transfers between devices, ring_scatter(): arrived = lax.ppermute(sums[i].astype(BF16), 'seq', ring_pairs(count, way))  52.1 us
    ppermute x42, starting transfers between devices, ring_gather(): moving[i] = lax.ppermute(moving[i], 'seq', ring_pairs(count, way))  48.5 us
    dynamic_update_slice x42, local copies, waits for them, and re-layouts, ring_gather(): lax.dynamic_update_slice(full[i], moving[i], (spot * moving[i].shape[0], 0))  42 us
    ppermute x18, waiting for transfers between devices, shift(): lax.ppermute(values, axis, [(i, (i + step) % size) for i in range(size)])  31 us
    all_to_all x5, blocking collectives, to_owner(): lax.all_to_all(values, 'core', split_axis=0, concat_axis=1, tiled=True)  25.1 us
  transfers between devices with their start and end apart: 120, of which 51 were waited for; matrix products, arithmetic and copies ran while one was open for 30% of the time, Pallas kernels for 0%

profile of v1, /device:TPU:0, one launch (start us, length us, event | category | flops | bytes accessed | tf_op | source)
XLA Modules:
  0.0 732.5 jit_solution(10473747524583076670)
XLA Ops:
  9.0 5.1 all_to_all.207
  14.1 3.0 collective-permute-start.20
  34.1 3.3 all-to-all-start.2
  38.8 3.7 all_to_all.208
  47.0 4.9 all_to_all.209
  52.5 4.1 all_to_all.210
  56.6 6.2 all-to-all-start
  68.0 2.2 broadcast.377.clone
  73.1 2.3 broadcast.377.clone.1
  118.3 2.4 collective-permute-start.11
  122.0 4.0 collective-permute-done.4
  129.4 4.1 collective-permute-done.5
  152.7 2.7 collective-permute-done.13
  162.2 3.1 collective-permute-done.14
  183.7 7.3 collective-permute-done.38
  195.5 3.8 fusion.8
  200.3 2.4 fusion.56
  224.4 9.1 %collective-permute-done.47 = bf16[72,1728]{1,0:T(8,128)(2,1)S(1)} collective-permute-done((bf16[72,1728]{1,0:T(8,128)(2,1)}, bf16[72,1728]{1,0:T(8,128)(2,1)S(1)}, u32[]{:S(2)}, u32[]{:S(2)}) %collective-permute-start.47) | collective-permute-done | bytes 248864 | tf_op jit(solution)/shard_map/ppermute | solution.py:113
  234.9 2.4 pad_maximum_fusion
  239.0 6.5 collective-permute-done.24
  254.8 2.8 collective-permute-done.25
  264.9 2.6 collective-permute-done.26
  268.3 6.7 collective-permute-done.33
  275.9 7.5 %fusion.319 = f32[1024,1728]{0,1:T(8,128)S(1)} fusion(bf16[1152,1728]{1,0:T(8,128)(2,1)} %constant_dynamic-update-slice_fusion.24, bf16[512,1152]{1,0:T(8,128)(2,1)S(1)} %collective-permute-done.19, bf16[256,1152]{1,0:T(8,128)(2,1)S(1)} %collective-permute-done.18, bf16[256,1152]{1,0:T(8,128)(2,1)S(1)} %multiply_convert_fusion.4), kind=kOutput, calls=%fused_computation.464 | convolution fusion | flops 4083941376 | bytes 13418496 | tf_op jit(solution)/shard_map/dot_general | solution.py:16
  283.5 20.7 %multiply_convert_fusion.1 = (bf16[1024,1728]{0,1:T(8,128)(2,1)S(1)}, f32[1024,1728]{0,1:T(8,128)}) fusion(f32[1024,1728]{0,1:T(8,128)S(1)} %fusion.319, bf16[1152,1728]{1,0:T(8,128)(2,1)} %constant_dynamic-update-slice_fusion.16, bf16[512,1152]{1,0:T(8,128)(2,1)S(1)} %collective-permute-done.19, bf16[256,1152]{1,0:T(8,128)(2,1)S(1)} %collective-permute-done.18, ...), kind=kOutput, calls=%fused_computation.10 | convolution fusion | flops 4101636096 | bytes 24035328 | tf_op jit(solution)/shard_map/dot_general | solution.py:16
  304.1 5.0 fusion.325
  309.2 2.2 copy-done.28
  312.5 4.2 all-to-all-start.7
  316.7 2.2 slice_add_fusion.2
  322.9 14.4 %collective-permute-done.49 = bf16[256,1152]{1,0:T(8,128)(2,1)} collective-permute-done((bf16[256,1152]{1,0:T(8,128)(2,1)}, bf16[256,1152]{1,0:T(8,128)(2,1)}, u32[]{:S(2)}, u32[]{:S(2)}) %collective-permute-start.49) | collective-permute-done | bytes 589856 | tf_op jit(solution)/shard_map/ppermute | solution.py:63
  340.1 2.7 fusion.18
  342.8 2.9 fusion.16
  346.0 14.7 %collective-permute-done.50 = bf16[256,1152]{1,0:T(8,128)(2,1)S(1)} collective-permute-done((bf16[256,1152]{1,0:T(8,128)(2,1)S(1)}, bf16[256,1152]{1,0:T(8,128)(2,1)S(1)}, u32[]{:S(2)}, u32[]{:S(2)}) %collective-permute-start.50) | collective-permute-done | bytes 589856 | tf_op jit(solution)/shard_map/ppermute | solution.py:63
  376.7 3.4 pad_maximum_fusion.1
  381.7 5.8 all-to-all-start.6
  387.5 15.0 %fusion.6 = (bf16[1024,1728]{0,1:T(8,128)(2,1)S(1)}, bf16[1024,1728]{0,1:T(8,128)(2,1)S(1)}) fusion(f32[1024,1728]{0,1:T(8,128)} %copy-done.108, f32[1024,1728]{0,1:T(8,128)} %get-tuple-element.98, bf16[1152,1728]{1,0:T(8,128)(2,1)} %bitcast.283, bf16[512,1152]{1,0:T(8,128)(2,1)} %collective-permute-done.51, bf16[256,1152]{1,0:T(8,128)(2,1)} %copy-done.34, ...), kind=kOutput, calls=%fused_computation.8 | convolution fusion | flops 4126408704 | bytes 27574272 | tf_op jit(solution)/shard_map/dot_general | solution.py:16
  402.5 7.3 %fusion.326 = f32[1024,1152]{1,0:T(8,128)S(1)} fusion(bf16[1024,1728]{0,1:T(8,128)(2,1)S(1)} %get-tuple-element.37, bf16[1152,1728]{1,0:T(8,128)(2,1)} %constant_dynamic-update-slice_fusion.16), kind=kOutput, calls=%fused_computation.471 | convolution fusion | flops 4076863488 | bytes 12238848 | tf_op jit(solution)/shard_map/dot_general | solution.py:16
  412.8 7.3 convolution_add_fusion.1
  428.7 13.2 %collective-permute-done.102 = bf16[72,1728]{1,0:T(8,128)(2,1)S(1)} collective-permute-done((bf16[72,1728]{1,0:T(8,128)(2,1)S(1)}, bf16[72,1728]{1,0:T(8,128)(2,1)S(1)}, u32[]{:S(2)}, u32[]{:S(2)}) %collective-permute-start.102) | collective-permute-done | bytes 248864 | tf_op jit(solution)/shard_map/ppermute | solution.py:124
  456.9 11.9 %collective-permute-done.104 = bf16[72,1728]{1,0:T(8,128)(2,1)S(1)} collective-permute-done((bf16[72,1728]{1,0:T(8,128)(2,1)S(1)}, bf16[72,1728]{1,0:T(8,128)(2,1)S(1)}, u32[]{:S(2)}, u32[]{:S(2)}) %collective-permute-start.104) | collective-permute-done | bytes 248864 | tf_op jit(solution)/shard_map/ppermute | solution.py:124
  484.7 9.6 %collective-permute-done.106 = bf16[72,1728]{1,0:T(8,128)(2,1)S(1)} collective-permute-done((bf16[72,1728]{1,0:T(8,128)(2,1)S(1)}, bf16[72,1728]{1,0:T(8,128)(2,1)S(1)}, u32[]{:S(2)}, u32[]{:S(2)}) %collective-permute-start.106) | collective-permute-done | bytes 248864 | tf_op jit(solution)/shard_map/ppermute | solution.py:124
  509.3 9.2 %collective-permute-done.108 = bf16[72,1728]{1,0:T(8,128)(2,1)S(1)} collective-permute-done((bf16[72,1728]{1,0:T(8,128)(2,1)S(1)}, bf16[72,1728]{1,0:T(8,128)(2,1)S(1)}, u32[]{:S(2)}, u32[]{:S(2)}) %collective-permute-start.108) | collective-permute-done | bytes 248864 | tf_op jit(solution)/shard_map/ppermute | solution.py:124
  523.0 2.5 multiply_reduce_fusion.2
  531.3 6.3 collective-permute-done.85
  543.0 5.9 collective-permute-done.86
  554.4 5.2 collective-permute-done.87
  559.6 2.5 convert_add_fusion.2
  562.6 2.5 convert_add_fusion.1
  573.6 2.4 fusion.52
  585.6 2.7 fusion.47
  623.7 3.0 collective-permute-done.67
  628.0 3.2 collective-permute-done.68
  632.6 3.0 collective-permute-done.69
  636.8 3.2 collective-permute-done.70
  644.6 5.5 all_to_all.211
  650.1 5.9 all_to_all.212
  656.0 4.7 all_to_all.213
  660.7 4.5 all_to_all.214
  665.2 4.5 all_to_all.215
  669.7 4.2 all-to-all-start.8
  678.7 7.1 collective-permute-done.72
  695.5 3.0 collective-permute-done.111
  699.1 6.1 collective-permute-start.112
  716.5 3.6 collective-permute-done.113
  (660 shorter events, 317.3 us)
Async XLA Ops:
  14.1 120.6 %collective-permute-start.20 = (bf16[144,1728]{1,0:T(8,128)(2,1)}, bf16[144,1728]{1,0:T(8,128)(2,1)}, u32[]{:S(2)}, u32[]{:S(2)}) collective-permute-start(bf16[144,1728]{1,0:T(8,128)(2,1)} %bitcast.32), channel_id=1, source_target_pairs={{0,8},{8,16},{16,24},{24,28},{28,20},{20,12},{12,4},{4,0},{1,9},{9... | collective-permute-start | bytes 1493000 | tf_op jit(solution)/shard_map/ppermute | solution.py:113
  33.4 68.7 %collective-permute-start = (bf16[80,512]{1,0:T(8,128)(2,1)}, bf16[80,512]{1,0:T(8,128)(2,1)S(1)}, u32[]{:S(2)}, u32[]{:S(2)}) collective-permute-start(bf16[80,512]{1,0:T(8,128)(2,1)} %get-tuple-element.58), channel_id=1, source_target_pairs={{0,4},{8,0},{16,8},{24,16},{28,24},{20,28},{12,20},{4,12},{1,5},{9... | collective-permute-start | bytes 245768 | tf_op jit(solution)/shard_map/ppermute | solution.py:113
  44.4 58.5 %collective-permute-start.9 = (bf16[144,512]{1,0:T(8,128)(2,1)}, bf16[144,512]{1,0:T(8,128)(2,1)}, u32[]{:S(2)}, u32[]{:S(2)}) collective-permute-start(bf16[144,512]{1,0:T(8,128)(2,1)} %get-tuple-element.56), channel_id=1, source_target_pairs={{0,8},{8,16},{16,24},{24,28},{28,20},{20,12},{12,4},{4,0},{1,9},{9... | collective-permute-start | bytes 442376 | tf_op jit(solution)/shard_map/ppermute | solution.py:113
  51.9 84.3 %collective-permute-start.27 = (bf16[144,1728]{1,0:T(8,128)(2,1)}, bf16[144,1728]{1,0:T(8,128)(2,1)}, u32[]{:S(2)}, u32[]{:S(2)}) collective-permute-start(bf16[144,1728]{1,0:T(8,128)(2,1)} %bitcast.35), channel_id=1, source_target_pairs={{0,4},{8,0},{16,8},{24,16},{28,24},{20,28},{12,20},{4,12},{1,5},{9... | collective-permute-start | bytes 1493000 | tf_op jit(solution)/shard_map/ppermute | solution.py:113
  56.6 93.8 %all-to-all-start = ((bf16[8,32,1152]{2,1,0:T(8,128)(2,1)}), bf16[8,32,1152]{2,1,0:T(8,128)(2,1)S(1)}, u32[]{:S(2)}, u32[]{:S(2)}) async-start(bf16[8,32,1152]{2,1,0:T(8,128)(2,1)} %bitcast), calls=%async_computation | async-start | bytes 1179648 | tf_op jit(solution)/shard_map/all_to_all | solution.py:212
  62.9 87.8 %all-gather.2.cloned.1.call-start = ((), (), s32[]{:S(2)}) async-start(), calls=%async_computation.14 | async-start | bytes 1966080 | tf_op jit(solution)/shard_map/all_gather | solution.py:189
  63.7 50.7 %collective-permute-start.41 = (bf16[72,1728]{1,0:T(8,128)(2,1)}, bf16[72,1728]{1,0:T(8,128)(2,1)S(1)}, u32[]{:S(2)}, u32[]{:S(2)}) collective-permute-start(bf16[72,1728]{1,0:T(8,128)(2,1)} %get-tuple-element.53), channel_id=1, source_target_pairs={{0,4},{8,0},{16,8},{24,16},{28,24},{20,28},{12,20},{4,12},{1,5},{9... | collective-permute-start | bytes 746504 | tf_op jit(solution)/shard_map/ppermute | solution.py:113
  102.2 13.0 %collective-permute-start.34 = (bf16[72,1728]{1,0:T(8,128)(2,1)}, bf16[72,1728]{1,0:T(8,128)(2,1)S(1)}, u32[]{:S(2)}, u32[]{:S(2)}) collective-permute-start(bf16[72,1728]{1,0:T(8,128)(2,1)} %get-tuple-element.52), channel_id=1, source_target_pairs={{0,8},{8,16},{16,24},{24,28},{28,20},{20,12},{12,4},{4,0},{1,9},{9... | collective-permute-start | bytes 746504 | tf_op jit(solution)/shard_map/ppermute | solution.py:113
  115.2 22.4 %collective-permute-start.42 = (bf16[72,1728]{1,0:T(8,128)(2,1)S(1)}, bf16[72,1728]{1,0:T(8,128)(2,1)}, u32[]{:S(2)}, u32[]{:S(2)}) collective-permute-start(bf16[72,1728]{1,0:T(8,128)(2,1)S(1)} %collective-permute-done.41), channel_id=1, source_target_pairs={{0,4},{8,0},{16,8},{24,16},{28,24},{20,28},{12,20},{4,12},{1,5},{9... | collective-permute-start | bytes 746504 | tf_op jit(solution)/shard_map/ppermute | solution.py:113
  126.0 12.2 %collective-permute-start.35 = (bf16[72,1728]{1,0:T(8,128)(2,1)S(1)}, bf16[72,1728]{1,0:T(8,128)(2,1)}, u32[]{:S(2)}, u32[]{:S(2)}) collective-permute-start(bf16[72,1728]{1,0:T(8,128)(2,1)S(1)} %collective-permute-done.34), channel_id=1, source_target_pairs={{0,8},{8,16},{16,24},{24,28},{28,20},{20,12},{12,4},{4,0},{1,9},{9... | collective-permute-start | bytes 746504 | tf_op jit(solution)/shard_map/ppermute | solution.py:113
  134.7 12.8 %collective-permute-start.12 = (bf16[144,512]{1,0:T(8,128)(2,1)S(1)}, bf16[144,512]{1,0:T(8,128)(2,1)}, u32[]{:S(2)}, u32[]{:S(2)}) collective-permute-start(bf16[144,512]{1,0:T(8,128)(2,1)S(1)} %collective-permute-done.11), channel_id=1, source_target_pairs={{0,8},{8,16},{16,24},{24,28},{28,20},{20,12},{12,4},{4,0},{1,9},{9... | collective-permute-start | bytes 442376 | tf_op jit(solution)/shard_map/ppermute | solution.py:113
  136.2 30.9 %collective-permute-start.21 = (bf16[144,1728]{1,0:T(8,128)(2,1)}, bf16[144,1728]{1,0:T(8,128)(2,1)}, u32[]{:S(2)}, u32[]{:S(2)}) collective-permute-start(bf16[144,1728]{1,0:T(8,128)(2,1)} %collective-permute-done.20), channel_id=1, source_target_pairs={{0,8},{8,16},{16,24},{24,28},{28,20},{20,12},{12,4},{4,0},{1,9},{9... | collective-permute-start | bytes 1493000 | tf_op jit(solution)/shard_map/ppermute | solution.py:113
  137.6 36.2 %collective-permute-start.28 = (bf16[144,1728]{1,0:T(8,128)(2,1)}, bf16[144,1728]{1,0:T(8,128)(2,1)}, u32[]{:S(2)}, u32[]{:S(2)}) collective-permute-start(bf16[144,1728]{1,0:T(8,128)(2,1)} %collective-permute-done.27), channel_id=1, source_target_pairs={{0,4},{8,0},{16,8},{24,16},{28,24},{20,28},{12,20},{4,12},{1,5},{9... | collective-permute-start | bytes 1493000 | tf_op jit(solution)/shard_map/ppermute | solution.py:113
  138.2 20.2 %collective-permute-start.43 = (bf16[72,1728]{1,0:T(8,128)(2,1)}, bf16[72,1728]{1,0:T(8,128)(2,1)}, u32[]{:S(2)}, u32[]{:S(2)}) collective-permute-start(bf16[72,1728]{1,0:T(8,128)(2,1)} %collective-permute-done.42), channel_id=1, source_target_pairs={{0,4},{8,0},{16,8},{24,16},{28,24},{20,28},{12,20},{4,12},{1,5},{9... | collective-permute-start | bytes 746504 | tf_op jit(solution)/shard_map/ppermute | solution.py:113
  138.9 22.2 %collective-permute-start.36 = (bf16[72,1728]{1,0:T(8,128)(2,1)}, bf16[72,1728]{1,0:T(8,128)(2,1)S(1)}, u32[]{:S(2)}, u32[]{:S(2)}) collective-permute-start(bf16[72,1728]{1,0:T(8,128)(2,1)} %collective-permute-done.35), channel_id=1, source_target_pairs={{0,8},{8,16},{16,24},{24,28},{28,20},{20,12},{12,4},{4,0},{1,9},{9... | collective-permute-start | bytes 746504 | tf_op jit(solution)/shard_map/ppermute | solution.py:113
  155.3 13.4 %collective-permute-start.7 = (bf16[256,1152]{1,0:T(8,128)(2,1)S(1)}, bf16[256,1152]{1,0:T(8,128)(2,1)S(1)}, u32[]{:S(2)}, u32[]{:S(2)}) collective-permute-start(bf16[256,1152]{1,0:T(8,128)(2,1)S(1)} %fusion.21), channel_id=1, source_target_pairs={{0,1},{1,0},{2,3},{3,2},{4,5},{5,4},{6,7},{7,6},{8,9},{9,8},{10,11... | collective-permute-start | bytes 1769480 | tf_op jit(solution)/shard_map/ppermute | solution.py:63
  168.7 42.9 %collective-permute-start.22 = (bf16[144,1728]{1,0:T(8,128)(2,1)}, bf16[144,1728]{1,0:T(8,128)(2,1)}, u32[]{:S(2)}, u32[]{:S(2)}) collective-permute-start(bf16[144,1728]{1,0:T(8,128)(2,1)} %collective-permute-done.21), channel_id=1, source_target_pairs={{0,8},{8,16},{16,24},{24,28},{28,20},{20,12},{12,4},{4,0},{1,9},{9... | collective-permute-start | bytes 1493000 | tf_op jit(solution)/shard_map/ppermute | solution.py:113
  171.1 24.3 %collective-permute-start.8 = (bf16[512,1152]{1,0:T(8,128)(2,1)}, bf16[512,1152]{1,0:T(8,128)(2,1)}, u32[]{:S(2)}, u32[]{:S(2)}) collective-permute-start(bf16[512,1152]{1,0:T(8,128)(2,1)} %pad_maximum_fusion.5), channel_id=1, source_target_pairs={{0,2},{2,0},{1,3},{3,1},{4,6},{6,4},{5,7},{7,5},{8,10},{10,8},{9,1... | collective-permute-start | bytes 3538952 | tf_op jit(solution)/shard_map/ppermute | solution.py:63
  174.5 16.4 %collective-permute-start.38 = (bf16[72,1728]{1,0:T(8,128)(2,1)S(1)}, bf16[72,1728]{1,0:T(8,128)(2,1)S(1)}, u32[]{:S(2)}, u32[]{:S(2)}) collective-permute-start(bf16[72,1728]{1,0:T(8,128)(2,1)S(1)} %collective-permute-done.37), channel_id=1, source_target_pairs={{0,8},{8,16},{16,24},{24,28},{28,20},{20,12},{12,4},{4,0},{1,9},{9... | collective-permute-start | bytes 746504 | tf_op jit(solution)/shard_map/ppermute | solution.py:113
  177.7 37.6 %collective-permute-start.29 = (bf16[144,1728]{1,0:T(8,128)(2,1)}, bf16[144,1728]{1,0:T(8,128)(2,1)}, u32[]{:S(2)}, u32[]{:S(2)}) collective-permute-start(bf16[144,1728]{1,0:T(8,128)(2,1)} %collective-permute-done.28), channel_id=1, source_target_pairs={{0,4},{8,0},{16,8},{24,16},{28,24},{20,28},{12,20},{4,12},{1,5},{9... | collective-permute-start | bytes 1493000 | tf_op jit(solution)/shard_map/ppermute | solution.py:113
  182.9 34.6 %collective-permute-start.46 = (bf16[72,1728]{1,0:T(8,128)(2,1)}, bf16[72,1728]{1,0:T(8,128)(2,1)}, u32[]{:S(2)}, u32[]{:S(2)}) collective-permute-start(bf16[72,1728]{1,0:T(8,128)(2,1)} %collective-permute-done.45), channel_id=1, source_target_pairs={{0,4},{8,0},{16,8},{24,16},{28,24},{20,28},{12,20},{4,12},{1,5},{9... | collective-permute-start | bytes 746504 | tf_op jit(solution)/shard_map/ppermute | solution.py:113
  191.0 27.4 %collective-permute-start.39 = (bf16[72,1728]{1,0:T(8,128)(2,1)S(1)}, bf16[72,1728]{1,0:T(8,128)(2,1)}, u32[]{:S(2)}, u32[]{:S(2)}) collective-permute-start(bf16[72,1728]{1,0:T(8,128)(2,1)S(1)} %collective-permute-done.38), channel_id=1, source_target_pairs={{0,8},{8,16},{16,24},{24,28},{28,20},{20,12},{12,4},{4,0},{1,9},{9... | collective-permute-start | bytes 746504 | tf_op jit(solution)/shard_map/ppermute | solution.py:113
  209.2 13.6 %collective-permute-start.16 = (bf16[512,1152]{1,0:T(8,128)(2,1)S(1)}, bf16[512,1152]{1,0:T(8,128)(2,1)S(1)}, u32[]{:S(2)}, u32[]{:S(2)}) collective-permute-start(bf16[512,1152]{1,0:T(8,128)(2,1)S(1)} %slice.363), channel_id=1, source_target_pairs={{0,2},{2,0},{1,3},{3,1},{4,6},{6,4},{5,7},{7,5},{8,10},{10,8},{9,1... | collective-permute-start | bytes 3538952 | tf_op jit(solution)/shard_map/ppermute | solution.py:63
  211.6 21.9 %collective-permute-start.23 = (bf16[144,1728]{1,0:T(8,128)(2,1)}, bf16[144,1728]{1,0:T(8,128)(2,1)}, u32[]{:S(2)}, u32[]{:S(2)}) collective-permute-start(bf16[144,1728]{1,0:T(8,128)(2,1)} %collective-permute-done.22), channel_id=1, source_target_pairs={{0,8},{8,16},{16,24},{24,28},{28,20},{20,12},{12,4},{4,0},{1,9},{9... | collective-permute-start | bytes 1493000 | tf_op jit(solution)/shard_map/ppermute | solution.py:113
  215.2 22.9 %collective-permute-start.30 = (bf16[144,1728]{1,0:T(8,128)(2,1)}, bf16[144,1728]{1,0:T(8,128)(2,1)}, u32[]{:S(2)}, u32[]{:S(2)}) collective-permute-start(bf16[144,1728]{1,0:T(8,128)(2,1)} %collective-permute-done.29), channel_id=1, source_target_pairs={{0,4},{8,0},{16,8},{24,16},{28,24},{20,28},{12,20},{4,12},{1,5},{9... | collective-permute-start | bytes 1493000 | tf_op jit(solution)/shard_map/ppermute | solution.py:113
  217.5 16.0 %collective-permute-start.47 = (bf16[72,1728]{1,0:T(8,128)(2,1)}, bf16[72,1728]{1,0:T(8,128)(2,1)S(1)}, u32[]{:S(2)}, u32[]{:S(2)}) collective-permute-start(bf16[72,1728]{1,0:T(8,128)(2,1)} %collective-permute-done.46), channel_id=1, source_target_pairs={{0,4},{8,0},{16,8},{24,16},{28,24},{20,28},{12,20},{4,12},{1,5},{9... | collective-permute-start | bytes 746504 | tf_op jit(solution)/shard_map/ppermute | solution.py:113
  218.3 16.5 %collective-permute-start.40 = (bf16[72,1728]{1,0:T(8,128)(2,1)}, bf16[72,1728]{1,0:T(8,128)(2,1)S(1)}, u32[]{:S(2)}, u32[]{:S(2)}) collective-permute-start(bf16[72,1728]{1,0:T(8,128)(2,1)} %collective-permute-done.39), channel_id=1, source_target_pairs={{0,8},{8,16},{16,24},{24,28},{28,20},{20,12},{12,4},{4,0},{1,9},{9... | collective-permute-start | bytes 746504 | tf_op jit(solution)/shard_map/ppermute | solution.py:113
  223.9 22.9 %collective-permute-start.17 = (bf16[256,1152]{1,0:T(8,128)(2,1)}, bf16[256,1152]{1,0:T(8,128)(2,1)S(1)}, u32[]{:S(2)}, u32[]{:S(2)}) collective-permute-start(bf16[256,1152]{1,0:T(8,128)(2,1)} %slice.367), channel_id=1, source_target_pairs={{0,1},{1,0},{2,3},{3,2},{4,5},{5,4},{6,7},{7,6},{8,9},{9,8},{10,11... | collective-permute-start | bytes 1769480 | tf_op jit(solution)/shard_map/ppermute | solution.py:63
  238.2 13.8 %collective-permute-start.31 = (bf16[144,1728]{1,0:T(8,128)(2,1)}, bf16[144,1728]{1,0:T(8,128)(2,1)S(1)}, u32[]{:S(2)}, u32[]{:S(2)}) collective-permute-start(bf16[144,1728]{1,0:T(8,128)(2,1)} %collective-permute-done.30), channel_id=1, source_target_pairs={{0,4},{8,0},{16,8},{24,16},{28,24},{20,28},{12,20},{4,12},{1,5},{9... | collective-permute-start | bytes 1493000 | tf_op jit(solution)/shard_map/ppermute | solution.py:113
  245.5 12.1 %collective-permute-start.25 = (bf16[144,1728]{1,0:T(8,128)(2,1)}, bf16[144,1728]{1,0:T(8,128)(2,1)S(1)}, u32[]{:S(2)}, u32[]{:S(2)}) collective-permute-start(bf16[144,1728]{1,0:T(8,128)(2,1)} %collective-permute-done.24), channel_id=1, source_target_pairs={{0,8},{8,16},{16,24},{24,28},{28,20},{20,12},{12,4},{4,0},{1,9},{9... | collective-permute-start | bytes 1493000 | tf_op jit(solution)/shard_map/ppermute | solution.py:113
  247.8 12.0 %collective-permute-start.18 = (bf16[256,1152]{1,0:T(8,128)(2,1)S(1)}, bf16[256,1152]{1,0:T(8,128)(2,1)S(1)}, u32[]{:S(2)}, u32[]{:S(2)}) collective-permute-start(bf16[256,1152]{1,0:T(8,128)(2,1)S(1)} %multiply_convert_fusion.4), channel_id=1, source_target_pairs={{0,1},{1,0},{2,3},{3,2},{4,5},{5,4},{6,7},{7,6},{8,9},{9,8},{10,11... | collective-permute-start | bytes 1769480 | tf_op jit(solution)/shard_map/ppermute | solution.py:63
  260.0 15.9 %collective-permute-start.19 = (bf16[512,1152]{1,0:T(8,128)(2,1)S(1)}, bf16[512,1152]{1,0:T(8,128)(2,1)S(1)}, u32[]{:S(2)}, u32[]{:S(2)}) collective-permute-start(bf16[512,1152]{1,0:T(8,128)(2,1)S(1)} %pad_maximum_fusion.6), channel_id=1, source_target_pairs={{0,2},{2,0},{1,3},{3,1},{4,6},{6,4},{5,7},{7,5},{8,10},{10,8},{9,1... | collective-permute-start | bytes 3538952 | tf_op jit(solution)/shard_map/ppermute | solution.py:63
  262.4 12.6 %collective-permute-start.33 = (bf16[144,1728]{1,0:T(8,128)(2,1)S(1)}, bf16[144,1728]{1,0:T(8,128)(2,1)S(1)}, u32[]{:S(2)}, u32[]{:S(2)}) collective-permute-start(bf16[144,1728]{1,0:T(8,128)(2,1)S(1)} %collective-permute-done.32), channel_id=1, source_target_pairs={{0,4},{8,0},{16,8},{24,16},{28,24},{20,28},{12,20},{4,12},{1,5},{9... | collective-permute-start | bytes 1493000 | tf_op jit(solution)/shard_map/ppermute | solution.py:113
  312.5 27.6 %all-to-all-start.7 = ((bf16[8,32,1152]{2,1,0:T(8,128)(2,1)}), bf16[8,32,1152]{2,1,0:T(8,128)(2,1)}, u32[]{:S(2)}, u32[]{:S(2)}) async-start(bf16[8,32,1152]{2,1,0:T(8,128)(2,1)} %bitcast.299), calls=%async_computation.7 | async-start | bytes 1179648 | tf_op jit(solution)/shard_map/all_to_all | solution.py:212
  321.2 16.1 %collective-permute-start.49 = (bf16[256,1152]{1,0:T(8,128)(2,1)}, bf16[256,1152]{1,0:T(8,128)(2,1)}, u32[]{:S(2)}, u32[]{:S(2)}) collective-permute-start(bf16[256,1152]{1,0:T(8,128)(2,1)} %slice.366), channel_id=1, source_target_pairs={{0,1},{1,0},{2,3},{3,2},{4,5},{5,4},{6,7},{7,6},{8,9},{9,8},{10,11... | collective-permute-start | bytes 1769480 | tf_op jit(solution)/shard_map/ppermute | solution.py:63
  345.8 15.0 %collective-permute-start.50 = (bf16[256,1152]{1,0:T(8,128)(2,1)S(1)}, bf16[256,1152]{1,0:T(8,128)(2,1)S(1)}, u32[]{:S(2)}, u32[]{:S(2)}) collective-permute-start(bf16[256,1152]{1,0:T(8,128)(2,1)S(1)} %get-tuple-element.42), channel_id=1, source_target_pairs={{0,1},{1,0},{2,3},{3,2},{4,5},{5,4},{6,7},{7,6},{8,9},{9,8},{10,11... | collective-permute-start | bytes 1769480 | tf_op jit(solution)/shard_map/ppermute | solution.py:63
  361.9 25.6 %collective-permute-start.51 = (bf16[512,1152]{1,0:T(8,128)(2,1)}, bf16[512,1152]{1,0:T(8,128)(2,1)}, u32[]{:S(2)}, u32[]{:S(2)}) collective-permute-start(bf16[512,1152]{1,0:T(8,128)(2,1)} %pad_maximum_fusion.7), channel_id=1, source_target_pairs={{0,2},{2,0},{1,3},{3,1},{4,6},{6,4},{5,7},{7,5},{8,10},{10,8},{9,1... | collective-permute-start | bytes 3538952 | tf_op jit(solution)/shard_map/ppermute | solution.py:63
  381.7 262.9 %all-to-all-start.6 = ((bf16[8,32,1152]{2,1,0:T(8,128)(2,1)}), bf16[8,32,1152]{2,1,0:T(8,128)(2,1)}, u32[]{:S(2)}, u32[]{:S(2)}) async-start(bf16[8,32,1152]{2,1,0:T(8,128)(2,1)} %bitcast.290), calls=%async_computation.6 | async-start | bytes 1179648 | tf_op jit(solution)/shard_map/all_to_all | solution.py:216
  420.2 63.8 %collective-permute-start.52 = (bf16[512,1152]{1,0:T(8,128)(2,1)S(1)}, bf16[512,1152]{1,0:T(8,128)(2,1)S(1)}, u32[]{:S(2)}, u32[]{:S(2)}) collective-permute-start(bf16[512,1152]{1,0:T(8,128)(2,1)S(1)} %slice.361), channel_id=1, source_target_pairs={{0,2},{2,0},{1,3},{3,1},{4,6},{6,4},{5,7},{7,5},{8,10},{10,8},{9,1... | collective-permute-start | bytes 3538952 | tf_op jit(solution)/shard_map/ppermute | solution.py:63
  420.5 25.9 %collective-permute-start.81 = (bf16[144,1728]{1,0:T(8,128)(2,1)S(1)}, bf16[144,1728]{1,0:T(8,128)(2,1)S(1)}, u32[]{:S(2)}, u32[]{:S(2)}) collective-permute-start(bf16[144,1728]{1,0:T(8,128)(2,1)S(1)} %convolution_convert_fusion.1), channel_id=1, source_target_pairs={{0,8},{8,16},{16,24},{24,28},{28,20},{20,12},{12,4},{4,0},{1,9},{9... | collective-permute-start | bytes 1493000 | tf_op jit(solution)/shard_map/ppermute | solution.py:124
  422.6 27.0 %collective-permute-start.88 = (bf16[144,1728]{1,0:T(8,128)(2,1)S(1)}, bf16[144,1728]{1,0:T(8,128)(2,1)S(1)}, u32[]{:S(2)}, u32[]{:S(2)}) collective-permute-start(bf16[144,1728]{1,0:T(8,128)(2,1)S(1)} %convolution_convert_fusion), channel_id=1, source_target_pairs={{0,4},{8,0},{16,8},{24,16},{28,24},{20,28},{12,20},{4,12},{1,5},{9... | collective-permute-start | bytes 1493000 | tf_op jit(solution)/shard_map/ppermute | solution.py:124
  425.4 16.5 %collective-permute-start.102 = (bf16[72,1728]{1,0:T(8,128)(2,1)S(1)}, bf16[72,1728]{1,0:T(8,128)(2,1)S(1)}, u32[]{:S(2)}, u32[]{:S(2)}) collective-permute-start(bf16[72,1728]{1,0:T(8,128)(2,1)S(1)} %convolution_convert_fusion.2), channel_id=1, source_target_pairs={{0,4},{8,0},{16,8},{24,16},{28,24},{20,28},{12,20},{4,12},{1,5},{9... | collective-permute-start | bytes 746504 | tf_op jit(solution)/shard_map/ppermute | solution.py:124
  428.6 15.0 %collective-permute-start.95 = (bf16[72,1728]{1,0:T(8,128)(2,1)S(1)}, bf16[72,1728]{1,0:T(8,128)(2,1)S(1)}, u32[]{:S(2)}, u32[]{:S(2)}) collective-permute-start(bf16[72,1728]{1,0:T(8,128)(2,1)S(1)} %convolution_convert_fusion.3), channel_id=1, source_target_pairs={{0,8},{8,16},{16,24},{24,28},{28,20},{20,12},{12,4},{4,0},{1,9},{9... | collective-permute-start | bytes 746504 | tf_op jit(solution)/shard_map/ppermute | solution.py:124
  448.0 25.6 %collective-permute-start.82 = (bf16[144,1728]{1,0:T(8,128)(2,1)S(1)}, bf16[144,1728]{1,0:T(8,128)(2,1)S(1)}, u32[]{:S(2)}, u32[]{:S(2)}) collective-permute-start(bf16[144,1728]{1,0:T(8,128)(2,1)S(1)} %add_convert_fusion.12), channel_id=1, source_target_pairs={{0,8},{8,16},{16,24},{24,28},{28,20},{20,12},{12,4},{4,0},{1,9},{9... | collective-permute-start | bytes 1493000 | tf_op jit(solution)/shard_map/ppermute | solution.py:124
  451.0 25.6 %collective-permute-start.89 = (bf16[144,1728]{1,0:T(8,128)(2,1)S(1)}, bf16[144,1728]{1,0:T(8,128)(2,1)S(1)}, u32[]{:S(2)}, u32[]{:S(2)}) collective-permute-start(bf16[144,1728]{1,0:T(8,128)(2,1)S(1)} %add_convert_fusion.6), channel_id=1, source_target_pairs={{0,4},{8,0},{16,8},{24,16},{28,24},{20,28},{12,20},{4,12},{1,5},{9... | collective-permute-start | bytes 1493000 | tf_op jit(solution)/shard_map/ppermute | solution.py:124
  452.9 15.9 %collective-permute-start.104 = (bf16[72,1728]{1,0:T(8,128)(2,1)S(1)}, bf16[72,1728]{1,0:T(8,128)(2,1)S(1)}, u32[]{:S(2)}, u32[]{:S(2)}) collective-permute-start(bf16[72,1728]{1,0:T(8,128)(2,1)S(1)} %add_convert_fusion.17), channel_id=1, source_target_pairs={{0,4},{8,0},{16,8},{24,16},{28,24},{20,28},{12,20},{4,12},{1,5},{9... | collective-permute-start | bytes 746504 | tf_op jit(solution)/shard_map/ppermute | solution.py:124
  455.2 15.4 %collective-permute-start.97 = (bf16[72,1728]{1,0:T(8,128)(2,1)S(1)}, bf16[72,1728]{1,0:T(8,128)(2,1)S(1)}, u32[]{:S(2)}, u32[]{:S(2)}) collective-permute-start(bf16[72,1728]{1,0:T(8,128)(2,1)S(1)} %add_convert_fusion.23), channel_id=1, source_target_pairs={{0,8},{8,16},{16,24},{24,28},{28,20},{20,12},{12,4},{4,0},{1,9},{9... | collective-permute-start | bytes 746504 | tf_op jit(solution)/shard_map/ppermute | solution.py:124
  475.1 23.8 %collective-permute-start.83 = (bf16[144,1728]{1,0:T(8,128)(2,1)S(1)}, bf16[144,1728]{1,0:T(8,128)(2,1)S(1)}, u32[]{:S(2)}, u32[]{:S(2)}) collective-permute-start(bf16[144,1728]{1,0:T(8,128)(2,1)S(1)} %add_convert_fusion.11), channel_id=1, source_target_pairs={{0,8},{8,16},{16,24},{24,28},{28,20},{20,12},{12,4},{4,0},{1,9},{9... | collective-permute-start | bytes 1493000 | tf_op jit(solution)/shard_map/ppermute | solution.py:124
  478.1 23.8 %collective-permute-start.90 = (bf16[144,1728]{1,0:T(8,128)(2,1)S(1)}, bf16[144,1728]{1,0:T(8,128)(2,1)S(1)}, u32[]{:S(2)}, u32[]{:S(2)}) collective-permute-start(bf16[144,1728]{1,0:T(8,128)(2,1)S(1)} %add_convert_fusion.5), channel_id=1, source_target_pairs={{0,4},{8,0},{16,8},{24,16},{28,24},{20,28},{12,20},{4,12},{1,5},{9... | collective-permute-start | bytes 1493000 | tf_op jit(solution)/shard_map/ppermute | solution.py:124
  480.0 14.4 %collective-permute-start.106 = (bf16[72,1728]{1,0:T(8,128)(2,1)S(1)}, bf16[72,1728]{1,0:T(8,128)(2,1)S(1)}, u32[]{:S(2)}, u32[]{:S(2)}) collective-permute-start(bf16[72,1728]{1,0:T(8,128)(2,1)S(1)} %add_convert_fusion.15), channel_id=1, source_target_pairs={{0,4},{8,0},{16,8},{24,16},{28,24},{20,28},{12,20},{4,12},{1,5},{9... | collective-permute-start | bytes 746504 | tf_op jit(solution)/shard_map/ppermute | solution.py:124
  482.4 13.8 %collective-permute-start.99 = (bf16[72,1728]{1,0:T(8,128)(2,1)S(1)}, bf16[72,1728]{1,0:T(8,128)(2,1)S(1)}, u32[]{:S(2)}, u32[]{:S(2)}) collective-permute-start(bf16[72,1728]{1,0:T(8,128)(2,1)S(1)} %add_convert_fusion.21), channel_id=1, source_target_pairs={{0,8},{8,16},{16,24},{24,28},{28,20},{20,12},{12,4},{4,0},{1,9},{9... | collective-permute-start | bytes 746504 | tf_op jit(solution)/shard_map/ppermute | solution.py:124
  484.4 36.8 %collective-permute-start.53 = (bf16[256,1152]{1,0:T(8,128)(2,1)S(1)}, bf16[256,1152]{1,0:T(8,128)(2,1)S(1)}, u32[]{:S(2)}, u32[]{:S(2)}) collective-permute-start(bf16[256,1152]{1,0:T(8,128)(2,1)S(1)} %slice.365), channel_id=1, source_target_pairs={{0,1},{1,0},{2,3},{3,2},{4,5},{5,4},{6,7},{7,6},{8,9},{9,8},{10,11... | collective-permute-start | bytes 1769480 | tf_op jit(solution)/shard_map/ppermute | solution.py:63
  500.4 25.0 %collective-permute-start.84 = (bf16[144,1728]{1,0:T(8,128)(2,1)S(1)}, bf16[144,1728]{1,0:T(8,128)(2,1)S(1)}, u32[]{:S(2)}, u32[]{:S(2)}) collective-permute-start(bf16[144,1728]{1,0:T(8,128)(2,1)S(1)} %add_convert_fusion.10), channel_id=1, source_target_pairs={{0,8},{8,16},{16,24},{24,28},{28,20},{20,12},{12,4},{4,0},{1,9},{9... | collective-permute-start | bytes 1493000 | tf_op jit(solution)/shard_map/ppermute | solution.py:124
  503.5 25.0 %collective-permute-start.91 = (bf16[144,1728]{1,0:T(8,128)(2,1)S(1)}, bf16[144,1728]{1,0:T(8,128)(2,1)S(1)}, u32[]{:S(2)}, u32[]{:S(2)}) collective-permute-start(bf16[144,1728]{1,0:T(8,128)(2,1)S(1)} %add_convert_fusion.4), channel_id=1, source_target_pairs={{0,4},{8,0},{16,8},{24,16},{28,24},{20,28},{12,20},{4,12},{1,5},{9... | collective-permute-start | bytes 1493000 | tf_op jit(solution)/shard_map/ppermute | solution.py:124
  505.3 13.2 %collective-permute-start.108 = (bf16[72,1728]{1,0:T(8,128)(2,1)S(1)}, bf16[72,1728]{1,0:T(8,128)(2,1)S(1)}, u32[]{:S(2)}, u32[]{:S(2)}) collective-permute-start(bf16[72,1728]{1,0:T(8,128)(2,1)S(1)} %add_convert_fusion.13), channel_id=1, source_target_pairs={{0,4},{8,0},{16,8},{24,16},{28,24},{20,28},{12,20},{4,12},{1,5},{9... | collective-permute-start | bytes 746504 | tf_op jit(solution)/shard_map/ppermute | solution.py:124
  507.8 12.0 %collective-permute-start.101 = (bf16[72,1728]{1,0:T(8,128)(2,1)S(1)}, bf16[72,1728]{1,0:T(8,128)(2,1)S(1)}, u32[]{:S(2)}, u32[]{:S(2)}) collective-permute-start(bf16[72,1728]{1,0:T(8,128)(2,1)S(1)} %add_convert_fusion.19), channel_id=1, source_target_pairs={{0,8},{8,16},{16,24},{24,28},{28,20},{20,12},{12,4},{4,0},{1,9},{9... | collective-permute-start | bytes 746504 | tf_op jit(solution)/shard_map/ppermute | solution.py:124
  542.9 22.1 %collective-permute-start.55 = (bf16[512,1152]{1,0:T(8,128)(2,1)S(1)}, bf16[512,1152]{1,0:T(8,128)(2,1)S(1)}, u32[]{:S(2)}, u32[]{:S(2)}) collective-permute-start(bf16[512,1152]{1,0:T(8,128)(2,1)S(1)} %pad_maximum_fusion.8), channel_id=1, source_target_pairs={{0,2},{2,0},{1,3},{3,1},{4,6},{6,4},{5,7},{7,5},{8,10},{10,8},{9,1... | collective-permute-start | bytes 3538952 | tf_op jit(solution)/shard_map/ppermute | solution.py:63
  582.3 49.5 %collective-permute-start.56 = (bf16[512,1152]{1,0:T(8,128)(2,1)S(1)}, bf16[512,1152]{1,0:T(8,128)(2,1)S(1)}, u32[]{:S(2)}, u32[]{:S(2)}) collective-permute-start(bf16[512,1152]{1,0:T(8,128)(2,1)S(1)} %slice.360), channel_id=1, source_target_pairs={{0,2},{2,0},{1,3},{3,1},{4,6},{6,4},{5,7},{7,5},{8,10},{10,8},{9,1... | collective-permute-start | bytes 3538952 | tf_op jit(solution)/shard_map/ppermute | solution.py:63
  588.4 28.6 %collective-permute-start.65 = (bf16[8,72,512]{2,1,0:T(8,128)(2,1)S(1)}, bf16[8,72,512]{2,1,0:T(8,128)(2,1)S(1)}, u32[]{:S(2)}, u32[]{:S(2)}) collective-permute-start(bf16[8,72,512]{2,1,0:T(8,128)(2,1)S(1)} %fusion.49), channel_id=1, source_target_pairs={{0,2},{2,0},{1,3},{3,1},{4,6},{6,4},{5,7},{7,5},{8,10},{10,8},{9,1... | collective-permute-start | bytes 1769480 | tf_op jit(solution)/shard_map/ppermute | solution.py:63
  623.1 13.2 %collective-permute-start.80 = (bf16[144,256]{1,0:T(8,128)(2,1)S(1)}, bf16[144,256]{1,0:T(8,128)(2,1)S(1)}, u32[]{:S(2)}, u32[]{:S(2)}) collective-permute-start(bf16[144,256]{1,0:T(8,128)(2,1)S(1)} %add_convert_fusion.25), channel_id=1, source_target_pairs={{0,8},{8,16},{16,24},{24,28},{28,20},{20,12},{12,4},{4,0},{1,9},{9... | collective-permute-start | bytes 221192 | tf_op jit(solution)/shard_map/ppermute | solution.py:124
  640.7 33.3 %collective-permute-start.71 = (bf16[72,512]{1,0:T(8,128)(2,1)}, bf16[72,512]{1,0:T(8,128)(2,1)}, u32[]{:S(2)}, u32[]{:S(2)}) collective-permute-start(bf16[72,512]{1,0:T(8,128)(2,1)} %fusion.214), channel_id=1, source_target_pairs={{0,8},{8,16},{16,24},{24,28},{28,20},{20,12},{12,4},{4,0},{1,9},{9... | collective-permute-start | bytes 221192 | tf_op jit(solution)/shard_map/ppermute | solution.py:124
  669.7 51.6 %all-to-all-start.8 = ((bf16[8,32,1152]{2,1,0:T(8,128)(2,1)}), bf16[8,32,1152]{2,1,0:T(8,128)(2,1)}, u32[]{:S(2)}, u32[]{:S(2)}) async-start(bf16[8,32,1152]{2,1,0:T(8,128)(2,1)} %bitcast.289), calls=%async_computation.8 | async-start | bytes 1179648 | tf_op jit(solution)/shard_map/all_to_all | solution.py:216
  685.9 28.7 %collective-permute-start.73 = (f32[72,512]{1,0:T(8,128)S(1)}, f32[72,512]{1,0:T(8,128)S(1)}, u32[]{:S(2)}, u32[]{:S(2)}) collective-permute-start(f32[72,512]{1,0:T(8,128)S(1)} %bitcast_add_fusion.2), channel_id=1, source_target_pairs={{0,1},{1,0},{2,3},{3,2},{4,5},{5,4},{6,7},{7,6},{8,9},{9,8},{10,11... | collective-permute-start | bytes 442376 | tf_op jit(solution)/shard_map/ppermute | solution.py:63
  699.1 15.6 %collective-permute-start.112 = (f32[40,128]{1,0:T(8,128)}, f32[40,128]{1,0:T(8,128)}, u32[]{:S(2)}, u32[]{:S(2)}) collective-permute-start(f32[40,128]{1,0:T(8,128)} %add.1514), channel_id=1, source_target_pairs={{0,8},{4,12},{8,0},{12,4},{16,24},{20,28},{24,16},{28,20},{1,9},{5... | collective-permute-start | bytes 61448 | tf_op jit(solution)/shard_map/ppermute | solution.py:134
  (165 other events, 1478.8 us)
Sparse Core Ops, SparseCore 0:
  141.1 8.0 all-gather.1

commit v2 on v1

v2 whole, which is shorter than its diff:
```python
import functools

import jax
import jax.numpy as jnp
from jax import lax
from jax.experimental import pallas as pl
from jax.experimental.pallas import tpu as pltpu
from jax.sharding import Mesh
from jax.sharding import PartitionSpec as P

HD = 256
PIC = 256
EPSILON = 1e-06
ROPE_BASE = 1000000.0
SCALE = HD ** (-0.5)
TILE = 256
F32 = jnp.float32
BF16 = jnp.bfloat16


def dot(left, right, dims):
    return lax.dot_general(left, right, ((dims[0], dims[1]), ((), ())), preferred_element_type=F32)


def mm(left, right):
    return dot(left, right, ((1,), (0,)))


def mm_nt(left, right):
    return dot(left, right, ((1,), (1,)))


def mm_tn(left, right):
    return dot(left, right, ((0,), (0,)))


def inverse_root(values):
    return lax.rsqrt(jnp.mean(values * values, axis=-1, keepdims=True) + EPSILON)


def norm_back(values, factor, grad):
    root = inverse_root(values)
    scaled = grad * factor
    inner = jnp.mean(values * scaled, axis=-1, keepdims=True)
    grad_values = root * (scaled - values * (root * root * inner))
    return grad_values, jnp.sum(grad * (values * root), axis=0, keepdims=True)


def turn(values, cosine, sine):
    half = values.shape[-1] // 2
    first = values[..., :half]
    second = values[..., half:]
    return jnp.concatenate([first * cosine - second * sine, second * cosine + first * sine], axis=-1)


def gelu_parts(v):
    c = (2.0 / jnp.pi) ** 0.5
    square = v * v
    t = jnp.tanh(c * v * (1.0 + 0.044715 * square))
    value = 0.5 * v * (1.0 + t)
    slope = 0.5 * (1.0 + t) + 0.5 * v * (1.0 - t * t) * (c * (1.0 + 0.134145 * square))
    return value, slope


def call(kernel, outs, ins, scratch=(), mib=48, flops=0, moved=0, **more):
    return pl.pallas_call(
        kernel,
        out_shape=outs,
        scratch_shapes=list(scratch),
        compiler_params=pltpu.CompilerParams(vmem_limit_bytes=mib << 20),
        cost_estimate=pl.CostEstimate(flops=0, bytes_accessed=1, transcendentals=0),
        **more,
    )(*ins)


def small_call(kernel, outs, ins, **more):
    vmem = pl.BlockSpec(memory_space=pltpu.VMEM)
    moved = sum(v.size * v.dtype.itemsize for v in (*ins, *outs))
    return call(
        kernel, outs, ins, in_specs=[vmem] * len(ins), out_specs=[vmem] * len(outs), moved=moved, **more
    )


def struct(shape, kind):
    return jax.ShapeDtypeStruct(shape, kind)


def total_of(refs):
    total = refs[0][...].astype(F32)
    for ref in refs[1:]:
        total = total + ref[...].astype(F32)
    return total


def start_kernel(x_ref, gain_ref, a_ref):
    x = x_ref[...].astype(F32)
    a_ref[...] = (x * inverse_root(x) * gain_ref[...]).astype(BF16)


def middle_kernel(count, *refs):
    x_ref, g_ao, g_fi = refs[count : count + 3]
    r_ref, mid_ref, f_ref = refs[count + 3 :]
    r = total_of(refs[:count])
    mid = x_ref[...].astype(F32) + r * inverse_root(r) * g_ao[...]
    r_ref[...] = r
    mid_ref[...] = mid
    f_ref[...] = (mid * inverse_root(mid) * g_fi[...]).astype(BF16)


def close_kernel(count, *refs):
    mid_ref, cot_ref, g_fo = refs[count : count + 3]
    out_ref, de_ref, gain_ref = refs[count + 3 :]
    e = total_of(refs[:count])
    cot = cot_ref[...].astype(F32)
    out_ref[...] = (mid_ref[...] + e * inverse_root(e) * g_fo[...]).astype(BF16)
    de, gain = norm_back(e, g_fo[...], cot)
    de_ref[...] = de.astype(BF16)
    gain_ref[...] = gain


def turn_kernel(count, *refs):
    mid_ref, cot_ref, r_ref, g_fi, g_ao = refs[count : count + 5]
    dmid_ref, dr_ref, gain_fi, gain_ao = refs[count + 5 :]
    back, gain = norm_back(mid_ref[...], g_fi[...], total_of(refs[:count]))
    gain_fi[...] = gain
    dmid = cot_ref[...].astype(F32) + back
    dmid_ref[...] = dmid
    dr, gain = norm_back(r_ref[...], g_ao[...], dmid)
    gain_ao[...] = gain
    dr_ref[...] = dr.astype(BF16)


def last_kernel(count, *refs):
    x_ref, dmid_ref, g_in = refs[count : count + 3]
    dx_ref, gain_ref = refs[count + 3 :]
    back, gain = norm_back(x_ref[...].astype(F32), g_in[...], total_of(refs[:count]))
    dx_ref[...] = (dmid_ref[...] + back).astype(BF16)
    gain_ref[...] = gain


def attend_kernel(count, q_blocks, *refs):
    a_refs = refs[:count]
    qkv, out_w, cosine, sine, g_q, g_k, meta_q, meta_k = refs[count : count + 8]
    o_ref, prob_ref, raw_ref, q_ref, k_ref, v_ref = refs[count + 8 : count + 14]
    r_refs = refs[count + 14 :]
    size = a_refs[0].shape[0]
    for i, a_ref in enumerate(a_refs):
        rows = slice(i * size, (i + 1) * size)
        raw = mm(a_ref[...], qkv[...])
        raw_ref[rows] = raw[:, : 2 * HD].astype(BF16)
        cos, sin = cosine[rows], sine[rows]
        query, key = raw[:, :HD], raw[:, HD : 2 * HD]
        q_ref[rows] = (turn(query * inverse_root(query) * g_q[...], cos, sin) * SCALE).astype(BF16)
        k_ref[rows] = turn(key * inverse_root(key) * g_k[...], cos, sin).astype(BF16)
        v_ref[rows] = raw[:, 2 * HD :].astype(BF16)
    key_doc, key_place, key_pic = meta_k[0:1], meta_k[1:2], meta_k[2:3]
    for n, i in enumerate(q_blocks):
        rows = slice(i * size, (i + 1) * size)
        done = slice(n * size, (n + 1) * size)
        scores = mm_nt(q_ref[rows], k_ref[...])
        doc, place, pic = meta_q[rows, 0:1], meta_q[rows, 1:2], meta_q[rows, 2:3]
        allowed = (doc == key_doc) & ((key_place <= place) | ((pic == key_pic) & (pic >= 0)))
        scores = jnp.where(allowed, scores, -1e30)
        weight = jnp.exp(scores - jnp.max(scores, axis=-1, keepdims=True))
        prob = (weight * (1.0 / jnp.sum(weight, axis=-1, keepdims=True))).astype(BF16)
        prob_ref[done] = prob
        o = mm(prob, v_ref[...]).astype(BF16)
        o_ref[done] = o
        r_refs[n][...] = mm_nt(o, out_w[...]).astype(BF16)


def attend_back_kernel(count, q_blocks, total, *refs):
    dr_refs = refs[:count]
    prob_ref, raw_ref, q_ref, k_ref, v_ref, qkv, out_w, cosine, sine, g_q, g_k = refs[count : count + 11]
    grad_ref, gain_q, gain_k = refs[count + 11 : count + 14]
    da_refs = refs[count + 14 : count + 14 + total]
    dk_ref, dv_ref = refs[count + 14 + total :]
    size = dr_refs[0].shape[0]
    if len(q_blocks) != total:
        grad_ref[:, :HD] = jnp.zeros((size * total, HD), BF16)
    sum_q = jnp.zeros((1, HD), F32)
    sum_k = jnp.zeros((1, HD), F32)
    for n, i in enumerate(q_blocks):
        rows = slice(i * size, (i + 1) * size)
        done = slice(n * size, (n + 1) * size)
        do = mm(dr_refs[n][...], out_w[...]).astype(BF16)
        prob_low = prob_ref[done]
        prob = prob_low.astype(F32)
        dprob = mm_nt(do, v_ref[...])
        ds = (prob * (dprob - jnp.sum(prob * dprob, axis=-1, keepdims=True))).astype(BF16)
        dq = mm(ds, k_ref[...])
        dk = mm_tn(ds, q_ref[rows])
        dv = mm_tn(prob_low, do)
        if n == 0:
            dk_ref[...] = dk
            dv_ref[...] = dv
        else:
            dk_ref[...] += dk
            dv_ref[...] += dv
        raw = raw_ref[rows, :HD].astype(F32)
        back, gain = norm_back(raw, g_q[...], turn(dq * SCALE, cosine[rows], -sine[rows]))
        grad_ref[rows, :HD] = back.astype(BF16)
        sum_q = sum_q + gain
    for i in range(total):
        rows = slice(i * size, (i + 1) * size)
        raw = raw_ref[rows, HD:].astype(F32)
        back, gain = norm_back(raw, g_k[...], turn(dk_ref[rows], cosine[rows], -sine[rows]))
        grad_ref[rows, HD : 2 * HD] = back.astype(BF16)
        grad_ref[rows, 2 * HD :] = dv_ref[rows].astype(BF16)
        sum_k = sum_k + gain
        da_refs[i][...] = mm_nt(grad_ref[rows], qkv[...]).astype(BF16)
    gain_q[...] = sum_q
    gain_k[...] = sum_k


def hidden_kernel(count, *refs):
    gate_w, up_w, keep_gate, keep_up, hid_ref = refs[count:]
    size = refs[0].shape[0]
    for i in range(count):
        rows = slice(i * size, (i + 1) * size)
        gate = mm(refs[i][...], gate_w[...])
        up = mm(refs[i][...], up_w[...])
        value, slope = gelu_parts(gate)
        keep_gate[rows] = (up * slope).astype(BF16)
        keep_up[rows] = value.astype(BF16)
        hid_ref[rows] = (value * up).astype(BF16)


def down_kernel(hid_ref, down_w, *outs):
    size = outs[0].shape[0]
    part = mm_nt(hid_ref[...], down_w[...]).astype(BF16)
    for i, out in enumerate(outs):
        out[...] = part[i * size : (i + 1) * size]


def hidden_back_kernel(count, *refs):
    keep_gate, keep_up, gate_w, up_w, down_w, dgate_ref, dup_ref = refs[count : count + 7]
    df_refs = refs[count + 7 :]
    size = refs[0].shape[0]
    for i in range(count):
        rows = slice(i * size, (i + 1) * size)
        dhid = mm(refs[i][...], down_w[...])
        dgate_ref[rows] = (dhid * keep_gate[rows].astype(F32)).astype(BF16)
        dup_ref[rows] = (dhid * keep_up[rows].astype(F32)).astype(BF16)
        df_refs[i][...] = (mm_nt(dgate_ref[rows], gate_w[...]) + mm_nt(dup_ref[rows], up_w[...])).astype(BF16)


def hidden_forward(pieces, gate_w, up_w):
    size, hidden = pieces[0].shape[0], gate_w.shape[1]
    return small_call(
        functools.partial(hidden_kernel, len(pieces)),
        [struct((len(pieces) * size, hidden), BF16)] * 3,
        (*pieces, gate_w, up_w),
        mib=24,
    )


def down_forward(hid, down_w, count):
    shape = hid.shape[0] // count, down_w.shape[0]
    return small_call(down_kernel, [struct(shape, BF16)] * count, (hid, down_w), mib=24)


def hidden_backward(pieces, keep_gate, keep_up, gate_w, up_w, down_w):
    size, width = pieces[0].shape
    count, hidden = len(pieces), gate_w.shape[1]
    return small_call(
        functools.partial(hidden_back_kernel, count),
        [struct((count * size, hidden), BF16)] * 2 + [struct((size, width), BF16)] * count,
        (*pieces, keep_gate, keep_up, gate_w, up_w, down_w),
        mib=24,
    )


def outer_kernel(groups, spots, *refs):
    count = spots.shape[0]
    outs, whole = refs[-1 - count : -1], refs[-1]
    feats = whole.shape[0] // count
    used, column = 0, 0
    for lefts, rights in groups:
        left = jnp.concatenate([r[...] for r in refs[used : used + lefts]], axis=0)
        right = jnp.concatenate([r[...] for r in refs[used + lefts : used + lefts + rights]], axis=0)
        whole[:, column : column + right.shape[1]] = mm_tn(left, right).astype(BF16)
        used, column = used + lefts + rights, column + right.shape[1]
    for k, out in enumerate(outs):
        first = pl.multiple_of(spots[(k + 1) % count] * feats, 16)
        out[...] = whole[pl.ds(first, feats), :]


def outer(products, spots):
    count = spots.shape[0]
    width = products[0][0][0].shape[1]
    total = sum(right[0].shape[1] for _, right in products)
    ins = [v for left, right in products for v in (*left, *right)]
    vmem = pl.BlockSpec(memory_space=pltpu.VMEM)
    return call(
        functools.partial(outer_kernel, [(len(left), len(right)) for left, right in products]),
        [struct((width // count, total), BF16)] * count,
        (spots, *ins),
        scratch=[pltpu.VMEM((width, total), BF16)],
        in_specs=[pl.BlockSpec(memory_space=pltpu.SMEM)] + [vmem] * len(ins),
        out_specs=[vmem] * count,
        mib=32,
    )


def layout(lengths, starts, places):
    doc_ends = jnp.cumsum(lengths)
    before = places[:, None] >= doc_ends[None, :]
    doc_ids = jnp.sum(before.astype(jnp.int32), axis=1)
    opening = jnp.max(jnp.where(before, doc_ends[None, :], 0), axis=1)
    inside = (places[:, None] >= starts[None, :]) & (places[:, None] < starts[None, :] + PIC)
    labels = jnp.arange(1, starts.shape[0] + 1, dtype=jnp.int32)
    pictures = jnp.sum(jnp.where(inside, labels[None, :], 0), axis=1) - 1
    return doc_ids, places - opening, pictures


def shift(values, axis, step):
    size = lax.axis_size(axis)
    return lax.ppermute(values, axis, [(i, (i + step) % size) for i in range(size)])


def gather_rows(own):
    across = [own] + [shift(own, "tensor", k) for k in range(1, lax.axis_size("tensor"))]
    return [[p] + [shift(p, "core", k) for k in range(1, lax.axis_size("core"))] for p in across]


def scatter_rows(parts):
    result, sent = [], []
    for k in list(range(1, len(parts))) + [0]:
        first = [parts[k][0]] + [shift(p, "core", -j) for j, p in enumerate(parts[k]) if j]
        if k:
            total = first[0].astype(F32)
            for p in first[1:]:
                total = total + p.astype(F32)
            sent.append(total.astype(BF16))
            result.append(shift(sent[-1], "tensor", -k))
        else:
            result.extend(first)
    return result, sent


def ring_order(count):
    return list(range(0, count, 2)) + list(range(1, count, 2))[::-1]


def ring_spots():
    count = lax.axis_size("seq")
    ring = ring_order(count)
    table = [
        [[ring[(ring.index(i) - way * k) % count] for k in range(count)] for i in range(count)] for way in (1, -1)
    ]
    line = jnp.array(table, jnp.int32).reshape(2 * count, count)
    row = (lax.axis_index("core") % 2) * count + lax.axis_index("seq")
    line = lax.dynamic_index_in_dim(line, row, 0, keepdims=False, allow_negative_indices=False)
    return line, [line[k] for k in range(count)]


def together(values, *others):
    return lax.optimization_barrier((tuple(values), others))[0]


def hop(values):
    count, cores = lax.axis_size("seq"), lax.axis_size("core")
    ring = ring_order(count)
    pairs = [
        (ring[i] * cores + c, ring[(i + (-1) ** (c % 2)) % count] * cores + c)
        for i in range(count)
        for c in range(cores)
    ]
    return lax.ppermute(values, ("seq", "core"), pairs)


def put(full, block, row, spot):
    return lax.dynamic_update_slice(full, block[None], (spot, row, 0), allow_negative_indices=False)


def pick(array, spot, axis):
    return lax.dynamic_index_in_dim(array, spot, axis, keepdims=False, allow_negative_indices=False)


class RingSum:
    def __init__(self, blocks):
        self.blocks, self.hops = blocks, 0
        self.sum = blocks[0]

    def left(self):
        return len(self.blocks) - 1 - self.hops

    def step(self):
        self.hops += 1
        total = hop(self.sum).astype(F32) + self.blocks[self.hops].astype(F32)
        self.sum = total if self.left() == 0 else total.astype(BF16)

    def wait(self, *others):
        (self.sum,) = together([self.sum], *others)


def meet(rings, *others):
    values = [ring.sum for ring in rings]
    for ring in rings:
        ring.wait(*values, *others)


def exchanges():
    hops = []
    for axis in ("core", "tensor", "seq"):
        distance = 1
        while distance < lax.axis_size(axis):
            hops.append((axis, distance))
            distance *= 2
    return hops


def exchange(values, axis, distance):
    return values + lax.ppermute(values, axis, [(i, i ^ distance) for i in range(lax.axis_size(axis))])


def sum_tensor(values):
    if lax.axis_size("tensor") == 2:
        return values + shift(values, "tensor", 1)
    return lax.psum(values, "tensor")


def body(
    tokens,
    out_grad,
    doc_lengths,
    picture_starts,
    q_weight,
    k_weight,
    v_weight,
    out_weight,
    gate_weight,
    up_weight,
    down_weight,
    attn_in_gain,
    attn_out_gain,
    ffn_in_gain,
    ffn_out_gain,
    query_gain,
    key_gain,
):
    seqs = lax.axis_size("seq")
    cores = lax.axis_size("core")
    tensors = lax.axis_size("tensor")
    s_index = lax.axis_index("seq")
    c_index = lax.axis_index("core")
    t_index = lax.axis_index("tensor")
    micro, per_micro, span, width = tokens.shape
    split_heads = q_weight.shape[1] > HD
    assert q_weight.shape[1] == HD * (cores if split_heads else 1)
    own_feats = k_weight.shape[0]
    feats = own_feats * cores
    hidden_here = gate_weight.shape[1] // cores
    hidden = -(-hidden_here // TILE) * TILE

    def to_columns(arrays, padded):
        parts = [w.reshape(own_feats, cores, -1).transpose(1, 0, 2) for w in arrays]
        parts = [jnp.pad(p, ((0, 0), (0, 0), (0, padded - p.shape[2]))) for p in parts]
        moved = lax.all_to_all(jnp.concatenate(parts, axis=2), "core", split_axis=0, concat_axis=0, tiled=True)
        moved = moved.reshape(feats, -1)
        return [moved[:, i * padded : (i + 1) * padded] for i in range(len(arrays))]

    def to_rows(values):
        moved = lax.all_to_all(values.reshape(seqs, span, width), "seq", split_axis=0, concat_axis=0, tiled=True)
        return moved.reshape(seqs * span, width)

    def from_rows(values):
        moved = lax.all_to_all(values.reshape(seqs, span, width), "seq", split_axis=0, concat_axis=0, tiled=True)
        return moved.reshape(micro, per_micro, span, width)

    spot_line, spots = ring_spots()
    gains = (attn_in_gain, attn_out_gain, ffn_in_gain, ffn_out_gain, query_gain, key_gain)
    gain_sizes = [v.shape[0] for v in gains]
    gain_ends = [sum(gain_sizes[: i + 1]) for i in range(6)]
    gain_row = sum(jnp.pad(v, (e - n, 2 * HD - e)) for v, e, n in zip(gains, gain_ends, gain_sizes))
    gain_row = jnp.pad(gain_row[None, :], ((0, -(own_feats + 1) % 16), (0, 0)))
    kv_block = jnp.concatenate([jnp.concatenate([k_weight, v_weight], axis=1), gain_row], axis=0)
    some = jnp.concatenate([q_weight, out_weight], axis=1)
    some = jnp.concatenate([kv_block, jnp.pad(some, ((0, kv_block.shape[0] - own_feats), (0, 0)))], axis=1)
    moving = some
    some = put(jnp.zeros((seqs,) + some.shape, BF16), some, 0, spots[0])
    x = to_rows(tokens)
    for step in range(1, seqs):
        if step == 3:
            moving = together([moving], x)[0]
        moving = hop(moving)
        some = put(some, moving, 0, spots[step])
    early = moving
    if cores == 2:
        other = shift(some, "core", 1)
        some = jnp.where(c_index == 0, jnp.stack([some, other], axis=1), jnp.stack([other, some], axis=1))
    else:
        some = lax.all_gather(some, "core", axis=1)
    some = some.reshape((seqs * cores,) + some.shape[2:])
    gain_all = some[:, own_feats].astype(F32).reshape(seqs, cores, -1)
    first = 2 * HD + (c_index * HD if split_heads else 0)

    def columns(start, many):
        return lax.dynamic_slice(
            some, (0, 0, start), (seqs * cores, own_feats, many), allow_negative_indices=False
        ).reshape(width, many)

    q_full = columns(first, HD)
    out_full = columns(first + q_weight.shape[1], HD)
    qkv_full = jnp.concatenate([q_full, columns(0, 2 * HD)], axis=1)
    g_in, g_ao, g_fi, g_fo, g_q, g_k = (
        gain_all[:, :, end - size : end].reshape(1, -1) for end, size in zip(gain_ends, gain_sizes)
    )

    size = seqs * span
    group = cores * tensors
    rows = size * group

    owner_tensor = ((t_index - jnp.arange(tensors, dtype=jnp.int32)) % tensors)[:, None, None, None]
    owner_core = ((c_index - jnp.arange(cores, dtype=jnp.int32)) % cores)[None, :, None, None]
    block_index = jnp.arange(seqs, dtype=jnp.int32)[None, None, :, None]
    inner = jnp.arange(span, dtype=jnp.int32)[None, None, None, :]
    places = (((block_index * cores + owner_core) * tensors + owner_tensor) * span + inner).reshape(-1)
    docs, within, pics = layout(
        *(pick(v.reshape(seqs, -1), s_index, 0) for v in (doc_lengths, picture_starts)), places
    )
    frequency = ROPE_BASE ** (-2.0 * jnp.arange(HD // 2, dtype=F32) / HD)
    angles = within.astype(F32)[:, None] * frequency[None, :]
    cosine = jnp.cos(angles)
    sine = jnp.sin(angles)
    meta = [docs, places, pics] + [jnp.zeros_like(docs)] * 5
    meta_q = jnp.stack(meta, axis=1)
    meta_k = jnp.stack(meta, axis=0)
    q_blocks = list(range(group)) if split_heads else [k * cores for k in range(tensors)]
    q_count = len(q_blocks)
    block = struct((size, width), BF16)
    vector = struct((1, width), F32)

    def flat(lists):
        return [p for line in lists for p in line]

    def by_tensor(pieces):
        return [pieces[k * cores : (k + 1) * cores] for k in range(tensors)]

    (a_own,) = small_call(start_kernel, [block], (x, g_in))
    a_all = flat(gather_rows(a_own))
    low_rows = struct((rows, HD), BF16)
    o, prob, raw, query, key, value, *r_parts = small_call(
        functools.partial(attend_kernel, group, q_blocks),
        [struct((q_count * size, HD), BF16), struct((q_count * size, rows), BF16), struct((rows, 2 * HD), BF16)]
        + [low_rows] * 3
        + [block] * q_count,
        (*a_all, qkv_full, out_full, cosine, sine, g_q, g_k, meta_q, meta_k),
        flops=2 * rows * width * 3 * HD + 2 * q_count * size * HD * (2 * rows + width),
    )
    if q_count != group:
        spread = [jnp.zeros((size, width), BF16)] * group
        for i, part in zip(q_blocks, r_parts):
            spread[i] = part
        r_parts = spread
    shares, _ = scatter_rows(by_tensor(r_parts))

    branch, middle, f_own = small_call(
        functools.partial(middle_kernel, len(shares)),
        [struct((size, width), F32)] * 2 + [block],
        (*shares, x, g_ao, g_fi),
    )
    f_all = gather_rows(f_own)

    blocks = to_columns([gate_weight, up_weight, down_weight], hidden)
    moving = together(blocks, early)
    fulls = [put(jnp.zeros((seqs, feats, hidden), BF16), v, 0, spots[0]) for v in moving]
    ahead = {2: a_own, 4: o, 6: f_own}
    for step in range(1, seqs):
        if step in ahead:
            moving = together(moving, ahead[step])
        moving = [hop(v) for v in moving]
        fulls = [put(full, v, 0, spots[step]) for full, v in zip(fulls, moving)]
    gate_full, up_full, down_full = fulls
    gate_full, up_full, down_full = (w.reshape(width, hidden) for w in (gate_full, up_full, down_full))
    gates, ups, hids = zip(*(hidden_forward(line, gate_full, up_full) for line in f_all))
    cotangent = to_rows(together([out_grad], *moving)[0])
    e_parts = [None] * tensors
    for k in list(range(1, tensors)) + [0]:
        e_parts[k] = down_forward(hids[k] if k else together([hids[k]], cotangent)[0], down_full, cores)
    shares, _ = scatter_rows(e_parts)
    output, de_own, gain_fo = small_call(
        functools.partial(close_kernel, len(shares)),
        [block, block, vector],
        (*shares, middle, cotangent, g_fo),
    )

    de_all = gather_rows(de_own)
    downs = RingSum(outer([(flat(de_all), hids)], spot_line))
    dgates, dups, df_parts = [None] * tensors, [None] * tensors, [None] * tensors
    for k in list(range(1, tensors)) + [0]:
        dgates[k], dups[k], *df_parts[k] = hidden_backward(
            together(de_all[k], downs.sum), gates[k], ups[k], gate_full, up_full, down_full
        )
        downs.step()
        downs.wait(dgates[k])
    output = from_rows(together([output], downs.sum)[0])
    shares, _ = scatter_rows(df_parts)
    pieces = flat(f_all)
    bigs = RingSum(outer([(pieces, together(dgates, downs.sum)), (pieces, dups)], spot_line))
    downs.step()
    rings = [bigs, downs]
    meet(rings)

    def stage():
        for ring in rings:
            if ring.left():
                ring.step()

    stage()
    dmid, dr_own, gain_fi, gain_ao = small_call(
        functools.partial(turn_kernel, len(shares)),
        [struct((size, width), F32), block, vector, vector],
        (*together(shares, bigs.blocks[0]), middle, cotangent, branch, g_fi, g_ao),
    )
    meet(rings, dr_own, output)

    dr_all = flat(gather_rows(dr_own))
    dr_used = [dr_all[i] for i in q_blocks]
    stage()
    grads, gain_q, gain_k, *da_parts = small_call(
        functools.partial(attend_back_kernel, q_count, q_blocks, group),
        [struct((rows, 3 * HD), BF16), struct((1, HD), F32), struct((1, HD), F32)] + [block] * group,
        (
            *dr_used,
            *(prob, raw, query, key, value, qkv_full, out_full, cosine, sine, g_q, g_k),
        ),
        scratch=[pltpu.VMEM((rows, HD), F32)] * 2,
    )
    meet(rings, grads)
    shares, sent = scatter_rows(by_tensor(da_parts))
    stage()
    smalls = RingSum(outer([(a_all, [grads]), (dr_used, [o])], spot_line))
    rings.append(smalls)
    meet(rings, *sent)
    stage()
    input_grad, gain_in = small_call(
        functools.partial(last_kernel, len(shares)),
        [block, vector],
        (*shares, x, dmid, g_in),
    )
    gain_grads = (gain_in, gain_ao, gain_fi, gain_fo, gain_q, gain_k)
    packed = jnp.concatenate([g.reshape(seqs * cores, -1) for g in gain_grads], axis=1)
    meet(rings, input_grad, packed)
    input_grad = from_rows(input_grad)
    near = [e for e in exchanges() if e[0] != "seq"]
    far = [e for e in exchanges() if e[0] == "seq"]
    for way in near:
        packed = exchange(packed, *way)
    stage()
    meet(rings, packed)
    while bigs.left():
        stage()
        meet(rings, input_grad)
    (packed,) = together([packed], bigs.sum)
    while smalls.left() or far:
        if smalls.left():
            smalls.step()
        if far:
            packed = exchange(packed, *far.pop(0))
            smalls.wait(packed)
            (packed,) = together([packed], smalls.sum)
    down_sum, small_sum = downs.sum, smalls.sum
    gate_sum, up_sum = bigs.sum[:, :hidden], bigs.sum[:, hidden:]

    def to_owner(values):
        values = values.astype(F32)
        if cores != 2:
            return lax.all_to_all(values, "core", split_axis=0, concat_axis=1, tiled=True)
        halves = values.reshape(cores, own_feats, -1)
        mine = pick(halves, c_index, 0)
        other = shift(pick(halves, 1 - c_index, 0), "core", 1)
        return jnp.where(
            c_index == 0, jnp.concatenate([mine, other], axis=1), jnp.concatenate([other, mine], axis=1)
        )

    def sum_core(values):
        values = values.astype(F32)
        if cores != 2:
            return lax.psum_scatter(values, "core", scatter_dimension=0, tiled=True)
        halves = values.reshape(cores, own_feats, -1)
        return pick(halves, c_index, 0) + shift(pick(halves, 1 - c_index, 0), "core", 1)

    kv_sum = sum_tensor(sum_core(small_sum[:, HD : 3 * HD]))
    own_columns = to_owner if split_heads else sum_core
    q_grad, out_grad_w = own_columns(small_sum[:, :HD]), own_columns(small_sum[:, 3 * HD :])
    mine = pick(packed, s_index * cores + c_index, 0)
    gain_out = tuple(mine[end - n : end] for end, n in zip(gain_ends, gain_sizes))
    return (
        output,
        input_grad,
        q_grad,
        kv_sum[:, :HD],
        kv_sum[:, HD:],
        out_grad_w,
        to_owner(gate_sum[:, :hidden_here]),
        to_owner(up_sum[:, :hidden_here]),
        to_owner(down_sum[:, :hidden_here]),
    ) + gain_out


def solution(mesh):
    def run(tokens, *rest):
        seqs = tokens.shape[0] * tokens.shape[1]
        wide, tensor = mesh.shape["wide"], mesh.shape["tensor"]
        fine = Mesh(mesh.devices.reshape(seqs, wide // seqs, tensor), ("seq", "core", "tensor"))
        acts = P(None, None, ("seq", "core", "tensor"), None)
        both = P(("seq", "core"), "tensor")
        rows = P(("seq", "core"), None)
        vector = P(("seq", "core"))
        weights = (both, rows, rows, both, both, both, both) + (vector,) * 6
        return jax.shard_map(
            body,
            mesh=fine,
            in_specs=(acts, acts, P(), P()) + weights,
            out_specs=(acts, acts) + weights,
            check_vma=False,
        )(tokens, *rest)

    return run
```

time: 744 us -> 575 us (0.77)
  matrix products: 138 us -> 0 us
  Pallas kernels: 0 us -> 82.7 us
  between operations: 69.9 us -> 2.47 us
  blocking collectives: 43 us -> 0 us
  starting transfers between devices: 138 us -> 100 us
  waiting for transfers between devices: 192 us -> 215 us
  local copies, waits for them, and re-layouts: 104 us -> 120 us
    dot_general x66 -> x0, matrix products: 138 us -> none  [dot(): lax.dot_general(left, right, ((dims[0], dims[1]), ((), ())), preferred_el...]
    pallas_call x0 -> x16, Pallas kernels: none -> 82.7 us  [call(): pl.pallas_call(kernel, out_shape=outs, scratch_shapes=list(scratch), comp...]
    all_to_all x9 -> x0, blocking collectives: 43 us -> none  [the longest x5 25.1 us: to_owner(): lax.all_to_all(values, 'core', split_axis=0, concat_axis=1, tiled=True)]
    ppermute x96 -> x54, starting transfers between devices: 110 us -> 67.7 us  [the longest x49 62.8 us: hop(): return lax.ppermute(values, ('seq', 'core'), pairs)]
    unnamed x222 -> x259, local copies, waits for them, and re-layouts: 18.8 us -> 52.9 us
    all_to_all x16 -> x0, local copies, waits for them, and re-layouts: 13 us -> none  [the longest x8 9.49 us: to_owner(): lax.all_to_all(values, 'core', split_axis=0, concat_axis=1, tiled=True)]
    reduce_sum x11 -> x1, other arithmetic: 12 us -> 0.1 us  [layout(): doc_ids = jnp.sum(before.astype(jnp.int32), axis=1)]
    ppermute x18 -> x32, waiting for transfers between devices: 31 us -> 42.6 us  [shift(): lax.ppermute(values, axis, [(i, (i + step) % size) for i in range(size)])]
  transfers between devices with their start and end apart: 120 -> 91, of which waited for: 51 -> 45; matrix products, arithmetic and copies ran while one was open for 30% -> 18% of each run, Pallas kernels for 0% -> 13%
where the time goes in v2:
time: 575 us; the launch traced here: 564 us
  waiting for transfers between devices  215 us (37%)
  local copies, waits for them, and re-layouts  120 us (21%)
  starting transfers between devices  100 us (17%)
  Pallas kernels  82.7 us (14%)
  other arithmetic  43.5 us (8%)
    ppermute x49, waiting for transfers between devices, hop(): return lax.ppermute(values, ('seq', 'core'), pairs)  149 us
    pallas_call x16, Pallas kernels, call(): pl.pallas_call(kernel, out_shape=outs, scratch_shapes=list(scratch), comp...  82.7 us
    ppermute x49, starting transfers between devices, hop(): return lax.ppermute(values, ('seq', 'core'), pairs)  62.8 us
    unnamed x259, local copies, waits for them, and re-layouts  52.9 us
    dynamic_update_slice x31, local copies, waits for them, and re-layouts, put(): lax.dynamic_update_slice(full, block[None], (spot, row, 0), allow_negativ...  44.3 us
    ppermute x32, waiting for transfers between devices, shift(): lax.ppermute(values, axis, [(i, (i + step) % size) for i in range(size)])  42.6 us
    convert_element_type x18, other arithmetic, step(): self.sum = total if self.left() == 0 else total.astype(BF16)  15.7 us
    ppermute x32, starting transfers between devices, shift(): lax.ppermute(values, axis, [(i, (i + step) % size) for i in range(size)])  11.7 us
  transfers between devices with their start and end apart: 91, of which 45 were waited for; matrix products, arithmetic and copies ran while one was open for 18% of the time, Pallas kernels for 13%

profile of v2, /device:TPU:0, one launch (start us, length us, event | category | flops | bytes accessed | tf_op | source)
XLA Modules:
  0.0 564.2 jit_solution(15748142084071779981)
XLA Ops:
  4.0 3.0 collective-permute-start
  12.5 3.8 all-to-all-start.1
  20.9 4.8 all-to-all-start
  34.4 4.6 collective-permute-done.1
  39.0 4.0 all-to-all-done
  44.9 4.3 collective-permute-done.2
  51.0 4.3 collective-permute-done.3
  57.3 4.3 collective-permute-done.4
  63.5 4.3 collective-permute-done.5
  69.6 4.3 collective-permute-done.6
  82.1 2.5 collective-permute-done.16
  85.3 4.8 collective-permute-done.17
  90.9 4.8 collective-permute-done.18
  114.7 2.5 bitcast_dynamic-update-slice_fusion.21
  117.2 2.4 collective-permute-done.21
  120.2 5.0 collective-permute-done.23
  126.0 2.5 bitcast_dynamic-update-slice_fusion.13
  128.9 2.5 bitcast_dynamic-update-slice_fusion.5
  131.4 2.8 bitcast_dynamic-update-slice_fusion.20
  135.3 10.8 %shard_map.290 = (bf16[1024,256]{1,0:T(8,128)(2,1)S(1)}, bf16[1024,1024]{1,0:T(8,128)(2,1)}, bf16[1024,512]{1,0:T(8,128)(2,1)}, bf16[1024,256]{1,0:T(8,128)(2,1)...) custom-call(bf16[256,1152]{1,0:T(8,128)(2,1)} %copy-done.19, ...), custom_call_target="tpu_custom_call" | custom-call | bytes 1 | tf_op jit(solution)/shard_map/pallas_call | solution.py:66
  151.0 2.5 bitcast_dynamic-update-slice_fusion.4
  158.1 3.0 collective-permute-done.27
  163.1 3.6 collective-permute-done.29
  171.1 2.5 bitcast_dynamic-update-slice_fusion.3
  174.3 10.4 %collective-permute-done.12.refs_0_ = bf16[256,1152]{1,0:T(8,128)(2,1)S(1)} collective-permute-done((bf16[256,1152]{1,0:T(8,128)(2,1)S(1)}, bf16[256,1152]{1,0:T(8,128)(2,1)S(1)}, u32[]{:S(2)}, u32[]{:S(2)}) %collective-permute-start.12) | collective-permute-done | bytes 589856 | tf_op jit(solution)/shard_map/ppermute | solution.py:319
  190.0 2.5 bitcast_dynamic-update-slice_fusion.2
  196.3 4.1 collective-permute-done.33
  201.9 4.1 collective-permute-done.35
  208.7 2.8 collective-permute-done.32
  212.2 4.8 collective-permute-done.34
  217.7 4.8 collective-permute-done.36
  224.1 5.1 shard_map.292
  229.2 3.4 shard_map.293
  232.7 4.4 all-to-all-start.2
  241.5 5.1 shard_map.294
  257.6 3.4 shard_map.295
  263.2 5.1 collective-permute-done.38.refs_0_
  271.3 2.9 shard_map.296
  274.7 14.4 %collective-permute-done.42.refs_2_.refs_0_ = bf16[256,1152]{1,0:T(8,128)(2,1)S(1)} collective-permute-done((bf16[256,1152]{1,0:T(8,128)(2,1)S(1)}, bf16[256,1152]{1,0:T(8,128)(2,1)S(1)}, u32[]{:S(2)}, u32[]{:S(2)}) %collective-permute-start.42) | collective-permute-done | bytes 589856 | tf_op jit(solution)/shard_map/ppermute | solution.py:319
  294.8 5.3 shard_map.297
  310.8 7.7 %shard_map.298 = (bf16[512,1792]{1,0:T(8,128)(2,1)S(1)}, bf16[512,1792]{1,0:T(8,128)(2,1)S(1)}, bf16[256,1152]{1,0:T(8,128)(2,1)S(1)}, bf16[256,1152]{1,0:T(8,128)(2,1)S(1)}) custom-call(bf16[256,1152]{1,0:T(8,128)(2,1)S(1)} %collective-permute-done.42.refs_2_.refs_0_, bf16[256,1152]{1,0:T(8,128)(2,1)S(1)} %collective-permute-done.43.refs_3_.refs_1_, ...), custom_call_target="tpu_custom_call" | custom-call | bytes 1 | tf_op jit(solution)/shard_map/pallas_call | solution.py:66
  320.3 7.7 %shard_map.299 = (bf16[512,1792]{1,0:T(8,128)(2,1)S(1)}, bf16[512,1792]{1,0:T(8,128)(2,1)S(1)}, bf16[256,1152]{1,0:T(8,128)(2,1)S(1)}, bf16[256,1152]{1,0:T(8,128)(2,1)S(1)}) custom-call(bf16[256,1152]{1,0:T(8,128)(2,1)S(1)} %get-tuple-element.180.refs_0_, bf16[256,1152]{1,0:T(8,128)(2,1)S(1)} %collective-permute-done.41.refs_1_, ...), custom_call_target="tpu_custom_call" | custom-call | bytes 1 | tf_op jit(solution)/shard_map/pallas_call | solution.py:66
  333.7 10.8 %shard_map.300 = (bf16[144,3584]{1,0:T(8,128)(2,1)}, bf16[144,3584]{1,0:T(8,128)(2,1)S(1)}, bf16[144,3584]{1,0:T(8,128)(2,1)S(1)}, bf16[144,3584]{1,0:T(8,128)(2...) custom-call(s32[8]{0:T(128)S(1)} %copy-done.102, ...), custom_call_target="tpu_custom_call" | custom-call | bytes 1 | tf_op jit(solution)/shard_map/pallas_call | solution.py:66
  351.4 2.8 shard_map.301
  359.1 4.2 all-to-all-start.3
  363.4 6.4 %collective-permute-done.50.refs_2_.refs_7_ = bf16[256,1152]{1,0:T(8,128)(2,1)S(1)} collective-permute-done((bf16[256,1152]{1,0:T(8,128)(2,1)S(1)}, bf16[256,1152]{1,0:T(8,128)(2,1)S(1)}, u32[]{:S(2)}, u32[]{:S(2)}) %collective-permute-start.50) | collective-permute-done | bytes 589856 | tf_op jit(solution)/shard_map/ppermute | solution.py:319
  369.8 11.2 %collective-permute-done.57 = bf16[144,1792]{1,0:T(8,128)(2,1)S(1)} collective-permute-done((bf16[144,1792]{1,0:T(8,128)(2,1)S(1)}, bf16[144,1792]{1,0:T(8,128)(2,1)S(1)}, u32[]{:S(2)}, u32[]{:S(2)}) %collective-permute-start.57) | collective-permute-done | bytes 516128 | tf_op jit(solution)/shard_map/ppermute | solution.py:370
  384.0 2.7 add_convert_fusion.5
  387.7 2.5 collective-permute-start.58
  395.6 10.5 %shard_map.302 = (bf16[1024,768]{1,0:T(8,128)(2,1)}, f32[1,256]{1,0:T(1,128)S(1)}, f32[1,256]{1,0:T(1,128)S(1)}, bf16[256,1152]{1,0:T(8,128)(2,1)S(1)}, bf16[256...) custom-call(bf16[256,1152]{1,0:T(8,128)(2,1)S(1)} %get-tuple-element.200.refs_0_.refs_5_, ...), custom_call_target="tpu_custom_call" | custom-call | bytes 1 | tf_op jit(solution)/shard_map/pallas_call | solution.py:66
  406.2 3.1 collective-permute-done.59
  411.6 4.8 shard_map.304
  420.5 9.6 %collective-permute-done.61 = bf16[144,1792]{1,0:T(8,128)(2,1)S(1)} collective-permute-done((bf16[144,1792]{1,0:T(8,128)(2,1)S(1)}, bf16[144,1792]{1,0:T(8,128)(2,1)S(1)}, u32[]{:S(2)}, u32[]{:S(2)}) %collective-permute-start.61) | collective-permute-done | bytes 516128 | tf_op jit(solution)/shard_map/ppermute | solution.py:370
  450.4 5.7 %collective-permute-done.64 = bf16[144,1792]{1,0:T(8,128)(2,1)} collective-permute-done((bf16[144,1792]{1,0:T(8,128)(2,1)}, bf16[144,1792]{1,0:T(8,128)(2,1)}, u32[]{:S(2)}, u32[]{:S(2)}) %collective-permute-start.64) | collective-permute-done | bytes 516128 | tf_op jit(solution)/shard_map/ppermute | solution.py:370
  465.8 2.5 collective-permute-done.68
  468.9 8.8 %collective-permute-done.65 = bf16[144,1024]{1,0:T(8,128)(2,1)S(1)} collective-permute-done((bf16[144,1024]{1,0:T(8,128)(2,1)S(1)}, bf16[144,1024]{1,0:T(8,128)(2,1)S(1)}, u32[]{:S(2)}, u32[]{:S(2)}) %collective-permute-start.65) | collective-permute-done | bytes 294944 | tf_op jit(solution)/shard_map/ppermute | solution.py:370
  482.4 3.5 all-to-all-start.4
  486.0 14.5 %collective-permute-done.69 = bf16[144,1024]{1,0:T(8,128)(2,1)S(1)} collective-permute-done((bf16[144,1024]{1,0:T(8,128)(2,1)S(1)}, bf16[144,1024]{1,0:T(8,128)(2,1)S(1)}, u32[]{:S(2)}, u32[]{:S(2)}) %collective-permute-start.69) | collective-permute-done | bytes 294944 | tf_op jit(solution)/shard_map/ppermute | solution.py:370
  500.6 2.5 add_convert_fusion
  503.1 5.8 %all-to-all-done.4 = bf16[8,32,1152]{2,1,0:T(8,128)(2,1)S(1)} async-done(((bf16[8,32,1152]{2,1,0:T(8,128)(2,1)}), bf16[8,32,1152]{2,1,0:T(8,128)(2,1)S(1)}, u32[]{:S(2)}, u32[]{:S(2)}) %all-to-all-start.4) | async-done | bytes 589856 | tf_op jit(solution)/shard_map/all_to_all | solution.py:469
  511.1 17.0 %collective-permute-done.71 = bf16[144,1024]{1,0:T(8,128)(2,1)S(1)} collective-permute-done((bf16[144,1024]{1,0:T(8,128)(2,1)S(1)}, bf16[144,1024]{1,0:T(8,128)(2,1)S(1)}, u32[]{:S(2)}, u32[]{:S(2)}) %collective-permute-start.71) | collective-permute-done | bytes 294944 | tf_op jit(solution)/shard_map/ppermute | solution.py:370
  533.5 3.8 collective-permute-done.74
  549.2 2.5 collective-permute-done.78
  556.3 4.3 collective-permute-done.81
  (543 shorter events, 230.1 us)
Async XLA Ops:
  4.0 25.4 %collective-permute-start = (bf16[80,1536]{1,0:T(8,128)(2,1)}, bf16[80,1536]{1,0:T(8,128)(2,1)}, u32[]{:S(2)}, u32[]{:S(2)}) collective-permute-start(bf16[80,1536]{1,0:T(8,128)(2,1)} %fusion.8), channel_id=1, source_target_pairs={{0,8},{2,6},{8,16},{10,2},{16,24},{18,10},{24,28},{26,18},{28,20},... | collective-permute-start | bytes 737288 | tf_op jit(solution)/shard_map/ppermute | solution.py:370
  20.9 22.1 %all-to-all-start = ((bf16[8,32,1152]{2,1,0:T(8,128)(2,1)}), bf16[8,32,1152]{2,1,0:T(8,128)(2,1)S(1)}, u32[]{:S(2)}, u32[]{:S(2)}) async-start(bf16[8,32,1152]{2,1,0:T(8,128)(2,1)} %bitcast), calls=%async_computation | async-start | bytes 1179648 | tf_op jit(solution)/shard_map/all_to_all | solution.py:465
  29.4 9.5 %collective-permute-start.1 = (bf16[80,1536]{1,0:T(8,128)(2,1)}, bf16[80,1536]{1,0:T(8,128)(2,1)S(1)}, u32[]{:S(2)}, u32[]{:S(2)}) collective-permute-start(bf16[80,1536]{1,0:T(8,128)(2,1)} %collective-permute-done), channel_id=1, source_target_pairs={{0,8},{2,6},{8,16},{10,2},{16,24},{18,10},{24,28},{26,18},{28,20},... | collective-permute-start | bytes 737288 | tf_op jit(solution)/shard_map/ppermute | solution.py:370
  75.3 21.1 %collective-permute-start.7 = (bf16[8,80,1536]{2,1,0:T(8,128)(2,1)}, bf16[8,80,1536]{2,1,0:T(8,128)(2,1)S(1)}, u32[]{:S(2)}, u32[]{:S(2)}) collective-permute-start(bf16[8,80,1536]{2,1,0:T(8,128)(2,1)} %bitcast_dynamic-update-slice_fusion.24), channel_id=1, source_target_pairs={{0,2},{2,0},{1,3},{3,1},{4,6},{6,4},{5,7},{7,5},{8,10},{10,8},{9,1... | collective-permute-start | bytes 5898248 | tf_op jit(solution)/shard_map/ppermute | solution.py:319
  77.1 13.1 %collective-permute-start.17 = (bf16[144,1792]{1,0:T(8,128)(2,1)S(1)}, bf16[144,1792]{1,0:T(8,128)(2,1)S(1)}, u32[]{:S(2)}, u32[]{:S(2)}) collective-permute-start(bf16[144,1792]{1,0:T(8,128)(2,1)S(1)} %get-tuple-element.148), channel_id=1, source_target_pairs={{0,8},{2,6},{8,16},{10,2},{16,24},{18,10},{24,28},{26,18},{28,20},... | collective-permute-start | bytes 1548296 | tf_op jit(solution)/shard_map/ppermute | solution.py:370
  79.3 16.4 %collective-permute-start.18 = (bf16[144,1792]{1,0:T(8,128)(2,1)S(1)}, bf16[144,1792]{1,0:T(8,128)(2,1)S(1)}, u32[]{:S(2)}, u32[]{:S(2)}) collective-permute-start(bf16[144,1792]{1,0:T(8,128)(2,1)S(1)} %get-tuple-element.149), channel_id=1, source_target_pairs={{0,8},{2,6},{8,16},{10,2},{16,24},{18,10},{24,28},{26,18},{28,20},... | collective-permute-start | bytes 1548296 | tf_op jit(solution)/shard_map/ppermute | solution.py:370
  101.6 32.7 %collective-permute-start.8 = (bf16[256,1152]{1,0:T(8,128)(2,1)S(1)}, bf16[256,1152]{1,0:T(8,128)(2,1)S(1)}, u32[]{:S(2)}, u32[]{:S(2)}) collective-permute-start(bf16[256,1152]{1,0:T(8,128)(2,1)S(1)} %shard_map.289.refs_0_), channel_id=1, source_target_pairs={{0,2},{2,0},{1,3},{3,1},{4,6},{6,4},{5,7},{7,5},{8,10},{10,8},{9,1... | collective-permute-start | bytes 1769480 | tf_op jit(solution)/shard_map/ppermute | solution.py:319
  101.7 26.8 %collective-permute-start.9 = (bf16[256,1152]{1,0:T(8,128)(2,1)S(1)}, bf16[256,1152]{1,0:T(8,128)(2,1)}, u32[]{:S(2)}, u32[]{:S(2)}) collective-permute-start(bf16[256,1152]{1,0:T(8,128)(2,1)S(1)} %shard_map.289.refs_0_), channel_id=1, source_target_pairs={{0,1},{1,0},{2,3},{3,2},{4,5},{5,4},{6,7},{7,6},{8,9},{9,8},{10,11... | collective-permute-start | bytes 1769480 | tf_op jit(solution)/shard_map/ppermute | solution.py:319
  105.3 14.4 %collective-permute-start.21 = (bf16[144,1792]{1,0:T(8,128)(2,1)}, bf16[144,1792]{1,0:T(8,128)(2,1)}, u32[]{:S(2)}, u32[]{:S(2)}) collective-permute-start(bf16[144,1792]{1,0:T(8,128)(2,1)} %copy-done.116), channel_id=1, source_target_pairs={{0,8},{2,6},{8,16},{10,2},{16,24},{18,10},{24,28},{26,18},{28,20},... | collective-permute-start | bytes 1548296 | tf_op jit(solution)/shard_map/ppermute | solution.py:370
  107.6 17.6 %collective-permute-start.23 = (bf16[144,1792]{1,0:T(8,128)(2,1)}, bf16[144,1792]{1,0:T(8,128)(2,1)}, u32[]{:S(2)}, u32[]{:S(2)}) collective-permute-start(bf16[144,1792]{1,0:T(8,128)(2,1)} %copy-done.115), channel_id=1, source_target_pairs={{0,8},{2,6},{8,16},{10,2},{16,24},{18,10},{24,28},{26,18},{28,20},... | collective-permute-start | bytes 1548296 | tf_op jit(solution)/shard_map/ppermute | solution.py:370
  114.1 17.3 %collective-permute-start.20 = (bf16[144,1792]{1,0:T(8,128)(2,1)}, bf16[144,1792]{1,0:T(8,128)(2,1)}, u32[]{:S(2)}, u32[]{:S(2)}) collective-permute-start(bf16[144,1792]{1,0:T(8,128)(2,1)} %collective-permute-done.19), channel_id=1, source_target_pairs={{0,8},{2,6},{8,16},{10,2},{16,24},{18,10},{24,28},{26,18},{28,20},... | collective-permute-start | bytes 1548296 | tf_op jit(solution)/shard_map/ppermute | solution.py:370
  119.6 26.5 %collective-permute-start.22 = (bf16[144,1792]{1,0:T(8,128)(2,1)}, bf16[144,1792]{1,0:T(8,128)(2,1)}, u32[]{:S(2)}, u32[]{:S(2)}) collective-permute-start(bf16[144,1792]{1,0:T(8,128)(2,1)} %collective-permute-done.21), channel_id=1, source_target_pairs={{0,8},{2,6},{8,16},{10,2},{16,24},{18,10},{24,28},{26,18},{28,20},... | collective-permute-start | bytes 1548296 | tf_op jit(solution)/shard_map/ppermute | solution.py:370
  125.1 21.0 %collective-permute-start.24 = (bf16[144,1792]{1,0:T(8,128)(2,1)}, bf16[144,1792]{1,0:T(8,128)(2,1)}, u32[]{:S(2)}, u32[]{:S(2)}) collective-permute-start(bf16[144,1792]{1,0:T(8,128)(2,1)} %collective-permute-done.23), channel_id=1, source_target_pairs={{0,8},{2,6},{8,16},{10,2},{16,24},{18,10},{24,28},{26,18},{28,20},... | collective-permute-start | bytes 1548296 | tf_op jit(solution)/shard_map/ppermute | solution.py:370
  149.9 11.3 %collective-permute-start.27 = (bf16[144,1792]{1,0:T(8,128)(2,1)}, bf16[144,1792]{1,0:T(8,128)(2,1)}, u32[]{:S(2)}, u32[]{:S(2)}) collective-permute-start(bf16[144,1792]{1,0:T(8,128)(2,1)} %collective-permute-done.22), channel_id=1, source_target_pairs={{0,8},{2,6},{8,16},{10,2},{16,24},{18,10},{24,28},{26,18},{28,20},... | collective-permute-start | bytes 1548296 | tf_op jit(solution)/shard_map/ppermute | solution.py:370
  150.2 16.4 %collective-permute-start.29 = (bf16[144,1792]{1,0:T(8,128)(2,1)}, bf16[144,1792]{1,0:T(8,128)(2,1)}, u32[]{:S(2)}, u32[]{:S(2)}) collective-permute-start(bf16[144,1792]{1,0:T(8,128)(2,1)} %collective-permute-done.24), channel_id=1, source_target_pairs={{0,8},{2,6},{8,16},{10,2},{16,24},{18,10},{24,28},{26,18},{28,20},... | collective-permute-start | bytes 1548296 | tf_op jit(solution)/shard_map/ppermute | solution.py:370
  153.6 16.8 %collective-permute-start.11 = (bf16[256,1152]{1,0:T(8,128)(2,1)S(1)}, bf16[256,1152]{1,0:T(8,128)(2,1)S(1)}, u32[]{:S(2)}, u32[]{:S(2)}) collective-permute-start(bf16[256,1152]{1,0:T(8,128)(2,1)S(1)} %get-tuple-element.143), channel_id=1, source_target_pairs={{0,2},{2,0},{1,3},{3,1},{4,6},{6,4},{5,7},{7,5},{8,10},{10,8},{9,1... | collective-permute-start | bytes 1769480 | tf_op jit(solution)/shard_map/ppermute | solution.py:319
  155.2 19.2 %collective-permute-start.13 = (bf16[256,1152]{1,0:T(8,128)(2,1)S(1)}, bf16[256,1152]{1,0:T(8,128)(2,1)S(1)}, u32[]{:S(2)}, u32[]{:S(2)}) collective-permute-start(bf16[256,1152]{1,0:T(8,128)(2,1)S(1)} %get-tuple-element.145), channel_id=1, source_target_pairs={{0,2},{2,0},{1,3},{3,1},{4,6},{6,4},{5,7},{7,5},{8,10},{10,8},{9,1... | collective-permute-start | bytes 1769480 | tf_op jit(solution)/shard_map/ppermute | solution.py:319
  155.5 18.1 %collective-permute-start.26 = (bf16[144,1792]{1,0:T(8,128)(2,1)S(1)}, bf16[144,1792]{1,0:T(8,128)(2,1)S(1)}, u32[]{:S(2)}, u32[]{:S(2)}) collective-permute-start(bf16[144,1792]{1,0:T(8,128)(2,1)S(1)} %collective-permute-done.25), channel_id=1, source_target_pairs={{0,8},{2,6},{8,16},{10,2},{16,24},{18,10},{24,28},{26,18},{28,20},... | collective-permute-start | bytes 1548296 | tf_op jit(solution)/shard_map/ppermute | solution.py:370
  161.2 24.3 %collective-permute-start.28 = (bf16[144,1792]{1,0:T(8,128)(2,1)}, bf16[144,1792]{1,0:T(8,128)(2,1)}, u32[]{:S(2)}, u32[]{:S(2)}) collective-permute-start(bf16[144,1792]{1,0:T(8,128)(2,1)} %collective-permute-done.27), channel_id=1, source_target_pairs={{0,8},{2,6},{8,16},{10,2},{16,24},{18,10},{24,28},{26,18},{28,20},... | collective-permute-start | bytes 1548296 | tf_op jit(solution)/shard_map/ppermute | solution.py:370
  166.7 18.7 %collective-permute-start.30 = (bf16[144,1792]{1,0:T(8,128)(2,1)}, bf16[144,1792]{1,0:T(8,128)(2,1)}, u32[]{:S(2)}, u32[]{:S(2)}) collective-permute-start(bf16[144,1792]{1,0:T(8,128)(2,1)} %collective-permute-done.29), channel_id=1, source_target_pairs={{0,8},{2,6},{8,16},{10,2},{16,24},{18,10},{24,28},{26,18},{28,20},... | collective-permute-start | bytes 1548296 | tf_op jit(solution)/shard_map/ppermute | solution.py:370
  170.5 14.2 %collective-permute-start.12 = (bf16[256,1152]{1,0:T(8,128)(2,1)S(1)}, bf16[256,1152]{1,0:T(8,128)(2,1)S(1)}, u32[]{:S(2)}, u32[]{:S(2)}) collective-permute-start(bf16[256,1152]{1,0:T(8,128)(2,1)S(1)} %add_convert_fusion.9), channel_id=1, source_target_pairs={{0,1},{1,0},{2,3},{3,2},{4,5},{5,4},{6,7},{7,6},{8,9},{9,8},{10,11... | collective-permute-start | bytes 1769480 | tf_op jit(solution)/shard_map/ppermute | solution.py:319
  188.2 12.2 %collective-permute-start.33 = (bf16[144,1792]{1,0:T(8,128)(2,1)}, bf16[144,1792]{1,0:T(8,128)(2,1)S(1)}, u32[]{:S(2)}, u32[]{:S(2)}) collective-permute-start(bf16[144,1792]{1,0:T(8,128)(2,1)} %collective-permute-done.28), channel_id=1, source_target_pairs={{0,8},{2,6},{8,16},{10,2},{16,24},{18,10},{24,28},{26,18},{28,20},... | collective-permute-start | bytes 1548296 | tf_op jit(solution)/shard_map/ppermute | solution.py:370
  192.6 16.1 %collective-permute-start.14 = (bf16[256,1152]{1,0:T(8,128)(2,1)S(1)}, bf16[256,1152]{1,0:T(8,128)(2,1)S(1)}, u32[]{:S(2)}, u32[]{:S(2)}) collective-permute-start(bf16[256,1152]{1,0:T(8,128)(2,1)S(1)} %get-tuple-element.146.refs_0_.refs_6_), channel_id=1, source_target_pairs={{0,1},{1,0},{2,3},{3,2},{4,5},{5,4},{6,7},{7,6},{8,9},{9,8},{10,11... | collective-permute-start | bytes 1769480 | tf_op jit(solution)/shard_map/ppermute | solution.py:319
  193.1 44.1 %collective-permute-start.39 = (bf16[256,1152]{1,0:T(8,128)(2,1)S(1)}, bf16[256,1152]{1,0:T(8,128)(2,1)S(1)}, u32[]{:S(2)}, u32[]{:S(2)}) collective-permute-start(bf16[256,1152]{1,0:T(8,128)(2,1)S(1)} %get-tuple-element.146.refs_0_.refs_6_), channel_id=1, source_target_pairs={{0,2},{2,0},{1,3},{3,1},{4,6},{6,4},{5,7},{7,5},{8,10},{10,8},{9,1... | collective-permute-start | bytes 1769480 | tf_op jit(solution)/shard_map/ppermute | solution.py:319
  193.1 12.9 %collective-permute-start.35 = (bf16[144,1792]{1,0:T(8,128)(2,1)}, bf16[144,1792]{1,0:T(8,128)(2,1)S(1)}, u32[]{:S(2)}, u32[]{:S(2)}) collective-permute-start(bf16[144,1792]{1,0:T(8,128)(2,1)} %collective-permute-done.30), channel_id=1, source_target_pairs={{0,8},{2,6},{8,16},{10,2},{16,24},{18,10},{24,28},{26,18},{28,20},... | collective-permute-start | bytes 1548296 | tf_op jit(solution)/shard_map/ppermute | solution.py:370
  194.9 16.6 %collective-permute-start.32 = (bf16[144,1792]{1,0:T(8,128)(2,1)S(1)}, bf16[144,1792]{1,0:T(8,128)(2,1)S(1)}, u32[]{:S(2)}, u32[]{:S(2)}) collective-permute-start(bf16[144,1792]{1,0:T(8,128)(2,1)S(1)} %collective-permute-done.31), channel_id=1, source_target_pairs={{0,8},{2,6},{8,16},{10,2},{16,24},{18,10},{24,28},{26,18},{28,20},... | collective-permute-start | bytes 1548296 | tf_op jit(solution)/shard_map/ppermute | solution.py:370
  200.4 16.6 %collective-permute-start.34 = (bf16[144,1792]{1,0:T(8,128)(2,1)S(1)}, bf16[144,1792]{1,0:T(8,128)(2,1)S(1)}, u32[]{:S(2)}, u32[]{:S(2)}) collective-permute-start(bf16[144,1792]{1,0:T(8,128)(2,1)S(1)} %collective-permute-done.33), channel_id=1, source_target_pairs={{0,8},{2,6},{8,16},{10,2},{16,24},{18,10},{24,28},{26,18},{28,20},... | collective-permute-start | bytes 1548296 | tf_op jit(solution)/shard_map/ppermute | solution.py:370
  206.0 16.6 %collective-permute-start.36 = (bf16[144,1792]{1,0:T(8,128)(2,1)S(1)}, bf16[144,1792]{1,0:T(8,128)(2,1)S(1)}, u32[]{:S(2)}, u32[]{:S(2)}) collective-permute-start(bf16[144,1792]{1,0:T(8,128)(2,1)S(1)} %collective-permute-done.35), channel_id=1, source_target_pairs={{0,8},{2,6},{8,16},{10,2},{16,24},{18,10},{24,28},{26,18},{28,20},... | collective-permute-start | bytes 1548296 | tf_op jit(solution)/shard_map/ppermute | solution.py:370
  208.7 15.4 %collective-permute-start.15 = (bf16[256,1152]{1,0:T(8,128)(2,1)S(1)}, bf16[256,1152]{1,0:T(8,128)(2,1)S(1)}, u32[]{:S(2)}, u32[]{:S(2)}) collective-permute-start(bf16[256,1152]{1,0:T(8,128)(2,1)S(1)} %collective-permute-done.14.refs_0_.refs_2_.refs_8_), channel_id=1, source_target_pairs={{0,2},{2,0},{1,3},{3,1},{4,6},{6,4},{5,7},{7,5},{8,10},{10,8},{9,1... | collective-permute-start | bytes 1769480 | tf_op jit(solution)/shard_map/ppermute | solution.py:319
  232.6 17.8 %collective-permute-start.37 = (bf16[256,1152]{1,0:T(8,128)(2,1)}, bf16[256,1152]{1,0:T(8,128)(2,1)}, u32[]{:S(2)}, u32[]{:S(2)}) collective-permute-start(bf16[256,1152]{1,0:T(8,128)(2,1)} %get-tuple-element.162), channel_id=1, source_target_pairs={{0,2},{2,0},{1,3},{3,1},{4,6},{6,4},{5,7},{7,5},{8,10},{10,8},{9,1... | collective-permute-start | bytes 1769480 | tf_op jit(solution)/shard_map/ppermute | solution.py:319
  232.7 21.2 %all-to-all-start.2 = ((bf16[8,32,1152]{2,1,0:T(8,128)(2,1)}), bf16[8,32,1152]{2,1,0:T(8,128)(2,1)}, u32[]{:S(2)}, u32[]{:S(2)}) async-start(bf16[8,32,1152]{2,1,0:T(8,128)(2,1)} %bitcast.197), calls=%async_computation.2 | async-start | bytes 1179648 | tf_op jit(solution)/shard_map/all_to_all | solution.py:465
  252.4 15.9 %collective-permute-start.38 = (bf16[256,1152]{1,0:T(8,128)(2,1)}, bf16[256,1152]{1,0:T(8,128)(2,1)S(1)}, u32[]{:S(2)}, u32[]{:S(2)}) collective-permute-start(bf16[256,1152]{1,0:T(8,128)(2,1)} %add_convert_fusion.8), channel_id=1, source_target_pairs={{0,1},{1,0},{2,3},{3,2},{4,5},{5,4},{6,7},{7,6},{8,9},{9,8},{10,11... | collective-permute-start | bytes 1769480 | tf_op jit(solution)/shard_map/ppermute | solution.py:319
  274.2 14.9 %collective-permute-start.42 = (bf16[256,1152]{1,0:T(8,128)(2,1)S(1)}, bf16[256,1152]{1,0:T(8,128)(2,1)S(1)}, u32[]{:S(2)}, u32[]{:S(2)}) collective-permute-start(bf16[256,1152]{1,0:T(8,128)(2,1)S(1)} %get-tuple-element.180.refs_0_), channel_id=1, source_target_pairs={{0,1},{1,0},{2,3},{3,2},{4,5},{5,4},{6,7},{7,6},{8,9},{9,8},{10,11... | collective-permute-start | bytes 1769480 | tf_op jit(solution)/shard_map/ppermute | solution.py:319
  274.7 14.4 %collective-permute-start.41 = (bf16[256,1152]{1,0:T(8,128)(2,1)S(1)}, bf16[256,1152]{1,0:T(8,128)(2,1)S(1)}, u32[]{:S(2)}, u32[]{:S(2)}) collective-permute-start(bf16[256,1152]{1,0:T(8,128)(2,1)S(1)} %get-tuple-element.180.refs_0_), channel_id=1, source_target_pairs={{0,2},{2,0},{1,3},{3,1},{4,6},{6,4},{5,7},{7,5},{8,10},{10,8},{9,1... | collective-permute-start | bytes 1769480 | tf_op jit(solution)/shard_map/ppermute | solution.py:319
  304.1 14.5 %collective-permute-start.44 = (bf16[144,1792]{1,0:T(8,128)(2,1)S(1)}, bf16[144,1792]{1,0:T(8,128)(2,1)S(1)}, u32[]{:S(2)}, u32[]{:S(2)}) collective-permute-start(bf16[144,1792]{1,0:T(8,128)(2,1)S(1)} %get-tuple-element.171), channel_id=1, source_target_pairs={{0,8},{2,6},{8,16},{10,2},{16,24},{18,10},{24,28},{26,18},{28,20},... | collective-permute-start | bytes 1548296 | tf_op jit(solution)/shard_map/ppermute | solution.py:370
  318.5 10.9 %collective-permute-start.46 = (bf16[256,1152]{1,0:T(8,128)(2,1)S(1)}, bf16[256,1152]{1,0:T(8,128)(2,1)S(1)}, u32[]{:S(2)}, u32[]{:S(2)}) collective-permute-start(bf16[256,1152]{1,0:T(8,128)(2,1)S(1)} %get-tuple-element.188), channel_id=1, source_target_pairs={{0,2},{2,0},{1,3},{3,1},{4,6},{6,4},{5,7},{7,5},{8,10},{10,8},{9,1... | collective-permute-start | bytes 1769480 | tf_op jit(solution)/shard_map/ppermute | solution.py:319
  318.7 11.4 %collective-permute-start.45 = (bf16[144,1792]{1,0:T(8,128)(2,1)S(1)}, bf16[144,1792]{1,0:T(8,128)(2,1)S(1)}, u32[]{:S(2)}, u32[]{:S(2)}) collective-permute-start(bf16[144,1792]{1,0:T(8,128)(2,1)S(1)} %add_convert_fusion.15), channel_id=1, source_target_pairs={{0,8},{2,6},{8,16},{10,2},{16,24},{18,10},{24,28},{26,18},{28,20},... | collective-permute-start | bytes 1548296 | tf_op jit(solution)/shard_map/ppermute | solution.py:370
  329.3 22.1 %collective-permute-start.48 = (bf16[256,1152]{1,0:T(8,128)(2,1)S(1)}, bf16[256,1152]{1,0:T(8,128)(2,1)S(1)}, u32[]{:S(2)}, u32[]{:S(2)}) collective-permute-start(bf16[256,1152]{1,0:T(8,128)(2,1)S(1)} %get-tuple-element.190), channel_id=1, source_target_pairs={{0,2},{2,0},{1,3},{3,1},{4,6},{6,4},{5,7},{7,5},{8,10},{10,8},{9,1... | collective-permute-start | bytes 1769480 | tf_op jit(solution)/shard_map/ppermute | solution.py:319
  329.6 21.8 %collective-permute-start.47 = (bf16[256,1152]{1,0:T(8,128)(2,1)S(1)}, bf16[256,1152]{1,0:T(8,128)(2,1)S(1)}, u32[]{:S(2)}, u32[]{:S(2)}) collective-permute-start(bf16[256,1152]{1,0:T(8,128)(2,1)S(1)} %add_convert_fusion.7), channel_id=1, source_target_pairs={{0,1},{1,0},{2,3},{3,2},{4,5},{5,4},{6,7},{7,6},{8,9},{9,8},{10,11... | collective-permute-start | bytes 1769480 | tf_op jit(solution)/shard_map/ppermute | solution.py:319
  330.3 26.4 %collective-permute-start.55 = (bf16[144,1792]{1,0:T(8,128)(2,1)S(1)}, bf16[144,1792]{1,0:T(8,128)(2,1)S(1)}, u32[]{:S(2)}, u32[]{:S(2)}) collective-permute-start(bf16[144,1792]{1,0:T(8,128)(2,1)S(1)} %add_convert_fusion.14), channel_id=1, source_target_pairs={{0,8},{2,6},{8,16},{10,2},{16,24},{18,10},{24,28},{26,18},{28,20},... | collective-permute-start | bytes 1548296 | tf_op jit(solution)/shard_map/ppermute | solution.py:370
  355.2 14.6 %collective-permute-start.50 = (bf16[256,1152]{1,0:T(8,128)(2,1)S(1)}, bf16[256,1152]{1,0:T(8,128)(2,1)S(1)}, u32[]{:S(2)}, u32[]{:S(2)}) collective-permute-start(bf16[256,1152]{1,0:T(8,128)(2,1)S(1)} %get-tuple-element.200.refs_0_.refs_5_), channel_id=1, source_target_pairs={{0,1},{1,0},{2,3},{3,2},{4,5},{5,4},{6,7},{7,6},{8,9},{9,8},{10,11... | collective-permute-start | bytes 1769480 | tf_op jit(solution)/shard_map/ppermute | solution.py:319
  356.8 27.1 %collective-permute-start.56 = (bf16[144,3584]{1,0:T(8,128)(2,1)}, bf16[144,3584]{1,0:T(8,128)(2,1)}, u32[]{:S(2)}, u32[]{:S(2)}) collective-permute-start(bf16[144,3584]{1,0:T(8,128)(2,1)} %get-tuple-element.215), channel_id=1, source_target_pairs={{0,8},{2,6},{8,16},{10,2},{16,24},{18,10},{24,28},{26,18},{28,20},... | collective-permute-start | bytes 3096584 | tf_op jit(solution)/shard_map/ppermute | solution.py:370
  358.3 22.6 %collective-permute-start.57 = (bf16[144,1792]{1,0:T(8,128)(2,1)S(1)}, bf16[144,1792]{1,0:T(8,128)(2,1)S(1)}, u32[]{:S(2)}, u32[]{:S(2)}) collective-permute-start(bf16[144,1792]{1,0:T(8,128)(2,1)S(1)} %add_convert_fusion.13), channel_id=1, source_target_pairs={{0,8},{2,6},{8,16},{10,2},{16,24},{18,10},{24,28},{26,18},{28,20},... | collective-permute-start | bytes 1548296 | tf_op jit(solution)/shard_map/ppermute | solution.py:370
  359.1 28.6 %all-to-all-start.3 = ((bf16[8,32,1152]{2,1,0:T(8,128)(2,1)}), bf16[8,32,1152]{2,1,0:T(8,128)(2,1)}, u32[]{:S(2)}, u32[]{:S(2)}) async-start(bf16[8,32,1152]{2,1,0:T(8,128)(2,1)} %bitcast.70), calls=%async_computation.3 | async-start | bytes 1179648 | tf_op jit(solution)/shard_map/all_to_all | solution.py:469
  363.3 29.2 %collective-permute-start.49 = (bf16[256,1152]{1,0:T(8,128)(2,1)S(1)}, bf16[256,1152]{1,0:T(8,128)(2,1)S(1)}, u32[]{:S(2)}, u32[]{:S(2)}) collective-permute-start(bf16[256,1152]{1,0:T(8,128)(2,1)S(1)} %get-tuple-element.200.refs_0_.refs_5_), channel_id=1, source_target_pairs={{0,2},{2,0},{1,3},{3,1},{4,6},{6,4},{5,7},{7,5},{8,10},{10,8},{9,1... | collective-permute-start | bytes 1769480 | tf_op jit(solution)/shard_map/ppermute | solution.py:319
  369.8 22.7 %collective-permute-start.51 = (bf16[256,1152]{1,0:T(8,128)(2,1)S(1)}, bf16[256,1152]{1,0:T(8,128)(2,1)}, u32[]{:S(2)}, u32[]{:S(2)}) collective-permute-start(bf16[256,1152]{1,0:T(8,128)(2,1)S(1)} %collective-permute-done.50.refs_2_.refs_7_), channel_id=1, source_target_pairs={{0,2},{2,0},{1,3},{3,1},{4,6},{6,4},{5,7},{7,5},{8,10},{10,8},{9,1... | collective-permute-start | bytes 1769480 | tf_op jit(solution)/shard_map/ppermute | solution.py:319
  387.7 21.9 %collective-permute-start.58 = (bf16[144,3584]{1,0:T(8,128)(2,1)}, bf16[144,3584]{1,0:T(8,128)(2,1)S(1)}, u32[]{:S(2)}, u32[]{:S(2)}) collective-permute-start(bf16[144,3584]{1,0:T(8,128)(2,1)} %add_convert_fusion.5), channel_id=1, source_target_pairs={{0,8},{2,6},{8,16},{10,2},{16,24},{18,10},{24,28},{26,18},{28,20},... | collective-permute-start | bytes 3096584 | tf_op jit(solution)/shard_map/ppermute | solution.py:370
  390.2 19.1 %collective-permute-start.59 = (bf16[144,1792]{1,0:T(8,128)(2,1)}, bf16[144,1792]{1,0:T(8,128)(2,1)S(1)}, u32[]{:S(2)}, u32[]{:S(2)}) collective-permute-start(bf16[144,1792]{1,0:T(8,128)(2,1)} %add_convert_fusion.12), channel_id=1, source_target_pairs={{0,8},{2,6},{8,16},{10,2},{16,24},{18,10},{24,28},{26,18},{28,20},... | collective-permute-start | bytes 1548296 | tf_op jit(solution)/shard_map/ppermute | solution.py:370
  406.2 12.0 %collective-permute-start.52 = (bf16[256,1152]{1,0:T(8,128)(2,1)S(1)}, bf16[256,1152]{1,0:T(8,128)(2,1)S(1)}, u32[]{:S(2)}, u32[]{:S(2)}) collective-permute-start(bf16[256,1152]{1,0:T(8,128)(2,1)S(1)} %get-tuple-element.207), channel_id=1, source_target_pairs={{0,2},{2,0},{1,3},{3,1},{4,6},{6,4},{5,7},{7,5},{8,10},{10,8},{9,1... | collective-permute-start | bytes 1769480 | tf_op jit(solution)/shard_map/ppermute | solution.py:319
  409.9 21.1 %collective-permute-start.60 = (bf16[144,3584]{1,0:T(8,128)(2,1)S(1)}, bf16[144,3584]{1,0:T(8,128)(2,1)S(1)}, u32[]{:S(2)}, u32[]{:S(2)}) collective-permute-start(bf16[144,3584]{1,0:T(8,128)(2,1)S(1)} %add_convert_fusion.4), channel_id=1, source_target_pairs={{0,8},{2,6},{8,16},{10,2},{16,24},{18,10},{24,28},{26,18},{28,20},... | collective-permute-start | bytes 3096584 | tf_op jit(solution)/shard_map/ppermute | solution.py:370
  411.1 35.5 %collective-permute-start.54 = (bf16[256,1152]{1,0:T(8,128)(2,1)}, bf16[256,1152]{1,0:T(8,128)(2,1)S(1)}, u32[]{:S(2)}, u32[]{:S(2)}) collective-permute-start(bf16[256,1152]{1,0:T(8,128)(2,1)} %get-tuple-element.209), channel_id=1, source_target_pairs={{0,2},{2,0},{1,3},{3,1},{4,6},{6,4},{5,7},{7,5},{8,10},{10,8},{9,1... | collective-permute-start | bytes 1769480 | tf_op jit(solution)/shard_map/ppermute | solution.py:319
  416.4 13.6 %collective-permute-start.61 = (bf16[144,1792]{1,0:T(8,128)(2,1)S(1)}, bf16[144,1792]{1,0:T(8,128)(2,1)S(1)}, u32[]{:S(2)}, u32[]{:S(2)}) collective-permute-start(bf16[144,1792]{1,0:T(8,128)(2,1)S(1)} %add_convert_fusion.11), channel_id=1, source_target_pairs={{0,8},{2,6},{8,16},{10,2},{16,24},{18,10},{24,28},{26,18},{28,20},... | collective-permute-start | bytes 1548296 | tf_op jit(solution)/shard_map/ppermute | solution.py:370
  419.1 27.5 %collective-permute-start.53 = (bf16[256,1152]{1,0:T(8,128)(2,1)}, bf16[256,1152]{1,0:T(8,128)(2,1)S(1)}, u32[]{:S(2)}, u32[]{:S(2)}) collective-permute-start(bf16[256,1152]{1,0:T(8,128)(2,1)} %add_convert_fusion.6), channel_id=1, source_target_pairs={{0,1},{1,0},{2,3},{3,2},{4,5},{5,4},{6,7},{7,6},{8,9},{9,8},{10,11... | collective-permute-start | bytes 1769480 | tf_op jit(solution)/shard_map/ppermute | solution.py:319
  432.4 16.9 %collective-permute-start.62 = (bf16[144,1024]{1,0:T(8,128)(2,1)}, bf16[144,1024]{1,0:T(8,128)(2,1)}, u32[]{:S(2)}, u32[]{:S(2)}) collective-permute-start(bf16[144,1024]{1,0:T(8,128)(2,1)} %get-tuple-element.227), channel_id=1, source_target_pairs={{0,8},{2,6},{8,16},{10,2},{16,24},{18,10},{24,28},{26,18},{28,20},... | collective-permute-start | bytes 884744 | tf_op jit(solution)/shard_map/ppermute | solution.py:370
  433.6 24.7 %collective-permute-start.63 = (bf16[144,3584]{1,0:T(8,128)(2,1)}, bf16[144,3584]{1,0:T(8,128)(2,1)}, u32[]{:S(2)}, u32[]{:S(2)}) collective-permute-start(bf16[144,3584]{1,0:T(8,128)(2,1)} %add_convert_fusion.3), channel_id=1, source_target_pairs={{0,8},{2,6},{8,16},{10,2},{16,24},{18,10},{24,28},{26,18},{28,20},... | collective-permute-start | bytes 3096584 | tf_op jit(solution)/shard_map/ppermute | solution.py:370
  435.7 20.3 %collective-permute-start.64 = (bf16[144,1792]{1,0:T(8,128)(2,1)}, bf16[144,1792]{1,0:T(8,128)(2,1)}, u32[]{:S(2)}, u32[]{:S(2)}) collective-permute-start(bf16[144,1792]{1,0:T(8,128)(2,1)} %add_convert_fusion.10), channel_id=1, source_target_pairs={{0,8},{2,6},{8,16},{10,2},{16,24},{18,10},{24,28},{26,18},{28,20},... | collective-permute-start | bytes 1548296 | tf_op jit(solution)/shard_map/ppermute | solution.py:370
  459.9 17.9 %collective-permute-start.66 = (bf16[144,3584]{1,0:T(8,128)(2,1)S(1)}, bf16[144,3584]{1,0:T(8,128)(2,1)S(1)}, u32[]{:S(2)}, u32[]{:S(2)}) collective-permute-start(bf16[144,3584]{1,0:T(8,128)(2,1)S(1)} %add_convert_fusion.2), channel_id=1, source_target_pairs={{0,8},{2,6},{8,16},{10,2},{16,24},{18,10},{24,28},{26,18},{28,20},... | collective-permute-start | bytes 3096584 | tf_op jit(solution)/shard_map/ppermute | solution.py:370
  461.2 16.6 %collective-permute-start.65 = (bf16[144,1024]{1,0:T(8,128)(2,1)S(1)}, bf16[144,1024]{1,0:T(8,128)(2,1)S(1)}, u32[]{:S(2)}, u32[]{:S(2)}) collective-permute-start(bf16[144,1024]{1,0:T(8,128)(2,1)S(1)} %add_convert_fusion.21), channel_id=1, source_target_pairs={{0,8},{2,6},{8,16},{10,2},{16,24},{18,10},{24,28},{26,18},{28,20},... | collective-permute-start | bytes 884744 | tf_op jit(solution)/shard_map/ppermute | solution.py:370
  479.1 21.5 %collective-permute-start.70 = (bf16[144,3584]{1,0:T(8,128)(2,1)}, bf16[144,3584]{1,0:T(8,128)(2,1)}, u32[]{:S(2)}, u32[]{:S(2)}) collective-permute-start(bf16[144,3584]{1,0:T(8,128)(2,1)} %add_convert_fusion.1), channel_id=1, source_target_pairs={{0,8},{2,6},{8,16},{10,2},{16,24},{18,10},{24,28},{26,18},{28,20},... | collective-permute-start | bytes 3096584 | tf_op jit(solution)/shard_map/ppermute | solution.py:370
  480.3 20.2 %collective-permute-start.69 = (bf16[144,1024]{1,0:T(8,128)(2,1)S(1)}, bf16[144,1024]{1,0:T(8,128)(2,1)S(1)}, u32[]{:S(2)}, u32[]{:S(2)}) collective-permute-start(bf16[144,1024]{1,0:T(8,128)(2,1)S(1)} %add_convert_fusion.20), channel_id=1, source_target_pairs={{0,8},{2,6},{8,16},{10,2},{16,24},{18,10},{24,28},{26,18},{28,20},... | collective-permute-start | bytes 884744 | tf_op jit(solution)/shard_map/ppermute | solution.py:370
  482.4 26.5 %all-to-all-start.4 = ((bf16[8,32,1152]{2,1,0:T(8,128)(2,1)}), bf16[8,32,1152]{2,1,0:T(8,128)(2,1)S(1)}, u32[]{:S(2)}, u32[]{:S(2)}) async-start(bf16[8,32,1152]{2,1,0:T(8,128)(2,1)} %bitcast.72), calls=%async_computation.4 | async-start | bytes 1179648 | tf_op jit(solution)/shard_map/all_to_all | solution.py:469
  508.9 20.9 %collective-permute-start.72 = (bf16[144,3584]{1,0:T(8,128)(2,1)}, bf16[144,3584]{1,0:T(8,128)(2,1)S(1)}, u32[]{:S(2)}, u32[]{:S(2)}) collective-permute-start(bf16[144,3584]{1,0:T(8,128)(2,1)} %add_convert_fusion), channel_id=1, source_target_pairs={{0,8},{2,6},{8,16},{10,2},{16,24},{18,10},{24,28},{26,18},{28,20},... | collective-permute-start | bytes 3096584 | tf_op jit(solution)/shard_map/ppermute | solution.py:370
  511.0 17.0 %collective-permute-start.71 = (bf16[144,1024]{1,0:T(8,128)(2,1)S(1)}, bf16[144,1024]{1,0:T(8,128)(2,1)S(1)}, u32[]{:S(2)}, u32[]{:S(2)}) collective-permute-start(bf16[144,1024]{1,0:T(8,128)(2,1)S(1)} %add_convert_fusion.19), channel_id=1, source_target_pairs={{0,8},{2,6},{8,16},{10,2},{16,24},{18,10},{24,28},{26,18},{28,20},... | collective-permute-start | bytes 884744 | tf_op jit(solution)/shard_map/ppermute | solution.py:370
  532.9 9.7 %collective-permute-start.84 = (f32[72,1728]{1,0:T(8,128)S(1)}, f32[72,1728]{1,0:T(8,128)S(1)}, u32[]{:S(2)}, u32[]{:S(2)}) collective-permute-start(f32[72,1728]{1,0:T(8,128)S(1)} %get-tuple-element.279), channel_id=1, source_target_pairs={{0,2},{2,0},{1,3},{3,1},{4,6},{6,4},{5,7},{7,5},{8,10},{10,8},{9,1... | collective-permute-start | bytes 1493000 | tf_op jit(solution)/shard_map/ppermute | solution.py:319
  (155 other events, 1473.8 us)

commit v3 on v2

--- a/solution.py
+++ b/solution.py
@@ -273,17 +273,23 @@
 
 def outer_kernel(groups, spots, *refs):
     count = spots.shape[0]
-    outs, whole = refs[-1 - count : -1], refs[-1]
+    outs, whole, sems = refs[-2 - count : -2], refs[-2], refs[-1]
     feats = whole.shape[0] // count
-    used, column = 0, 0
-    for lefts, rights in groups:
+    used, column, copies = 0, 0, []
+    for n, (lefts, rights) in enumerate(groups):
         left = jnp.concatenate([r[...] for r in refs[used : used + lefts]], axis=0)
         right = jnp.concatenate([r[...] for r in refs[used + lefts : used + lefts + rights]], axis=0)
-        whole[:, column : column + right.shape[1]] = mm_tn(left, right).astype(BF16)
-        used, column = used + lefts + rights, column + right.shape[1]
-    for k, out in enumerate(outs):
-        first = pl.multiple_of(spots[(k + 1) % count] * feats, 16)
-        out[...] = whole[pl.ds(first, feats), :]
+        columns = slice(column, column + right.shape[1])
+        whole[:, columns] = mm_tn(left, right).astype(BF16)
+        for k, out in enumerate(outs):
+            first = pl.multiple_of(spots[(k + 1) % count] * feats, 16)
+            copies.append(
+                pltpu.make_async_copy(whole.at[pl.ds(first, feats), columns], out.at[:, columns], sems.at[n, k])
+            )
+            copies[-1].start()
+        used, column = used + lefts + rights, columns.stop
+    for copy in copies:
+        copy.wait()
 
 
 def outer(products, spots):
@@ -296,9 +302,9 @@
         functools.partial(outer_kernel, [(len(left), len(right)) for left, right in products]),
         [struct((width // count, total), BF16)] * count,
         (spots, *ins),
-        scratch=[pltpu.VMEM((width, total), BF16)],
+        scratch=[pltpu.VMEM((width, total), BF16), pltpu.SemaphoreType.DMA((len(products), count))],
         in_specs=[pl.BlockSpec(memory_space=pltpu.SMEM)] + [vmem] * len(ins),
-        out_specs=[vmem] * count,
+        out_specs=[pl.BlockSpec(memory_space=pl.ANY)] * count,
         mib=32,
     )
 
@@ -461,9 +467,10 @@
         moved = moved.reshape(feats, -1)
         return [moved[:, i * padded : (i + 1) * padded] for i in range(len(arrays))]
 
-    def to_rows(values):
-        moved = lax.all_to_all(values.reshape(seqs, span, width), "seq", split_axis=0, concat_axis=0, tiled=True)
-        return moved.reshape(seqs * span, width)
+    def to_rows(*arrays):
+        values = jnp.concatenate([v.reshape(seqs, span, width) for v in arrays], axis=1)
+        moved = lax.all_to_all(values, "seq", split_axis=0, concat_axis=0, tiled=True)
+        return [moved[:, i * span : (i + 1) * span].reshape(seqs * span, width) for i in range(len(arrays))]
 
     def from_rows(values):
         moved = lax.all_to_all(values.reshape(seqs, span, width), "seq", split_axis=0, concat_axis=0, tiled=True)
@@ -480,20 +487,25 @@
     some = jnp.concatenate([kv_block, jnp.pad(some, ((0, kv_block.shape[0] - own_feats), (0, 0)))], axis=1)
     moving = some
     some = put(jnp.zeros((seqs,) + some.shape, BF16), some, 0, spots[0])
-    x = to_rows(tokens)
+    gain_rows = moving[own_feats:, : 2 * HD]
+    gain_rows = put(jnp.zeros((seqs,) + gain_rows.shape, BF16), gain_rows, 0, spots[0])
+    (x,) = to_rows(tokens)
     for step in range(1, seqs):
-        if step == 3:
+        if step == 5:
             moving = together([moving], x)[0]
         moving = hop(moving)
         some = put(some, moving, 0, spots[step])
+        gain_rows = put(gain_rows, moving[own_feats:, : 2 * HD], 0, spots[step])
     early = moving
-    if cores == 2:
-        other = shift(some, "core", 1)
-        some = jnp.where(c_index == 0, jnp.stack([some, other], axis=1), jnp.stack([other, some], axis=1))
-    else:
-        some = lax.all_gather(some, "core", axis=1)
+    def with_core(values):
+        if cores != 2:
+            return lax.all_gather(values, "core", axis=1)
+        other = shift(values, "core", 1)
+        return jnp.where(c_index == 0, jnp.stack([values, other], axis=1), jnp.stack([other, values], axis=1))
+
+    gain_all = with_core(gain_rows)[:, :, 0].astype(F32)
+    some = with_core(some)
     some = some.reshape((seqs * cores,) + some.shape[2:])
-    gain_all = some[:, own_feats].astype(F32).reshape(seqs, cores, -1)
     first = 2 * HD + (c_index * HD if split_heads else 0)
 
     def columns(start, many):
@@ -554,7 +566,7 @@
         for i, part in zip(q_blocks, r_parts):
             spread[i] = part
         r_parts = spread
-    shares, _ = scatter_rows(by_tensor(r_parts))
+    shares, sent = scatter_rows(by_tensor(r_parts))
 
     branch, middle, f_own = small_call(
         functools.partial(middle_kernel, len(shares)),
@@ -566,41 +578,45 @@
     blocks = to_columns([gate_weight, up_weight, down_weight], hidden)
     moving = together(blocks, early)
     fulls = [put(jnp.zeros((seqs, feats, hidden), BF16), v, 0, spots[0]) for v in moving]
-    ahead = {2: a_own, 4: o, 6: f_own}
+    ahead = {2: (0, [a_own]), 3: (1, [qkv_full, out_full]), 4: (2, sent), 6: (0, [f_own])}
     for step in range(1, seqs):
         if step in ahead:
-            moving = together(moving, ahead[step])
+            chain, values = ahead[step]
+            moving = list(moving)
+            (moving[chain],) = together([moving[chain]], *values)
         moving = [hop(v) for v in moving]
+        if step == seqs - 2:
+            nearly = moving
         fulls = [put(full, v, 0, spots[step]) for full, v in zip(fulls, moving)]
     gate_full, up_full, down_full = fulls
     gate_full, up_full, down_full = (w.reshape(width, hidden) for w in (gate_full, up_full, down_full))
-    gates, ups, hids = zip(*(hidden_forward(line, gate_full, up_full) for line in f_all))
-    cotangent = to_rows(together([out_grad], *moving)[0])
-    e_parts = [None] * tensors
-    for k in list(range(1, tensors)) + [0]:
-        e_parts[k] = down_forward(hids[k] if k else together([hids[k]], cotangent)[0], down_full, cores)
-    shares, _ = scatter_rows(e_parts)
+    f_pieces = flat(f_all)
+    keep_gate, keep_up, hid = hidden_forward(f_pieces, gate_full, up_full)
+    (cotangent,) = to_rows(*together([out_grad], *nearly))
+    shares, _ = scatter_rows(by_tensor(down_forward(hid, down_full, group)))
     output, de_own, gain_fo = small_call(
         functools.partial(close_kernel, len(shares)),
         [block, block, vector],
         (*shares, middle, cotangent, g_fo),
     )
 
-    de_all = gather_rows(de_own)
-    downs = RingSum(outer([(flat(de_all), hids)], spot_line))
-    dgates, dups, df_parts = [None] * tensors, [None] * tensors, [None] * tensors
-    for k in list(range(1, tensors)) + [0]:
-        dgates[k], dups[k], *df_parts[k] = hidden_backward(
-            together(de_all[k], downs.sum), gates[k], ups[k], gate_full, up_full, down_full
-        )
-        downs.step()
-        downs.wait(dgates[k])
-    output = from_rows(together([output], downs.sum)[0])
-    shares, _ = scatter_rows(df_parts)
-    pieces = flat(f_all)
-    bigs = RingSum(outer([(pieces, together(dgates, downs.sum)), (pieces, dups)], spot_line))
+    output = from_rows(output)
+    de_all = flat(gather_rows(de_own))
+    downs = RingSum(outer([(de_all, together([hid], output))], spot_line))
+    dgate, dup, *df_parts = hidden_backward(
+        together(de_all, downs.sum), keep_gate, keep_up, gate_full, up_full, down_full
+    )
     downs.step()
-    rings = [bigs, downs]
+    downs.wait(dgate)
+    shares, _ = scatter_rows(by_tensor(df_parts))
+    gates = RingSum(outer([(f_pieces, together([dgate], downs.sum))], spot_line))
+    downs.step()
+    downs.wait(gates.sum)
+    first_gate = gates.sum
+    gates.step()
+    ups = RingSum(outer([(f_pieces, together([dup], first_gate, downs.sum))], spot_line))
+    downs.step()
+    rings = [ups, gates, downs]
     meet(rings)
 
     def stage():
@@ -612,9 +628,9 @@
     dmid, dr_own, gain_fi, gain_ao = small_call(
         functools.partial(turn_kernel, len(shares)),
         [struct((size, width), F32), block, vector, vector],
-        (*together(shares, bigs.blocks[0]), middle, cotangent, branch, g_fi, g_ao),
-    )
-    meet(rings, dr_own, output)
+        (*together(shares, ups.blocks[0]), middle, cotangent, branch, g_fi, g_ao),
+    )
+    meet(rings, dr_own)
 
     dr_all = flat(gather_rows(dr_own))
     dr_used = [dr_all[i] for i in q_blocks]
@@ -632,8 +648,10 @@
     shares, sent = scatter_rows(by_tensor(da_parts))
     stage()
     smalls = RingSum(outer([(a_all, [grads]), (dr_used, [o])], spot_line))
-    rings.append(smalls)
+    smalls.step()
     meet(rings, *sent)
+    smalls.wait(ups.sum)
+    smalls.step()
     stage()
     input_grad, gain_in = small_call(
         functools.partial(last_kernel, len(shares)),
@@ -642,27 +660,25 @@
     )
     gain_grads = (gain_in, gain_ao, gain_fi, gain_fo, gain_q, gain_k)
     packed = jnp.concatenate([g.reshape(seqs * cores, -1) for g in gain_grads], axis=1)
+    rings.append(smalls)
     meet(rings, input_grad, packed)
     input_grad = from_rows(input_grad)
-    near = [e for e in exchanges() if e[0] != "seq"]
+    for way in [e for e in exchanges() if e[0] != "seq"]:
+        packed = exchange(packed, *way)
     far = [e for e in exchanges() if e[0] == "seq"]
-    for way in near:
-        packed = exchange(packed, *way)
-    stage()
-    meet(rings, packed)
-    while bigs.left():
+    while ups.left():
         stage()
-        meet(rings, input_grad)
-    (packed,) = together([packed], bigs.sum)
+        meet(rings, packed)
+    (packed,) = together([packed], ups.sum)
     while smalls.left() or far:
         if smalls.left():
             smalls.step()
         if far:
             packed = exchange(packed, *far.pop(0))
-            smalls.wait(packed)
-            (packed,) = together([packed], smalls.sum)
+        smalls.wait(packed)
+        (packed,) = together([packed], smalls.sum)
     down_sum, small_sum = downs.sum, smalls.sum
-    gate_sum, up_sum = bigs.sum[:, :hidden], bigs.sum[:, hidden:]
+    gate_sum, up_sum = gates.sum, ups.sum
 
     def to_owner(values):
         values = values.astype(F32)

time: 575 us -> 561 us (0.976)
  waiting for transfers between devices: 215 us -> 171 us
  Pallas kernels: 82.7 us -> 98.8 us
  starting transfers between devices: 100 us -> 116 us
  local copies, waits for them, and re-layouts: 120 us -> 108 us
  other arithmetic: 43.5 us -> 53.9 us
    ppermute x49 -> x56, waiting for transfers between devices: 149 us -> 117 us  [hop(): return lax.ppermute(values, ('seq', 'core'), pairs)]
    unnamed x259 -> x222, local copies, waits for them, and re-layouts: 52.9 us -> 27.3 us
    pallas_call x16 -> x14, Pallas kernels: 82.7 us -> 98.8 us  [call(): pl.pallas_call(kernel, out_shape=outs, scratch_shapes=list(scratch), comp...]
    ppermute x32 -> x33, waiting for transfers between devices: 42.6 us -> 28.2 us  [shift(): lax.ppermute(values, axis, [(i, (i + step) % size) for i in range(size)])]
    dynamic_update_slice x31 -> x39, local copies, waits for them, and re-layouts: 44.3 us -> 53.3 us  [put(): lax.dynamic_update_slice(full, block[None], (spot, row, 0), allow_negativ...]
    convert_element_type x18 -> x24, other arithmetic: 15.7 us -> 22.7 us  [step(): self.sum = total if self.left() == 0 else total.astype(BF16)]
    ppermute x49 -> x56, starting transfers between devices: 62.8 us -> 68.8 us  [hop(): return lax.ppermute(values, ('seq', 'core'), pairs)]
    ppermute x32 -> x33, starting transfers between devices: 11.7 us -> 17 us  [shift(): lax.ppermute(values, axis, [(i, (i + step) % size) for i in range(size)])]
  transfers between devices with their start and end apart: 91 -> 99, of which waited for: 45 -> 46; matrix products, arithmetic and copies ran while one was open for 18% -> 23% of each run, Pallas kernels for 13% -> 15%
where the time goes in v3:
time: 561 us; the launch traced here: 550 us
  waiting for transfers between devices  171 us (30%)
  starting transfers between devices  116 us (21%)
  local copies, waits for them, and re-layouts  108 us (19%)
  Pallas kernels  98.8 us (18%)
  other arithmetic  53.9 us (10%)
    ppermute x56, waiting for transfers between devices, hop(): return lax.ppermute(values, ('seq', 'core'), pairs)  117 us
    pallas_call x14, Pallas kernels, call(): pl.pallas_call(kernel, out_shape=outs, scratch_shapes=list(scratch), comp...  98.8 us
    ppermute x56, starting transfers between devices, hop(): return lax.ppermute(values, ('seq', 'core'), pairs)  68.8 us
    dynamic_update_slice x39, local copies, waits for them, and re-layouts, put(): lax.dynamic_update_slice(full, block[None], (spot, row, 0), allow_negativ...  53.3 us
    ppermute x33, waiting for transfers between devices, shift(): lax.ppermute(values, axis, [(i, (i + step) % size) for i in range(size)])  28.2 us
    unnamed x222, local copies, waits for them, and re-layouts  27.3 us
    convert_element_type x24, other arithmetic, step(): self.sum = total if self.left() == 0 else total.astype(BF16)  22.7 us
    ppermute x33, starting transfers between devices, shift(): lax.ppermute(values, axis, [(i, (i + step) % size) for i in range(size)])  17 us
  transfers between devices with their start and end apart: 99, of which 46 were waited for; matrix products, arithmetic and copies ran while one was open for 23% of the time, Pallas kernels for 15%

profile of v3, /device:TPU:0, one launch (start us, length us, event | category | flops | bytes accessed | tf_op | source)
XLA Modules:
  0.0 550.0 jit_solution(730419549110864992)
XLA Ops:
  3.2 3.1 collective-permute-start
  13.8 3.7 all-to-all-start.1
  19.9 4.8 all-to-all-start
  37.7 3.0 collective-permute-done.1
  44.2 3.5 collective-permute-done.2
  50.4 3.8 collective-permute-done.3
  56.6 3.8 collective-permute-done.4
  62.8 3.8 collective-permute-done.5
  69.0 3.8 collective-permute-done.6
  82.3 2.7 broadcast.201.clone
  85.0 2.6 bitcast_dynamic-update-slice_fusion.23
  90.8 2.5 bitcast_dynamic-update-slice_fusion.22
  94.8 2.6 bitcast_dynamic-update-slice_fusion.6
  97.4 2.4 collective-permute-start.33
  99.8 2.5 bitcast_dynamic-update-slice_fusion.14
  111.2 3.7 collective-permute-done.26
  115.3 2.5 bitcast_dynamic-update-slice_fusion.13
  117.8 2.7 collective-permute-done.20
  120.8 2.5 bitcast_dynamic-update-slice_fusion.20
  123.3 4.3 maximum_select_fusion
  130.1 2.7 collective-permute-start.27
  134.5 10.8 %shard_map.290 = (bf16[1024,256]{1,0:T(8,128)(2,1)S(1)}, bf16[1024,1024]{1,0:T(8,128)(2,1)}, bf16[1024,512]{1,0:T(8,128)(2,1)}, bf16[1024,256]{1,0:T(8,128)(2,1)...) custom-call(bf16[256,1152]{1,0:T(8,128)(2,1)} %copy-done.9, ...), custom_call_target="tpu_custom_call" | custom-call | bytes 1 | tf_op jit(solution)/shard_map/pallas_call | solution.py:66
  148.1 2.5 bitcast_dynamic-update-slice_fusion.19
  157.4 4.2 collective-permute-done.28
  180.2 3.4 collective-permute-done.23
  186.5 2.6 collective-permute-done.30
  191.2 3.4 collective-permute-done.37
  197.2 3.0 collective-permute-done.24
  201.7 4.0 collective-permute-done.31
  206.4 14.5 %shard_map.292 = (bf16[1024,1792]{1,0:T(8,128)(2,1)S(1)}, bf16[1024,1792]{1,0:T(8,128)(2,1)S(1)}, bf16[1024,1792]{1,0:T(8,128)(2,1)S(1)}) custom-call(bf16[256,1152]{1,0:T(8,128)(2,1)S(1)} %get-tuple-element.151.refs_0_, bf16[256,1152]{1,0:T(8,128)(2,1)S(1)} %collective-permute-done.15.refs_1_, bf16[256,1152]{1,0:T(8,128)(2,1)S(1)} %collective-permute-done.16.refs_2_, ...), custom_call_target="tpu_custom_call" | custom-call | bytes 1 | tf_op jit(solution)/shard_map/pallas_call | solution.py:66
  225.4 5.9 %shard_map.293 = (bf16[256,1152]{1,0:T(8,128)(2,1)S(1)}, bf16[256,1152]{1,0:T(8,128)(2,1)S(1)}, bf16[256,1152]{1,0:T(8,128)(2,1)S(1)}, bf16[256,1152]{1,0:T(8,128)(2,1)}) custom-call(bf16[1024,1792]{1,0:T(8,128)(2,1)S(1)} %get-tuple-element.168.hid_ref.refs_4_, bf16[1152,1792]{1,0:T(8,128)(2,1)S(1)} %bitcast.198), custom_call_target="tpu_custom_call" | custom-call | bytes 1 | tf_op jit(solution)/shard_map/pallas_call | solution.py:66
  233.0 4.8 all-to-all-start.2
  244.3 10.1 %all-to-all-done.2 = bf16[8,32,1152]{2,1,0:T(8,128)(2,1)S(1)} async-done(((bf16[8,32,1152]{2,1,0:T(8,128)(2,1)}), bf16[8,32,1152]{2,1,0:T(8,128)(2,1)S(1)}, u32[]{:S(2)}, u32[]{:S(2)}) %all-to-all-start.2) | async-done | bytes 589856 | tf_op jit(solution)/shard_map/all_to_all | solution.py:472
  258.8 2.8 shard_map.294
  263.8 6.0 %all-to-all-start.3 = ((bf16[8,32,1152]{2,1,0:T(8,128)(2,1)}), bf16[8,32,1152]{2,1,0:T(8,128)(2,1)S(1)}, u32[]{:S(2)}, u32[]{:S(2)}) async-start(bf16[8,32,1152]{2,1,0:T(8,128)(2,1)} %bitcast.79), calls=%async_computation.3 | async-start | bytes 1179648 | tf_op jit(solution)/shard_map/all_to_all | solution.py:476
  269.8 7.5 %collective-permute-done.43.refs_2_ = bf16[256,1152]{1,0:T(8,128)(2,1)} collective-permute-done((bf16[256,1152]{1,0:T(8,128)(2,1)}, bf16[256,1152]{1,0:T(8,128)(2,1)}, u32[]{:S(2)}, u32[]{:S(2)}) %collective-permute-start.43) | collective-permute-done | bytes 589856 | tf_op jit(solution)/shard_map/ppermute | solution.py:325
  277.3 8.0 %all-to-all-done.3 = bf16[8,32,1152]{2,1,0:T(8,128)(2,1)S(1)} async-done(((bf16[8,32,1152]{2,1,0:T(8,128)(2,1)}), bf16[8,32,1152]{2,1,0:T(8,128)(2,1)S(1)}, u32[]{:S(2)}, u32[]{:S(2)}) %all-to-all-start.3) | async-done | bytes 589856 | tf_op jit(solution)/shard_map/all_to_all | solution.py:476
  286.2 2.6 copy-done.8
  289.5 9.0 %shard_map.295 = (bf16[144,1792]{1,0:T(8,128)(2,1)S(1)}, bf16[144,1792]{1,0:T(8,128)(2,1)S(1)}, bf16[144,1792]{1,0:T(8,128)(2,1)S(1)}, bf16[144,1792]{1,0:T(8,12...) custom-call(s32[8]{0:T(128)S(1)} %copy-done.86, ...), custom_call_target="tpu_custom_call" | custom-call | bytes 1 | tf_op jit(solution)/shard_map/pallas_call | solution.py:66
  303.2 19.1 %shard_map.296 = (bf16[1024,1792]{1,0:T(8,128)(2,1)S(1)}, bf16[1024,1792]{1,0:T(8,128)(2,1)S(1)}, bf16[256,1152]{1,0:T(8,128)(2,1)S(1)}, bf16[256,1152]{1,0:T(8,...) custom-call(bf16[256,1152]{1,0:T(8,128)(2,1)} %get-tuple-element.170.refs_0_, ...), custom_call_target="tpu_custom_call" | custom-call | bytes 1 | tf_op jit(solution)/shard_map/pallas_call | solution.py:66
  324.2 8.0 %shard_map.297 = (bf16[144,1792]{1,0:T(8,128)(2,1)S(1)}, bf16[144,1792]{1,0:T(8,128)(2,1)S(1)}, bf16[144,1792]{1,0:T(8,128)(2,1)S(1)}, bf16[144,1792]{1,0:T(8,12...) custom-call(s32[8]{0:T(128)S(1)} %copy-done.86, ...), custom_call_target="tpu_custom_call" | custom-call | bytes 1 | tf_op jit(solution)/shard_map/pallas_call | solution.py:66
  336.7 7.9 %shard_map.298 = (bf16[144,1792]{1,0:T(8,128)(2,1)S(1)}, bf16[144,1792]{1,0:T(8,128)(2,1)S(1)}, bf16[144,1792]{1,0:T(8,128)(2,1)S(1)}, bf16[144,1792]{1,0:T(8,12...) custom-call(s32[8]{0:T(128)S(1)} %copy-done.87, ...), custom_call_target="tpu_custom_call" | custom-call | bytes 1 | tf_op jit(solution)/shard_map/pallas_call | solution.py:66
  346.4 3.0 collective-permute-done.46.refs_0_
  349.4 2.7 shard_map.299
  356.0 11.3 %collective-permute-done.51.refs_2_.refs_7_ = bf16[256,1152]{1,0:T(8,128)(2,1)S(1)} collective-permute-done((bf16[256,1152]{1,0:T(8,128)(2,1)S(1)}, bf16[256,1152]{1,0:T(8,128)(2,1)S(1)}, u32[]{:S(2)}, u32[]{:S(2)}) %collective-permute-start.51) | collective-permute-done | bytes 589856 | tf_op jit(solution)/shard_map/ppermute | solution.py:325
  369.7 4.6 collective-permute-done.59
  378.2 10.5 %shard_map.300 = (bf16[1024,768]{1,0:T(8,128)(2,1)}, f32[1,256]{1,0:T(1,128)S(1)}, f32[1,256]{1,0:T(1,128)S(1)}, bf16[256,1152]{1,0:T(8,128)(2,1)S(1)}, bf16[256...) custom-call(bf16[256,1152]{1,0:T(8,128)(2,1)S(1)} %get-tuple-element.194.refs_0_.refs_5_, ...), custom_call_target="tpu_custom_call" | custom-call | bytes 1 | tf_op jit(solution)/shard_map/pallas_call | solution.py:66
  392.9 5.2 shard_map.302
  409.5 2.5 collective-permute-done.67
  413.0 4.6 collective-permute-done.66
  418.5 4.6 collective-permute-done.65
  444.5 6.3 %collective-permute-done.71 = bf16[144,1792]{1,0:T(8,128)(2,1)} collective-permute-done((bf16[144,1792]{1,0:T(8,128)(2,1)}, bf16[144,1792]{1,0:T(8,128)(2,1)}, u32[]{:S(2)}, u32[]{:S(2)}) %collective-permute-start.71) | collective-permute-done | bytes 516128 | tf_op jit(solution)/shard_map/ppermute | solution.py:376
  459.0 2.5 collective-permute-done.76
  462.2 3.7 collective-permute-done.74
  466.7 4.6 collective-permute-done.73
  475.1 4.2 all-to-all-start.4
  482.2 5.7 %collective-permute-done.78 = bf16[144,1792]{1,0:T(8,128)(2,1)} collective-permute-done((bf16[144,1792]{1,0:T(8,128)(2,1)}, bf16[144,1792]{1,0:T(8,128)(2,1)}, u32[]{:S(2)}, u32[]{:S(2)}) %collective-permute-start.78) | collective-permute-done | bytes 516128 | tf_op jit(solution)/shard_map/ppermute | solution.py:376
  489.9 8.4 %collective-permute-done.79 = bf16[144,1792]{1,0:T(8,128)(2,1)S(1)} collective-permute-done((bf16[144,1792]{1,0:T(8,128)(2,1)}, bf16[144,1792]{1,0:T(8,128)(2,1)S(1)}, u32[]{:S(2)}, u32[]{:S(2)}) %collective-permute-start.79) | collective-permute-done | bytes 516128 | tf_op jit(solution)/shard_map/ppermute | solution.py:376
  499.3 4.9 collective-permute-start.80
  508.6 5.5 %collective-permute-done.81 = bf16[144,1792]{1,0:T(8,128)(2,1)} collective-permute-done((bf16[144,1792]{1,0:T(8,128)(2,1)}, bf16[144,1792]{1,0:T(8,128)(2,1)}, u32[]{:S(2)}, u32[]{:S(2)}) %collective-permute-start.81) | collective-permute-done | bytes 516128 | tf_op jit(solution)/shard_map/ppermute | solution.py:376
  519.9 3.8 collective-permute-done.82
  530.6 2.6 collective-permute-done.84
  535.3 2.7 collective-permute-done.86
  542.9 3.5 collective-permute-done.89
  (541 shorter events, 233.0 us)
Async XLA Ops:
  3.2 30.4 %collective-permute-start = (bf16[80,1536]{1,0:T(8,128)(2,1)S(1)}, bf16[80,1536]{1,0:T(8,128)(2,1)S(1)}, u32[]{:S(2)}, u32[]{:S(2)}) collective-permute-start(bf16[80,1536]{1,0:T(8,128)(2,1)S(1)} %pad_maximum_fusion.2), channel_id=1, source_target_pairs={{0,8},{2,6},{8,16},{10,2},{16,24},{18,10},{24,28},{26,18},{28,20},... | collective-permute-start | bytes 737288 | tf_op jit(solution)/shard_map/ppermute | solution.py:376
  19.9 34.3 %all-to-all-start = ((bf16[8,32,1152]{2,1,0:T(8,128)(2,1)}), bf16[8,32,1152]{2,1,0:T(8,128)(2,1)S(1)}, u32[]{:S(2)}, u32[]{:S(2)}) async-start(bf16[8,32,1152]{2,1,0:T(8,128)(2,1)} %bitcast), calls=%async_computation | async-start | bytes 1179648 | tf_op jit(solution)/shard_map/all_to_all | solution.py:472
  74.2 49.1 %collective-permute-start.11 = (bf16[8,80,1536]{2,1,0:T(8,128)(2,1)}, bf16[8,80,1536]{2,1,0:T(8,128)(2,1)}, u32[]{:S(2)}, u32[]{:S(2)}) collective-permute-start(bf16[8,80,1536]{2,1,0:T(8,128)(2,1)} %bitcast_dynamic-update-slice_fusion.24), channel_id=1, source_target_pairs={{0,2},{2,0},{1,3},{3,1},{4,6},{6,4},{5,7},{7,5},{8,10},{10,8},{9,1... | collective-permute-start | bytes 5898248 | tf_op jit(solution)/shard_map/ppermute | solution.py:325
  74.2 23.2 %collective-permute-start.25 = (bf16[144,1792]{1,0:T(8,128)(2,1)S(1)}, bf16[144,1792]{1,0:T(8,128)(2,1)}, u32[]{:S(2)}, u32[]{:S(2)}) collective-permute-start(bf16[144,1792]{1,0:T(8,128)(2,1)S(1)} %get-tuple-element.155), channel_id=1, source_target_pairs={{0,8},{2,6},{8,16},{10,2},{16,24},{18,10},{24,28},{26,18},{28,20},... | collective-permute-start | bytes 1548296 | tf_op jit(solution)/shard_map/ppermute | solution.py:376
  75.2 12.4 %collective-permute-start.7 = (bf16[8,8,512]{2,1,0:T(8,128)(2,1)S(1)}, bf16[8,8,512]{2,1,0:T(8,128)(2,1)S(1)}, u32[]{:S(2)}, u32[]{:S(2)}) collective-permute-start(bf16[8,8,512]{2,1,0:T(8,128)(2,1)S(1)} %constant_dynamic-update-slice_fusion), channel_id=1, source_target_pairs={{0,2},{2,0},{1,3},{3,1},{4,6},{6,4},{5,7},{7,5},{8,10},{10,8},{9,1... | collective-permute-start | bytes 196616 | tf_op jit(solution)/shard_map/ppermute | solution.py:325
  77.1 13.6 %collective-permute-start.18 = (bf16[144,1792]{1,0:T(8,128)(2,1)}, bf16[144,1792]{1,0:T(8,128)(2,1)}, u32[]{:S(2)}, u32[]{:S(2)}) collective-permute-start(bf16[144,1792]{1,0:T(8,128)(2,1)} %get-tuple-element.152), channel_id=1, source_target_pairs={{0,8},{2,6},{8,16},{10,2},{16,24},{18,10},{24,28},{26,18},{28,20},... | collective-permute-start | bytes 1548296 | tf_op jit(solution)/shard_map/ppermute | solution.py:376
  77.8 16.6 %collective-permute-start.32 = (bf16[144,1792]{1,0:T(8,128)(2,1)}, bf16[144,1792]{1,0:T(8,128)(2,1)}, u32[]{:S(2)}, u32[]{:S(2)}) collective-permute-start(bf16[144,1792]{1,0:T(8,128)(2,1)} %get-tuple-element.158), channel_id=1, source_target_pairs={{0,8},{2,6},{8,16},{10,2},{16,24},{18,10},{24,28},{26,18},{28,20},... | collective-permute-start | bytes 1548296 | tf_op jit(solution)/shard_map/ppermute | solution.py:376
  88.7 15.0 %collective-permute-start.9 = (bf16[256,1152]{1,0:T(8,128)(2,1)S(1)}, bf16[256,1152]{1,0:T(8,128)(2,1)S(1)}, u32[]{:S(2)}, u32[]{:S(2)}) collective-permute-start(bf16[256,1152]{1,0:T(8,128)(2,1)S(1)} %shard_map.289.refs_0_), channel_id=1, source_target_pairs={{0,1},{1,0},{2,3},{3,2},{4,5},{5,4},{6,7},{7,6},{8,9},{9,8},{10,11... | collective-permute-start | bytes 1769480 | tf_op jit(solution)/shard_map/ppermute | solution.py:325
  90.7 42.7 %collective-permute-start.8 = (bf16[256,1152]{1,0:T(8,128)(2,1)S(1)}, bf16[256,1152]{1,0:T(8,128)(2,1)S(1)}, u32[]{:S(2)}, u32[]{:S(2)}) collective-permute-start(bf16[256,1152]{1,0:T(8,128)(2,1)S(1)} %shard_map.289.refs_0_), channel_id=1, source_target_pairs={{0,2},{2,0},{1,3},{3,1},{4,6},{6,4},{5,7},{7,5},{8,10},{10,8},{9,1... | collective-permute-start | bytes 1769480 | tf_op jit(solution)/shard_map/ppermute | solution.py:325
  94.4 11.0 %collective-permute-start.19 = (bf16[144,1792]{1,0:T(8,128)(2,1)}, bf16[144,1792]{1,0:T(8,128)(2,1)S(1)}, u32[]{:S(2)}, u32[]{:S(2)}) collective-permute-start(bf16[144,1792]{1,0:T(8,128)(2,1)} %collective-permute-done.18), channel_id=1, source_target_pairs={{0,8},{2,6},{8,16},{10,2},{16,24},{18,10},{24,28},{26,18},{28,20},... | collective-permute-start | bytes 1548296 | tf_op jit(solution)/shard_map/ppermute | solution.py:376
  97.4 11.9 %collective-permute-start.33 = (bf16[144,1792]{1,0:T(8,128)(2,1)}, bf16[144,1792]{1,0:T(8,128)(2,1)S(1)}, u32[]{:S(2)}, u32[]{:S(2)}) collective-permute-start(bf16[144,1792]{1,0:T(8,128)(2,1)} %collective-permute-done.32), channel_id=1, source_target_pairs={{0,8},{2,6},{8,16},{10,2},{16,24},{18,10},{24,28},{26,18},{28,20},... | collective-permute-start | bytes 1548296 | tf_op jit(solution)/shard_map/ppermute | solution.py:376
  103.7 11.2 %collective-permute-start.26 = (bf16[144,1792]{1,0:T(8,128)(2,1)}, bf16[144,1792]{1,0:T(8,128)(2,1)}, u32[]{:S(2)}, u32[]{:S(2)}) collective-permute-start(bf16[144,1792]{1,0:T(8,128)(2,1)} %collective-permute-done.25), channel_id=1, source_target_pairs={{0,8},{2,6},{8,16},{10,2},{16,24},{18,10},{24,28},{26,18},{28,20},... | collective-permute-start | bytes 1548296 | tf_op jit(solution)/shard_map/ppermute | solution.py:376
  105.4 28.0 %collective-permute-start.10 = (bf16[256,1152]{1,0:T(8,128)(2,1)S(1)}, bf16[256,1152]{1,0:T(8,128)(2,1)S(1)}, u32[]{:S(2)}, u32[]{:S(2)}) collective-permute-start(bf16[256,1152]{1,0:T(8,128)(2,1)S(1)} %collective-permute-done.9.refs_2_), channel_id=1, source_target_pairs={{0,2},{2,0},{1,3},{3,1},{4,6},{6,4},{5,7},{7,5},{8,10},{10,8},{9,1... | collective-permute-start | bytes 1769480 | tf_op jit(solution)/shard_map/ppermute | solution.py:325
  109.3 11.2 %collective-permute-start.20 = (bf16[144,1792]{1,0:T(8,128)(2,1)S(1)}, bf16[144,1792]{1,0:T(8,128)(2,1)}, u32[]{:S(2)}, u32[]{:S(2)}) collective-permute-start(bf16[144,1792]{1,0:T(8,128)(2,1)S(1)} %collective-permute-done.19), channel_id=1, source_target_pairs={{0,8},{2,6},{8,16},{10,2},{16,24},{18,10},{24,28},{26,18},{28,20},... | collective-permute-start | bytes 1548296 | tf_op jit(solution)/shard_map/ppermute | solution.py:376
  114.9 17.8 %collective-permute-start.34 = (bf16[144,1792]{1,0:T(8,128)(2,1)S(1)}, bf16[144,1792]{1,0:T(8,128)(2,1)S(1)}, u32[]{:S(2)}, u32[]{:S(2)}) collective-permute-start(bf16[144,1792]{1,0:T(8,128)(2,1)S(1)} %collective-permute-done.33), channel_id=1, source_target_pairs={{0,8},{2,6},{8,16},{10,2},{16,24},{18,10},{24,28},{26,18},{28,20},... | collective-permute-start | bytes 1548296 | tf_op jit(solution)/shard_map/ppermute | solution.py:376
  120.4 26.2 %collective-permute-start.21 = (bf16[144,1792]{1,0:T(8,128)(2,1)}, bf16[144,1792]{1,0:T(8,128)(2,1)}, u32[]{:S(2)}, u32[]{:S(2)}) collective-permute-start(bf16[144,1792]{1,0:T(8,128)(2,1)} %collective-permute-done.20), channel_id=1, source_target_pairs={{0,8},{2,6},{8,16},{10,2},{16,24},{18,10},{24,28},{26,18},{28,20},... | collective-permute-start | bytes 1548296 | tf_op jit(solution)/shard_map/ppermute | solution.py:376
  130.1 20.5 %collective-permute-start.27 = (bf16[144,1792]{1,0:T(8,128)(2,1)}, bf16[144,1792]{1,0:T(8,128)(2,1)}, u32[]{:S(2)}, u32[]{:S(2)}) collective-permute-start(bf16[144,1792]{1,0:T(8,128)(2,1)} %collective-permute-done.26), channel_id=1, source_target_pairs={{0,8},{2,6},{8,16},{10,2},{16,24},{18,10},{24,28},{26,18},{28,20},... | collective-permute-start | bytes 1548296 | tf_op jit(solution)/shard_map/ppermute | solution.py:376
  146.1 24.1 %collective-permute-start.14 = (bf16[256,1152]{1,0:T(8,128)(2,1)S(1)}, bf16[256,1152]{1,0:T(8,128)(2,1)S(1)}, u32[]{:S(2)}, u32[]{:S(2)}) collective-permute-start(bf16[256,1152]{1,0:T(8,128)(2,1)S(1)} %get-tuple-element.150), channel_id=1, source_target_pairs={{0,2},{2,0},{1,3},{3,1},{4,6},{6,4},{5,7},{7,5},{8,10},{10,8},{9,1... | collective-permute-start | bytes 1769480 | tf_op jit(solution)/shard_map/ppermute | solution.py:325
  150.6 11.0 %collective-permute-start.28 = (bf16[144,1792]{1,0:T(8,128)(2,1)}, bf16[144,1792]{1,0:T(8,128)(2,1)}, u32[]{:S(2)}, u32[]{:S(2)}) collective-permute-start(bf16[144,1792]{1,0:T(8,128)(2,1)} %collective-permute-done.27), channel_id=1, source_target_pairs={{0,8},{2,6},{8,16},{10,2},{16,24},{18,10},{24,28},{26,18},{28,20},... | collective-permute-start | bytes 1548296 | tf_op jit(solution)/shard_map/ppermute | solution.py:376
  152.9 17.4 %collective-permute-start.13 = (bf16[256,1152]{1,0:T(8,128)(2,1)S(1)}, bf16[256,1152]{1,0:T(8,128)(2,1)S(1)}, u32[]{:S(2)}, u32[]{:S(2)}) collective-permute-start(bf16[256,1152]{1,0:T(8,128)(2,1)S(1)} %add_convert_fusion.3), channel_id=1, source_target_pairs={{0,1},{1,0},{2,3},{3,2},{4,5},{5,4},{6,7},{7,6},{8,9},{9,8},{10,11... | collective-permute-start | bytes 1769480 | tf_op jit(solution)/shard_map/ppermute | solution.py:325
  154.5 12.6 %collective-permute-start.35 = (bf16[144,1792]{1,0:T(8,128)(2,1)S(1)}, bf16[144,1792]{1,0:T(8,128)(2,1)}, u32[]{:S(2)}, u32[]{:S(2)}) collective-permute-start(bf16[144,1792]{1,0:T(8,128)(2,1)S(1)} %copy-done.103), channel_id=1, source_target_pairs={{0,8},{2,6},{8,16},{10,2},{16,24},{18,10},{24,28},{26,18},{28,20},... | collective-permute-start | bytes 1548296 | tf_op jit(solution)/shard_map/ppermute | solution.py:376
  161.6 11.4 %collective-permute-start.29 = (bf16[144,1792]{1,0:T(8,128)(2,1)}, bf16[144,1792]{1,0:T(8,128)(2,1)}, u32[]{:S(2)}, u32[]{:S(2)}) collective-permute-start(bf16[144,1792]{1,0:T(8,128)(2,1)} %collective-permute-done.28), channel_id=1, source_target_pairs={{0,8},{2,6},{8,16},{10,2},{16,24},{18,10},{24,28},{26,18},{28,20},... | collective-permute-start | bytes 1548296 | tf_op jit(solution)/shard_map/ppermute | solution.py:376
  167.1 11.0 %collective-permute-start.36 = (bf16[144,1792]{1,0:T(8,128)(2,1)}, bf16[144,1792]{1,0:T(8,128)(2,1)S(1)}, u32[]{:S(2)}, u32[]{:S(2)}) collective-permute-start(bf16[144,1792]{1,0:T(8,128)(2,1)} %collective-permute-done.35), channel_id=1, source_target_pairs={{0,8},{2,6},{8,16},{10,2},{16,24},{18,10},{24,28},{26,18},{28,20},... | collective-permute-start | bytes 1548296 | tf_op jit(solution)/shard_map/ppermute | solution.py:376
  171.0 15.6 %collective-permute-start.16 = (bf16[256,1152]{1,0:T(8,128)(2,1)S(1)}, bf16[256,1152]{1,0:T(8,128)(2,1)S(1)}, u32[]{:S(2)}, u32[]{:S(2)}) collective-permute-start(bf16[256,1152]{1,0:T(8,128)(2,1)S(1)} %get-tuple-element.151.refs_0_), channel_id=1, source_target_pairs={{0,1},{1,0},{2,3},{3,2},{4,5},{5,4},{6,7},{7,6},{8,9},{9,8},{10,11... | collective-permute-start | bytes 1769480 | tf_op jit(solution)/shard_map/ppermute | solution.py:325
  172.6 33.8 %collective-permute-start.15 = (bf16[256,1152]{1,0:T(8,128)(2,1)S(1)}, bf16[256,1152]{1,0:T(8,128)(2,1)S(1)}, u32[]{:S(2)}, u32[]{:S(2)}) collective-permute-start(bf16[256,1152]{1,0:T(8,128)(2,1)S(1)} %get-tuple-element.151.refs_0_), channel_id=1, source_target_pairs={{0,2},{2,0},{1,3},{3,1},{4,6},{6,4},{5,7},{7,5},{8,10},{10,8},{9,1... | collective-permute-start | bytes 1769480 | tf_op jit(solution)/shard_map/ppermute | solution.py:325
  172.6 11.0 %collective-permute-start.23 = (bf16[144,1792]{1,0:T(8,128)(2,1)}, bf16[144,1792]{1,0:T(8,128)(2,1)S(1)}, u32[]{:S(2)}, u32[]{:S(2)}) collective-permute-start(bf16[144,1792]{1,0:T(8,128)(2,1)} %copy-done.104), channel_id=1, source_target_pairs={{0,8},{2,6},{8,16},{10,2},{16,24},{18,10},{24,28},{26,18},{28,20},... | collective-permute-start | bytes 1548296 | tf_op jit(solution)/shard_map/ppermute | solution.py:376
  173.0 16.1 %collective-permute-start.30 = (bf16[144,1792]{1,0:T(8,128)(2,1)}, bf16[144,1792]{1,0:T(8,128)(2,1)S(1)}, u32[]{:S(2)}, u32[]{:S(2)}) collective-permute-start(bf16[144,1792]{1,0:T(8,128)(2,1)} %collective-permute-done.29), channel_id=1, source_target_pairs={{0,8},{2,6},{8,16},{10,2},{16,24},{18,10},{24,28},{26,18},{28,20},... | collective-permute-start | bytes 1548296 | tf_op jit(solution)/shard_map/ppermute | solution.py:376
  178.0 16.6 %collective-permute-start.37 = (bf16[144,1792]{1,0:T(8,128)(2,1)S(1)}, bf16[144,1792]{1,0:T(8,128)(2,1)S(1)}, u32[]{:S(2)}, u32[]{:S(2)}) collective-permute-start(bf16[144,1792]{1,0:T(8,128)(2,1)S(1)} %collective-permute-done.36), channel_id=1, source_target_pairs={{0,8},{2,6},{8,16},{10,2},{16,24},{18,10},{24,28},{26,18},{28,20},... | collective-permute-start | bytes 1548296 | tf_op jit(solution)/shard_map/ppermute | solution.py:376
  183.6 16.6 %collective-permute-start.24 = (bf16[144,1792]{1,0:T(8,128)(2,1)S(1)}, bf16[144,1792]{1,0:T(8,128)(2,1)S(1)}, u32[]{:S(2)}, u32[]{:S(2)}) collective-permute-start(bf16[144,1792]{1,0:T(8,128)(2,1)S(1)} %collective-permute-done.23), channel_id=1, source_target_pairs={{0,8},{2,6},{8,16},{10,2},{16,24},{18,10},{24,28},{26,18},{28,20},... | collective-permute-start | bytes 1548296 | tf_op jit(solution)/shard_map/ppermute | solution.py:376
  186.5 19.9 %collective-permute-start.17 = (bf16[256,1152]{1,0:T(8,128)(2,1)S(1)}, bf16[256,1152]{1,0:T(8,128)(2,1)S(1)}, u32[]{:S(2)}, u32[]{:S(2)}) collective-permute-start(bf16[256,1152]{1,0:T(8,128)(2,1)S(1)} %collective-permute-done.16.refs_2_), channel_id=1, source_target_pairs={{0,2},{2,0},{1,3},{3,1},{4,6},{6,4},{5,7},{7,5},{8,10},{10,8},{9,1... | collective-permute-start | bytes 1769480 | tf_op jit(solution)/shard_map/ppermute | solution.py:325
  189.1 16.6 %collective-permute-start.31 = (bf16[144,1792]{1,0:T(8,128)(2,1)S(1)}, bf16[144,1792]{1,0:T(8,128)(2,1)S(1)}, u32[]{:S(2)}, u32[]{:S(2)}) collective-permute-start(bf16[144,1792]{1,0:T(8,128)(2,1)S(1)} %collective-permute-done.30), channel_id=1, source_target_pairs={{0,8},{2,6},{8,16},{10,2},{16,24},{18,10},{24,28},{26,18},{28,20},... | collective-permute-start | bytes 1548296 | tf_op jit(solution)/shard_map/ppermute | solution.py:376
  194.6 30.1 %collective-permute-start.38 = (bf16[144,1792]{1,0:T(8,128)(2,1)S(1)}, bf16[144,1792]{1,0:T(8,128)(2,1)S(1)}, u32[]{:S(2)}, u32[]{:S(2)}) collective-permute-start(bf16[144,1792]{1,0:T(8,128)(2,1)S(1)} %collective-permute-done.37), channel_id=1, source_target_pairs={{0,8},{2,6},{8,16},{10,2},{16,24},{18,10},{24,28},{26,18},{28,20},... | collective-permute-start | bytes 1548296 | tf_op jit(solution)/shard_map/ppermute | solution.py:376
  233.0 21.4 %all-to-all-start.2 = ((bf16[8,32,1152]{2,1,0:T(8,128)(2,1)}), bf16[8,32,1152]{2,1,0:T(8,128)(2,1)S(1)}, u32[]{:S(2)}, u32[]{:S(2)}) async-start(bf16[8,32,1152]{2,1,0:T(8,128)(2,1)} %bitcast.223), calls=%async_computation.2 | async-start | bytes 1179648 | tf_op jit(solution)/shard_map/all_to_all | solution.py:472
  237.8 16.6 %collective-permute-start.41 = (bf16[256,1152]{1,0:T(8,128)(2,1)}, bf16[256,1152]{1,0:T(8,128)(2,1)}, u32[]{:S(2)}, u32[]{:S(2)}) collective-permute-start(bf16[256,1152]{1,0:T(8,128)(2,1)} %copy-done.98), channel_id=1, source_target_pairs={{0,2},{2,0},{1,3},{3,1},{4,6},{6,4},{5,7},{7,5},{8,10},{10,8},{9,1... | collective-permute-start | bytes 1769480 | tf_op jit(solution)/shard_map/ppermute | solution.py:325
  240.1 15.7 %collective-permute-start.40 = (bf16[256,1152]{1,0:T(8,128)(2,1)}, bf16[256,1152]{1,0:T(8,128)(2,1)S(1)}, u32[]{:S(2)}, u32[]{:S(2)}) collective-permute-start(bf16[256,1152]{1,0:T(8,128)(2,1)} %add_convert_fusion.2), channel_id=1, source_target_pairs={{0,1},{1,0},{2,3},{3,2},{4,5},{5,4},{6,7},{7,6},{8,9},{9,8},{10,11... | collective-permute-start | bytes 1769480 | tf_op jit(solution)/shard_map/ppermute | solution.py:325
  262.2 15.0 %collective-permute-start.43 = (bf16[256,1152]{1,0:T(8,128)(2,1)}, bf16[256,1152]{1,0:T(8,128)(2,1)}, u32[]{:S(2)}, u32[]{:S(2)}) collective-permute-start(bf16[256,1152]{1,0:T(8,128)(2,1)} %get-tuple-element.170.refs_0_), channel_id=1, source_target_pairs={{0,1},{1,0},{2,3},{3,2},{4,5},{5,4},{6,7},{7,6},{8,9},{9,8},{10,11... | collective-permute-start | bytes 1769480 | tf_op jit(solution)/shard_map/ppermute | solution.py:325
  263.8 21.5 %all-to-all-start.3 = ((bf16[8,32,1152]{2,1,0:T(8,128)(2,1)}), bf16[8,32,1152]{2,1,0:T(8,128)(2,1)S(1)}, u32[]{:S(2)}, u32[]{:S(2)}) async-start(bf16[8,32,1152]{2,1,0:T(8,128)(2,1)} %bitcast.79), calls=%async_computation.3 | async-start | bytes 1179648 | tf_op jit(solution)/shard_map/all_to_all | solution.py:476
  269.8 15.6 %collective-permute-start.42 = (bf16[256,1152]{1,0:T(8,128)(2,1)}, bf16[256,1152]{1,0:T(8,128)(2,1)}, u32[]{:S(2)}, u32[]{:S(2)}) collective-permute-start(bf16[256,1152]{1,0:T(8,128)(2,1)} %get-tuple-element.170.refs_0_), channel_id=1, source_target_pairs={{0,2},{2,0},{1,3},{3,1},{4,6},{6,4},{5,7},{7,5},{8,10},{10,8},{9,1... | collective-permute-start | bytes 1769480 | tf_op jit(solution)/shard_map/ppermute | solution.py:325
  298.5 24.5 %collective-permute-start.48 = (bf16[144,1792]{1,0:T(8,128)(2,1)S(1)}, bf16[144,1792]{1,0:T(8,128)(2,1)S(1)}, u32[]{:S(2)}, u32[]{:S(2)}) collective-permute-start(bf16[144,1792]{1,0:T(8,128)(2,1)S(1)} %get-tuple-element.169), channel_id=1, source_target_pairs={{0,8},{2,6},{8,16},{10,2},{16,24},{18,10},{24,28},{26,18},{28,20},... | collective-permute-start | bytes 1548296 | tf_op jit(solution)/shard_map/ppermute | solution.py:376
  322.4 24.0 %collective-permute-start.47 = (bf16[256,1152]{1,0:T(8,128)(2,1)S(1)}, bf16[256,1152]{1,0:T(8,128)(2,1)S(1)}, u32[]{:S(2)}, u32[]{:S(2)}) collective-permute-start(bf16[256,1152]{1,0:T(8,128)(2,1)S(1)} %get-tuple-element.179), channel_id=1, source_target_pairs={{0,2},{2,0},{1,3},{3,1},{4,6},{6,4},{5,7},{7,5},{8,10},{10,8},{9,1... | collective-permute-start | bytes 1769480 | tf_op jit(solution)/shard_map/ppermute | solution.py:325
  332.2 13.2 %collective-permute-start.57 = (bf16[144,1792]{1,0:T(8,128)(2,1)S(1)}, bf16[144,1792]{1,0:T(8,128)(2,1)S(1)}, u32[]{:S(2)}, u32[]{:S(2)}) collective-permute-start(bf16[144,1792]{1,0:T(8,128)(2,1)S(1)} %get-tuple-element.185), channel_id=1, source_target_pairs={{0,8},{2,6},{8,16},{10,2},{16,24},{18,10},{24,28},{26,18},{28,20},... | collective-permute-start | bytes 1548296 | tf_op jit(solution)/shard_map/ppermute | solution.py:376
  333.4 16.0 %collective-permute-start.46 = (bf16[256,1152]{1,0:T(8,128)(2,1)S(1)}, bf16[256,1152]{1,0:T(8,128)(2,1)S(1)}, u32[]{:S(2)}, u32[]{:S(2)}) collective-permute-start(bf16[256,1152]{1,0:T(8,128)(2,1)S(1)} %add_convert_fusion.1), channel_id=1, source_target_pairs={{0,1},{1,0},{2,3},{3,2},{4,5},{5,4},{6,7},{7,6},{8,9},{9,8},{10,11... | collective-permute-start | bytes 1769480 | tf_op jit(solution)/shard_map/ppermute | solution.py:325
  334.9 17.9 %collective-permute-start.58 = (bf16[144,1792]{1,0:T(8,128)(2,1)}, bf16[144,1792]{1,0:T(8,128)(2,1)}, u32[]{:S(2)}, u32[]{:S(2)}) collective-permute-start(bf16[144,1792]{1,0:T(8,128)(2,1)} %add_convert_fusion.20), channel_id=1, source_target_pairs={{0,8},{2,6},{8,16},{10,2},{16,24},{18,10},{24,28},{26,18},{28,20},... | collective-permute-start | bytes 1548296 | tf_op jit(solution)/shard_map/ppermute | solution.py:376
  352.2 15.1 %collective-permute-start.51 = (bf16[256,1152]{1,0:T(8,128)(2,1)S(1)}, bf16[256,1152]{1,0:T(8,128)(2,1)S(1)}, u32[]{:S(2)}, u32[]{:S(2)}) collective-permute-start(bf16[256,1152]{1,0:T(8,128)(2,1)S(1)} %get-tuple-element.194.refs_0_.refs_5_), channel_id=1, source_target_pairs={{0,1},{1,0},{2,3},{3,2},{4,5},{5,4},{6,7},{7,6},{8,9},{9,8},{10,11... | collective-permute-start | bytes 1769480 | tf_op jit(solution)/shard_map/ppermute | solution.py:325
  354.1 13.2 %collective-permute-start.61 = (bf16[144,1792]{1,0:T(8,128)(2,1)S(1)}, bf16[144,1792]{1,0:T(8,128)(2,1)S(1)}, u32[]{:S(2)}, u32[]{:S(2)}) collective-permute-start(bf16[144,1792]{1,0:T(8,128)(2,1)S(1)} %add_convert_fusion.18), channel_id=1, source_target_pairs={{0,8},{2,6},{8,16},{10,2},{16,24},{18,10},{24,28},{26,18},{28,20},... | collective-permute-start | bytes 1548296 | tf_op jit(solution)/shard_map/ppermute | solution.py:376
  354.8 14.0 %collective-permute-start.60 = (bf16[144,1792]{1,0:T(8,128)(2,1)}, bf16[144,1792]{1,0:T(8,128)(2,1)S(1)}, u32[]{:S(2)}, u32[]{:S(2)}) collective-permute-start(bf16[144,1792]{1,0:T(8,128)(2,1)} %add_convert_fusion.19), channel_id=1, source_target_pairs={{0,8},{2,6},{8,16},{10,2},{16,24},{18,10},{24,28},{26,18},{28,20},... | collective-permute-start | bytes 1548296 | tf_op jit(solution)/shard_map/ppermute | solution.py:376
  355.4 21.9 %collective-permute-start.50 = (bf16[256,1152]{1,0:T(8,128)(2,1)S(1)}, bf16[256,1152]{1,0:T(8,128)(2,1)S(1)}, u32[]{:S(2)}, u32[]{:S(2)}) collective-permute-start(bf16[256,1152]{1,0:T(8,128)(2,1)S(1)} %get-tuple-element.194.refs_0_.refs_5_), channel_id=1, source_target_pairs={{0,2},{2,0},{1,3},{3,1},{4,6},{6,4},{5,7},{7,5},{8,10},{10,8},{9,1... | collective-permute-start | bytes 1769480 | tf_op jit(solution)/shard_map/ppermute | solution.py:325
  355.4 18.9 %collective-permute-start.59 = (bf16[144,1792]{1,0:T(8,128)(2,1)S(1)}, bf16[144,1792]{1,0:T(8,128)(2,1)S(1)}, u32[]{:S(2)}, u32[]{:S(2)}) collective-permute-start(bf16[144,1792]{1,0:T(8,128)(2,1)S(1)} %get-tuple-element.212), channel_id=1, source_target_pairs={{0,8},{2,6},{8,16},{10,2},{16,24},{18,10},{24,28},{26,18},{28,20},... | collective-permute-start | bytes 1548296 | tf_op jit(solution)/shard_map/ppermute | solution.py:376
  375.2 23.0 %collective-permute-start.64 = (bf16[144,1792]{1,0:T(8,128)(2,1)}, bf16[144,1792]{1,0:T(8,128)(2,1)}, u32[]{:S(2)}, u32[]{:S(2)}) collective-permute-start(bf16[144,1792]{1,0:T(8,128)(2,1)} %add_convert_fusion.15), channel_id=1, source_target_pairs={{0,8},{2,6},{8,16},{10,2},{16,24},{18,10},{24,28},{26,18},{28,20},... | collective-permute-start | bytes 1548296 | tf_op jit(solution)/shard_map/ppermute | solution.py:376
  375.8 24.6 %collective-permute-start.63 = (bf16[144,1792]{1,0:T(8,128)(2,1)}, bf16[144,1792]{1,0:T(8,128)(2,1)}, u32[]{:S(2)}, u32[]{:S(2)}) collective-permute-start(bf16[144,1792]{1,0:T(8,128)(2,1)} %add_convert_fusion.16), channel_id=1, source_target_pairs={{0,8},{2,6},{8,16},{10,2},{16,24},{18,10},{24,28},{26,18},{28,20},... | collective-permute-start | bytes 1548296 | tf_op jit(solution)/shard_map/ppermute | solution.py:376
  376.5 25.2 %collective-permute-start.62 = (bf16[144,1792]{1,0:T(8,128)(2,1)}, bf16[144,1792]{1,0:T(8,128)(2,1)}, u32[]{:S(2)}, u32[]{:S(2)}) collective-permute-start(bf16[144,1792]{1,0:T(8,128)(2,1)} %add_convert_fusion.17), channel_id=1, source_target_pairs={{0,8},{2,6},{8,16},{10,2},{16,24},{18,10},{24,28},{26,18},{28,20},... | collective-permute-start | bytes 1548296 | tf_op jit(solution)/shard_map/ppermute | solution.py:376
  388.8 18.4 %collective-permute-start.53 = (bf16[256,1152]{1,0:T(8,128)(2,1)S(1)}, bf16[256,1152]{1,0:T(8,128)(2,1)S(1)}, u32[]{:S(2)}, u32[]{:S(2)}) collective-permute-start(bf16[256,1152]{1,0:T(8,128)(2,1)S(1)} %get-tuple-element.201), channel_id=1, source_target_pairs={{0,2},{2,0},{1,3},{3,1},{4,6},{6,4},{5,7},{7,5},{8,10},{10,8},{9,1... | collective-permute-start | bytes 1769480 | tf_op jit(solution)/shard_map/ppermute | solution.py:325
  388.9 51.6 %collective-permute-start.55 = (bf16[256,1152]{1,0:T(8,128)(2,1)}, bf16[256,1152]{1,0:T(8,128)(2,1)S(1)}, u32[]{:S(2)}, u32[]{:S(2)}) collective-permute-start(bf16[256,1152]{1,0:T(8,128)(2,1)} %get-tuple-element.203), channel_id=1, source_target_pairs={{0,2},{2,0},{1,3},{3,1},{4,6},{6,4},{5,7},{7,5},{8,10},{10,8},{9,1... | collective-permute-start | bytes 1769480 | tf_op jit(solution)/shard_map/ppermute | solution.py:325
  404.7 12.9 %collective-permute-start.66 = (bf16[144,1792]{1,0:T(8,128)(2,1)S(1)}, bf16[144,1792]{1,0:T(8,128)(2,1)S(1)}, u32[]{:S(2)}, u32[]{:S(2)}) collective-permute-start(bf16[144,1792]{1,0:T(8,128)(2,1)S(1)} %add_convert_fusion.13), channel_id=1, source_target_pairs={{0,8},{2,6},{8,16},{10,2},{16,24},{18,10},{24,28},{26,18},{28,20},... | collective-permute-start | bytes 1548296 | tf_op jit(solution)/shard_map/ppermute | solution.py:376
  405.3 17.8 %collective-permute-start.65 = (bf16[144,1792]{1,0:T(8,128)(2,1)S(1)}, bf16[144,1792]{1,0:T(8,128)(2,1)S(1)}, u32[]{:S(2)}, u32[]{:S(2)}) collective-permute-start(bf16[144,1792]{1,0:T(8,128)(2,1)S(1)} %add_convert_fusion.14), channel_id=1, source_target_pairs={{0,8},{2,6},{8,16},{10,2},{16,24},{18,10},{24,28},{26,18},{28,20},... | collective-permute-start | bytes 1548296 | tf_op jit(solution)/shard_map/ppermute | solution.py:376
  408.2 32.3 %collective-permute-start.54 = (bf16[256,1152]{1,0:T(8,128)(2,1)}, bf16[256,1152]{1,0:T(8,128)(2,1)S(1)}, u32[]{:S(2)}, u32[]{:S(2)}) collective-permute-start(bf16[256,1152]{1,0:T(8,128)(2,1)} %add_convert_fusion), channel_id=1, source_target_pairs={{0,1},{1,0},{2,3},{3,2},{4,5},{5,4},{6,7},{7,6},{8,9},{9,8},{10,11... | collective-permute-start | bytes 1769480 | tf_op jit(solution)/shard_map/ppermute | solution.py:325
  424.0 12.9 %collective-permute-start.68 = (bf16[144,1024]{1,0:T(8,128)(2,1)}, bf16[144,1024]{1,0:T(8,128)(2,1)}, u32[]{:S(2)}, u32[]{:S(2)}) collective-permute-start(bf16[144,1024]{1,0:T(8,128)(2,1)} %add_convert_fusion.27), channel_id=1, source_target_pairs={{0,8},{2,6},{8,16},{10,2},{16,24},{18,10},{24,28},{26,18},{28,20},... | collective-permute-start | bytes 884744 | tf_op jit(solution)/shard_map/ppermute | solution.py:376
  425.7 17.4 %collective-permute-start.70 = (bf16[144,1792]{1,0:T(8,128)(2,1)}, bf16[144,1792]{1,0:T(8,128)(2,1)}, u32[]{:S(2)}, u32[]{:S(2)}) collective-permute-start(bf16[144,1792]{1,0:T(8,128)(2,1)} %add_convert_fusion.10), channel_id=1, source_target_pairs={{0,8},{2,6},{8,16},{10,2},{16,24},{18,10},{24,28},{26,18},{28,20},... | collective-permute-start | bytes 1548296 | tf_op jit(solution)/shard_map/ppermute | solution.py:376
  435.6 16.5 %collective-permute-start.69 = (bf16[144,1792]{1,0:T(8,128)(2,1)}, bf16[144,1792]{1,0:T(8,128)(2,1)}, u32[]{:S(2)}, u32[]{:S(2)}) collective-permute-start(bf16[144,1792]{1,0:T(8,128)(2,1)} %add_convert_fusion.11), channel_id=1, source_target_pairs={{0,8},{2,6},{8,16},{10,2},{16,24},{18,10},{24,28},{26,18},{28,20},... | collective-permute-start | bytes 1548296 | tf_op jit(solution)/shard_map/ppermute | solution.py:376
  436.9 13.9 %collective-permute-start.71 = (bf16[144,1792]{1,0:T(8,128)(2,1)}, bf16[144,1792]{1,0:T(8,128)(2,1)}, u32[]{:S(2)}, u32[]{:S(2)}) collective-permute-start(bf16[144,1792]{1,0:T(8,128)(2,1)} %add_convert_fusion.9), channel_id=1, source_target_pairs={{0,8},{2,6},{8,16},{10,2},{16,24},{18,10},{24,28},{26,18},{28,20},... | collective-permute-start | bytes 1548296 | tf_op jit(solution)/shard_map/ppermute | solution.py:376
  454.7 11.2 %collective-permute-start.74 = (bf16[144,1792]{1,0:T(8,128)(2,1)S(1)}, bf16[144,1792]{1,0:T(8,128)(2,1)S(1)}, u32[]{:S(2)}, u32[]{:S(2)}) collective-permute-start(bf16[144,1792]{1,0:T(8,128)(2,1)S(1)} %add_convert_fusion.7), channel_id=1, source_target_pairs={{0,8},{2,6},{8,16},{10,2},{16,24},{18,10},{24,28},{26,18},{28,20},... | collective-permute-start | bytes 1548296 | tf_op jit(solution)/shard_map/ppermute | solution.py:376
  473.3 14.6 %collective-permute-start.78 = (bf16[144,1792]{1,0:T(8,128)(2,1)}, bf16[144,1792]{1,0:T(8,128)(2,1)}, u32[]{:S(2)}, u32[]{:S(2)}) collective-permute-start(bf16[144,1792]{1,0:T(8,128)(2,1)} %add_convert_fusion.6), channel_id=1, source_target_pairs={{0,8},{2,6},{8,16},{10,2},{16,24},{18,10},{24,28},{26,18},{28,20},... | collective-permute-start | bytes 1548296 | tf_op jit(solution)/shard_map/ppermute | solution.py:376
  475.1 31.5 %all-to-all-start.4 = ((bf16[8,32,1152]{2,1,0:T(8,128)(2,1)}), bf16[8,32,1152]{2,1,0:T(8,128)(2,1)}, u32[]{:S(2)}, u32[]{:S(2)}) async-start(bf16[8,32,1152]{2,1,0:T(8,128)(2,1)} %bitcast.82), calls=%async_computation.4 | async-start | bytes 1179648 | tf_op jit(solution)/shard_map/all_to_all | solution.py:476
  479.3 19.0 %collective-permute-start.79 = (bf16[144,1792]{1,0:T(8,128)(2,1)}, bf16[144,1792]{1,0:T(8,128)(2,1)S(1)}, u32[]{:S(2)}, u32[]{:S(2)}) collective-permute-start(bf16[144,1792]{1,0:T(8,128)(2,1)} %add_convert_fusion.5), channel_id=1, source_target_pairs={{0,8},{2,6},{8,16},{10,2},{16,24},{18,10},{24,28},{26,18},{28,20},... | collective-permute-start | bytes 1548296 | tf_op jit(solution)/shard_map/ppermute | solution.py:376
  (144 other events, 2116.9 us)

commit v4 on v3

--- a/solution.py
+++ b/solution.py
@@ -387,13 +387,14 @@
 class RingSum:
     def __init__(self, blocks):
         self.blocks, self.hops = blocks, 0
-        self.sum = blocks[0]
+        self.sum = self.before = blocks[0]
 
     def left(self):
         return len(self.blocks) - 1 - self.hops
 
     def step(self):
         self.hops += 1
+        self.before = self.sum
         total = hop(self.sum).astype(F32) + self.blocks[self.hops].astype(F32)
         self.sum = total if self.left() == 0 else total.astype(BF16)
 
@@ -402,14 +403,13 @@
 
 
 def meet(rings, *others):
-    values = [ring.sum for ring in rings]
     for ring in rings:
-        ring.wait(*values, *others)
+        ring.wait(*(r.before for r in rings if r is not ring), *(others if ring is rings[0] else ()))
 
 
 def exchanges():
     hops = []
-    for axis in ("core", "tensor", "seq"):
+    for axis in ("core", "tensor"):
         distance = 1
         while distance < lax.axis_size(axis):
             hops.append((axis, distance))
@@ -651,8 +651,8 @@
     smalls.step()
     meet(rings, *sent)
     smalls.wait(ups.sum)
+    stage()
     smalls.step()
-    stage()
     input_grad, gain_in = small_call(
         functools.partial(last_kernel, len(shares)),
         [block, vector],
@@ -663,20 +663,16 @@
     rings.append(smalls)
     meet(rings, input_grad, packed)
     input_grad = from_rows(input_grad)
-    for way in [e for e in exchanges() if e[0] != "seq"]:
+    for way in exchanges():
         packed = exchange(packed, *way)
-    far = [e for e in exchanges() if e[0] == "seq"]
+    packed = lax.all_to_all(
+        packed.reshape(seqs, cores, -1), "seq", split_axis=0, concat_axis=0, tiled=True
+    ).sum(axis=0)
     while ups.left():
         stage()
-        meet(rings, packed)
-    (packed,) = together([packed], ups.sum)
-    while smalls.left() or far:
-        if smalls.left():
-            smalls.step()
-        if far:
-            packed = exchange(packed, *far.pop(0))
-        smalls.wait(packed)
-        (packed,) = together([packed], smalls.sum)
+        meet(rings, *([packed] if ups.left() == 1 else []))
+    while smalls.left():
+        smalls.step()
     down_sum, small_sum = downs.sum, smalls.sum
     gate_sum, up_sum = gates.sum, ups.sum
 
@@ -701,7 +697,7 @@
     kv_sum = sum_tensor(sum_core(small_sum[:, HD : 3 * HD]))
     own_columns = to_owner if split_heads else sum_core
     q_grad, out_grad_w = own_columns(small_sum[:, :HD]), own_columns(small_sum[:, 3 * HD :])
-    mine = pick(packed, s_index * cores + c_index, 0)
+    mine = pick(packed, c_index, 0)
     gain_out = tuple(mine[end - n : end] for end, n in zip(gain_ends, gain_sizes))
     return (
         output,

time: 561 us -> 548 us (0.977)
  waiting for transfers between devices: 171 us -> 134 us
  local copies, waits for them, and re-layouts: 108 us -> 123 us
  other arithmetic: 53.9 us -> 59.8 us
    ppermute x56, waiting for transfers between devices: 117 us -> 96 us  [hop(): return lax.ppermute(values, ('seq', 'core'), pairs)]
    unnamed x222 -> x238, local copies, waits for them, and re-layouts: 27.3 us -> 42.2 us
    ppermute x33, waiting for transfers between devices: 28.2 us -> 18.7 us  [shift(): lax.ppermute(values, axis, [(i, (i + step) % size) for i in range(size)])]
    ppermute x5 -> x2, waiting for transfers between devices: 7.91 us -> 0.01 us  [exchange(): lax.ppermute(values, axis, [(i, i ^ distance) for i in range(lax.axis_siz...]
    ppermute x56, starting transfers between devices: 68.8 us -> 74.6 us  [hop(): return lax.ppermute(values, ('seq', 'core'), pairs)]
  transfers between devices with their start and end apart: 99 -> 97, of which waited for: 46 -> 36; matrix products, arithmetic and copies ran while one was open for 23% -> 25% of each run, Pallas kernels for 15% -> 15%
where the time goes in v4:
time: 548 us; the launch traced here: 538 us
  waiting for transfers between devices  134 us (24%)
  local copies, waits for them, and re-layouts  123 us (22%)
  starting transfers between devices  119 us (22%)
  Pallas kernels  100 us (18%)
  other arithmetic  59.8 us (11%)
    pallas_call x14, Pallas kernels, call(): pl.pallas_call(kernel, out_shape=outs, scratch_shapes=list(scratch), comp...  100 us
    ppermute x56, waiting for transfers between devices, hop(): return lax.ppermute(values, ('seq', 'core'), pairs)  96 us
    ppermute x56, starting transfers between devices, hop(): return lax.ppermute(values, ('seq', 'core'), pairs)  74.6 us
    dynamic_update_slice x39, local copies, waits for them, and re-layouts, put(): lax.dynamic_update_slice(full, block[None], (spot, row, 0), allow_negativ...  53.3 us
    unnamed x238, local copies, waits for them, and re-layouts  42.2 us
    convert_element_type x24, other arithmetic, step(): self.sum = total if self.left() == 0 else total.astype(BF16)  27.7 us
    ppermute x33, waiting for transfers between devices, shift(): lax.ppermute(values, axis, [(i, (i + step) % size) for i in range(size)])  18.7 us
    ppermute x33, starting transfers between devices, shift(): lax.ppermute(values, axis, [(i, (i + step) % size) for i in range(size)])  16.1 us
  transfers between devices with their start and end apart: 97, of which 36 were waited for; matrix products, arithmetic and copies ran while one was open for 25% of the time, Pallas kernels for 15%

profile of v4, /device:TPU:0, one launch (start us, length us, event | category | flops | bytes accessed | tf_op | source)
XLA Modules:
  0.0 537.8 jit_solution(16338399608531233957)
XLA Ops:
  3.2 3.1 collective-permute-start
  13.8 3.7 all-to-all-start.1
  20.0 4.8 all-to-all-start
  37.7 3.0 collective-permute-done.1
  44.2 3.5 collective-permute-done.2
  50.4 3.8 collective-permute-done.3
  56.6 3.8 collective-permute-done.4
  62.8 3.8 collective-permute-done.5
  69.0 3.8 collective-permute-done.6
  82.3 2.7 broadcast.201.clone
  85.0 2.5 bitcast_dynamic-update-slice_fusion.23
  90.8 2.5 bitcast_dynamic-update-slice_fusion.22
  94.8 2.6 bitcast_dynamic-update-slice_fusion.6
  97.4 2.4 collective-permute-start.33
  99.8 2.5 bitcast_dynamic-update-slice_fusion.14
  106.9 2.4 collective-permute-done.33
  111.3 3.6 collective-permute-done.26
  115.3 2.5 bitcast_dynamic-update-slice_fusion.13
  117.8 2.6 collective-permute-done.20
  120.8 2.5 bitcast_dynamic-update-slice_fusion.20
  123.3 4.3 maximum_select_fusion
  130.1 2.6 collective-permute-start.27
  134.5 10.8 %shard_map.290 = (bf16[1024,256]{1,0:T(8,128)(2,1)S(1)}, bf16[1024,1024]{1,0:T(8,128)(2,1)}, bf16[1024,512]{1,0:T(8,128)(2,1)}, bf16[1024,256]{1,0:T(8,128)(2,1)...) custom-call(bf16[256,1152]{1,0:T(8,128)(2,1)} %copy-done.9, ...), custom_call_target="tpu_custom_call" | custom-call | bytes 1 | tf_op jit(solution)/shard_map/pallas_call | solution.py:66
  148.1 2.5 bitcast_dynamic-update-slice_fusion.19
  157.4 4.2 collective-permute-done.28
  164.8 2.3 collective-permute-done.35
  180.2 3.4 collective-permute-done.23
  186.6 2.5 collective-permute-done.30
  191.3 3.4 collective-permute-done.37
  197.2 3.0 collective-permute-done.24
  201.7 4.0 collective-permute-done.31
  206.4 14.5 %shard_map.292 = (bf16[1024,1792]{1,0:T(8,128)(2,1)S(1)}, bf16[1024,1792]{1,0:T(8,128)(2,1)S(1)}, bf16[1024,1792]{1,0:T(8,128)(2,1)S(1)}) custom-call(bf16[256,1152]{1,0:T(8,128)(2,1)S(1)} %get-tuple-element.144.refs_0_, bf16[256,1152]{1,0:T(8,128)(2,1)S(1)} %collective-permute-done.15.refs_1_, bf16[256,1152]{1,0:T(8,128)(2,1)S(1)} %collective-permute-done.16.refs_2_, ...), custom_call_target="tpu_custom_call" | custom-call | bytes 1 | tf_op jit(solution)/shard_map/pallas_call | solution.py:66
  225.4 5.9 %shard_map.293 = (bf16[256,1152]{1,0:T(8,128)(2,1)S(1)}, bf16[256,1152]{1,0:T(8,128)(2,1)S(1)}, bf16[256,1152]{1,0:T(8,128)(2,1)S(1)}, bf16[256,1152]{1,0:T(8,128)(2,1)}) custom-call(bf16[1024,1792]{1,0:T(8,128)(2,1)S(1)} %get-tuple-element.161.hid_ref.refs_4_, bf16[1152,1792]{1,0:T(8,128)(2,1)S(1)} %bitcast.198), custom_call_target="tpu_custom_call" | custom-call | bytes 1 | tf_op jit(solution)/shard_map/pallas_call | solution.py:66
  233.0 4.8 all-to-all-start.2
  244.3 10.1 %all-to-all-done.2 = bf16[8,32,1152]{2,1,0:T(8,128)(2,1)S(1)} async-done(((bf16[8,32,1152]{2,1,0:T(8,128)(2,1)}), bf16[8,32,1152]{2,1,0:T(8,128)(2,1)S(1)}, u32[]{:S(2)}, u32[]{:S(2)}) %all-to-all-start.2) | async-done | bytes 589856 | tf_op jit(solution)/shard_map/all_to_all | solution.py:472
  258.8 2.8 shard_map.294
  263.7 6.0 %all-to-all-start.3 = ((bf16[8,32,1152]{2,1,0:T(8,128)(2,1)}), bf16[8,32,1152]{2,1,0:T(8,128)(2,1)S(1)}, u32[]{:S(2)}, u32[]{:S(2)}) async-start(bf16[8,32,1152]{2,1,0:T(8,128)(2,1)} %bitcast.79), calls=%async_computation.3 | async-start | bytes 1179648 | tf_op jit(solution)/shard_map/all_to_all | solution.py:476
  269.7 7.5 %collective-permute-done.43.refs_2_ = bf16[256,1152]{1,0:T(8,128)(2,1)} collective-permute-done((bf16[256,1152]{1,0:T(8,128)(2,1)}, bf16[256,1152]{1,0:T(8,128)(2,1)}, u32[]{:S(2)}, u32[]{:S(2)}) %collective-permute-start.43) | collective-permute-done | bytes 589856 | tf_op jit(solution)/shard_map/ppermute | solution.py:325
  277.2 8.0 %all-to-all-done.3 = bf16[8,32,1152]{2,1,0:T(8,128)(2,1)S(1)} async-done(((bf16[8,32,1152]{2,1,0:T(8,128)(2,1)}), bf16[8,32,1152]{2,1,0:T(8,128)(2,1)S(1)}, u32[]{:S(2)}, u32[]{:S(2)}) %all-to-all-start.3) | async-done | bytes 589856 | tf_op jit(solution)/shard_map/all_to_all | solution.py:476
  285.3 2.3 copy-done.8
  288.5 9.0 %shard_map.295 = (bf16[144,1792]{1,0:T(8,128)(2,1)S(1)}, bf16[144,1792]{1,0:T(8,128)(2,1)S(1)}, bf16[144,1792]{1,0:T(8,128)(2,1)S(1)}, bf16[144,1792]{1,0:T(8,12...) custom-call(s32[8]{0:T(128)S(1)} %copy-done.93, ...), custom_call_target="tpu_custom_call" | custom-call | bytes 1 | tf_op jit(solution)/shard_map/pallas_call | solution.py:66
  306.1 19.0 %shard_map.296 = (bf16[1024,1792]{1,0:T(8,128)(2,1)S(1)}, bf16[1024,1792]{1,0:T(8,128)(2,1)S(1)}, bf16[256,1152]{1,0:T(8,128)(2,1)S(1)}, bf16[256,1152]{1,0:T(8,...) custom-call(bf16[256,1152]{1,0:T(8,128)(2,1)} %get-tuple-element.163.refs_0_, ...), custom_call_target="tpu_custom_call" | custom-call | bytes 1 | tf_op jit(solution)/shard_map/pallas_call | solution.py:66
  326.4 7.9 %shard_map.297 = (bf16[144,1792]{1,0:T(8,128)(2,1)S(1)}, bf16[144,1792]{1,0:T(8,128)(2,1)S(1)}, bf16[144,1792]{1,0:T(8,128)(2,1)S(1)}, bf16[144,1792]{1,0:T(8,12...) custom-call(s32[8]{0:T(128)S(1)} %copy-done.94, ...), custom_call_target="tpu_custom_call" | custom-call | bytes 1 | tf_op jit(solution)/shard_map/pallas_call | solution.py:66
  340.3 7.9 %shard_map.298 = (bf16[144,1792]{1,0:T(8,128)(2,1)S(1)}, bf16[144,1792]{1,0:T(8,128)(2,1)S(1)}, bf16[144,1792]{1,0:T(8,128)(2,1)S(1)}, bf16[144,1792]{1,0:T(8,12...) custom-call(s32[8]{0:T(128)S(1)} %copy-done.94, ...), custom_call_target="tpu_custom_call" | custom-call | bytes 1 | tf_op jit(solution)/shard_map/pallas_call | solution.py:66
  358.9 2.9 shard_map.299
  367.2 2.3 collective-permute-start.62
  373.8 3.6 collective-permute-done.51.refs_2_.refs_7_
  379.6 2.3 collective-permute-done.64
  382.8 2.4 collective-permute-start.67
  389.3 11.4 %shard_map.300 = (bf16[1024,768]{1,0:T(8,128)(2,1)}, f32[1,256]{1,0:T(1,128)S(1)}, f32[1,256]{1,0:T(1,128)S(1)}, bf16[256,1152]{1,0:T(8,128)(2,1)S(1)}, bf16[256...) custom-call(bf16[256,1152]{1,0:T(8,128)(2,1)S(1)} %get-tuple-element.187.refs_0_.refs_5_, ...), custom_call_target="tpu_custom_call" | custom-call | bytes 1 | tf_op jit(solution)/shard_map/pallas_call | solution.py:66
  407.4 5.6 %shard_map.302 = (bf16[144,1024]{1,0:T(8,128)(2,1)}, bf16[144,1024]{1,0:T(8,128)(2,1)S(1)}, bf16[144,1024]{1,0:T(8,128)(2,1)S(1)}, bf16[144,1024]{1,0:T(8,128)(2...) custom-call(s32[8]{0:T(128)S(1)} %copy-done.95, ...), custom_call_target="tpu_custom_call" | custom-call | bytes 1 | tf_op jit(solution)/shard_map/pallas_call | solution.py:66
  434.4 3.1 collective-permute-done.71
  439.9 6.3 %collective-permute-done.66 = bf16[144,1024]{1,0:T(8,128)(2,1)S(1)} collective-permute-done((bf16[144,1024]{1,0:T(8,128)(2,1)S(1)}, bf16[144,1024]{1,0:T(8,128)(2,1)S(1)}, u32[]{:S(2)}, u32[]{:S(2)}) %collective-permute-start.66) | collective-permute-done | bytes 294944 | tf_op jit(solution)/shard_map/ppermute | solution.py:376
  454.0 6.5 %collective-permute-done.69 = bf16[144,1024]{1,0:T(8,128)(2,1)} collective-permute-done((bf16[144,1024]{1,0:T(8,128)(2,1)}, bf16[144,1024]{1,0:T(8,128)(2,1)}, u32[]{:S(2)}, u32[]{:S(2)}) %collective-permute-start.69) | collective-permute-done | bytes 294944 | tf_op jit(solution)/shard_map/ppermute | solution.py:376
  465.2 3.6 all-to-all-start.5
  476.2 4.3 all-to-all-start.4
  487.6 12.6 %collective-permute-done.75 = bf16[144,1024]{1,0:T(8,128)(2,1)S(1)} collective-permute-done((bf16[144,1024]{1,0:T(8,128)(2,1)S(1)}, bf16[144,1024]{1,0:T(8,128)(2,1)S(1)}, u32[]{:S(2)}, u32[]{:S(2)}) %collective-permute-start.75) | collective-permute-done | bytes 294944 | tf_op jit(solution)/shard_map/ppermute | solution.py:376
  501.2 4.6 collective-permute-start.87
  505.8 2.5 collective-permute-start.79
  509.9 5.9 %collective-permute-done.79 = bf16[144,1024]{1,0:T(8,128)(2,1)} collective-permute-done((bf16[144,1024]{1,0:T(8,128)(2,1)S(1)}, bf16[144,1024]{1,0:T(8,128)(2,1)}, u32[]{:S(2)}, u32[]{:S(2)}) %collective-permute-start.79) | collective-permute-done | bytes 294944 | tf_op jit(solution)/shard_map/ppermute | solution.py:376
  516.8 2.6 collective-permute-start.80
  519.4 2.5 maximum_select_fusion.3
  522.0 2.5 maximum_select_fusion.1
  529.9 4.0 collective-permute-done.83
  (552 shorter events, 232.6 us)
Async XLA Ops:
  3.2 30.4 %collective-permute-start = (bf16[80,1536]{1,0:T(8,128)(2,1)S(1)}, bf16[80,1536]{1,0:T(8,128)(2,1)S(1)}, u32[]{:S(2)}, u32[]{:S(2)}) collective-permute-start(bf16[80,1536]{1,0:T(8,128)(2,1)S(1)} %pad_maximum_fusion.2), channel_id=1, source_target_pairs={{0,8},{2,6},{8,16},{10,2},{16,24},{18,10},{24,28},{26,18},{28,20},... | collective-permute-start | bytes 737288 | tf_op jit(solution)/shard_map/ppermute | solution.py:376
  20.0 34.3 %all-to-all-start = ((bf16[8,32,1152]{2,1,0:T(8,128)(2,1)}), bf16[8,32,1152]{2,1,0:T(8,128)(2,1)S(1)}, u32[]{:S(2)}, u32[]{:S(2)}) async-start(bf16[8,32,1152]{2,1,0:T(8,128)(2,1)} %bitcast), calls=%async_computation | async-start | bytes 1179648 | tf_op jit(solution)/shard_map/all_to_all | solution.py:472
  74.2 49.2 %collective-permute-start.11 = (bf16[8,80,1536]{2,1,0:T(8,128)(2,1)}, bf16[8,80,1536]{2,1,0:T(8,128)(2,1)}, u32[]{:S(2)}, u32[]{:S(2)}) collective-permute-start(bf16[8,80,1536]{2,1,0:T(8,128)(2,1)} %bitcast_dynamic-update-slice_fusion.24), channel_id=1, source_target_pairs={{0,2},{2,0},{1,3},{3,1},{4,6},{6,4},{5,7},{7,5},{8,10},{10,8},{9,1... | collective-permute-start | bytes 5898248 | tf_op jit(solution)/shard_map/ppermute | solution.py:325
  74.2 23.2 %collective-permute-start.25 = (bf16[144,1792]{1,0:T(8,128)(2,1)S(1)}, bf16[144,1792]{1,0:T(8,128)(2,1)}, u32[]{:S(2)}, u32[]{:S(2)}) collective-permute-start(bf16[144,1792]{1,0:T(8,128)(2,1)S(1)} %get-tuple-element.148), channel_id=1, source_target_pairs={{0,8},{2,6},{8,16},{10,2},{16,24},{18,10},{24,28},{26,18},{28,20},... | collective-permute-start | bytes 1548296 | tf_op jit(solution)/shard_map/ppermute | solution.py:376
  75.2 12.3 %collective-permute-start.7 = (bf16[8,8,512]{2,1,0:T(8,128)(2,1)S(1)}, bf16[8,8,512]{2,1,0:T(8,128)(2,1)S(1)}, u32[]{:S(2)}, u32[]{:S(2)}) collective-permute-start(bf16[8,8,512]{2,1,0:T(8,128)(2,1)S(1)} %constant_dynamic-update-slice_fusion), channel_id=1, source_target_pairs={{0,2},{2,0},{1,3},{3,1},{4,6},{6,4},{5,7},{7,5},{8,10},{10,8},{9,1... | collective-permute-start | bytes 196616 | tf_op jit(solution)/shard_map/ppermute | solution.py:325
  77.1 13.6 %collective-permute-start.18 = (bf16[144,1792]{1,0:T(8,128)(2,1)}, bf16[144,1792]{1,0:T(8,128)(2,1)}, u32[]{:S(2)}, u32[]{:S(2)}) collective-permute-start(bf16[144,1792]{1,0:T(8,128)(2,1)} %get-tuple-element.145), channel_id=1, source_target_pairs={{0,8},{2,6},{8,16},{10,2},{16,24},{18,10},{24,28},{26,18},{28,20},... | collective-permute-start | bytes 1548296 | tf_op jit(solution)/shard_map/ppermute | solution.py:376
  77.8 16.6 %collective-permute-start.32 = (bf16[144,1792]{1,0:T(8,128)(2,1)}, bf16[144,1792]{1,0:T(8,128)(2,1)}, u32[]{:S(2)}, u32[]{:S(2)}) collective-permute-start(bf16[144,1792]{1,0:T(8,128)(2,1)} %get-tuple-element.151), channel_id=1, source_target_pairs={{0,8},{2,6},{8,16},{10,2},{16,24},{18,10},{24,28},{26,18},{28,20},... | collective-permute-start | bytes 1548296 | tf_op jit(solution)/shard_map/ppermute | solution.py:376
  88.7 15.0 %collective-permute-start.9 = (bf16[256,1152]{1,0:T(8,128)(2,1)S(1)}, bf16[256,1152]{1,0:T(8,128)(2,1)S(1)}, u32[]{:S(2)}, u32[]{:S(2)}) collective-permute-start(bf16[256,1152]{1,0:T(8,128)(2,1)S(1)} %shard_map.289.refs_0_), channel_id=1, source_target_pairs={{0,1},{1,0},{2,3},{3,2},{4,5},{5,4},{6,7},{7,6},{8,9},{9,8},{10,11... | collective-permute-start | bytes 1769480 | tf_op jit(solution)/shard_map/ppermute | solution.py:325
  90.7 42.8 %collective-permute-start.8 = (bf16[256,1152]{1,0:T(8,128)(2,1)S(1)}, bf16[256,1152]{1,0:T(8,128)(2,1)S(1)}, u32[]{:S(2)}, u32[]{:S(2)}) collective-permute-start(bf16[256,1152]{1,0:T(8,128)(2,1)S(1)} %shard_map.289.refs_0_), channel_id=1, source_target_pairs={{0,2},{2,0},{1,3},{3,1},{4,6},{6,4},{5,7},{7,5},{8,10},{10,8},{9,1... | collective-permute-start | bytes 1769480 | tf_op jit(solution)/shard_map/ppermute | solution.py:325
  97.4 11.9 %collective-permute-start.33 = (bf16[144,1792]{1,0:T(8,128)(2,1)}, bf16[144,1792]{1,0:T(8,128)(2,1)S(1)}, u32[]{:S(2)}, u32[]{:S(2)}) collective-permute-start(bf16[144,1792]{1,0:T(8,128)(2,1)} %collective-permute-done.32), channel_id=1, source_target_pairs={{0,8},{2,6},{8,16},{10,2},{16,24},{18,10},{24,28},{26,18},{28,20},... | collective-permute-start | bytes 1548296 | tf_op jit(solution)/shard_map/ppermute | solution.py:376
  103.7 11.2 %collective-permute-start.26 = (bf16[144,1792]{1,0:T(8,128)(2,1)}, bf16[144,1792]{1,0:T(8,128)(2,1)}, u32[]{:S(2)}, u32[]{:S(2)}) collective-permute-start(bf16[144,1792]{1,0:T(8,128)(2,1)} %collective-permute-done.25), channel_id=1, source_target_pairs={{0,8},{2,6},{8,16},{10,2},{16,24},{18,10},{24,28},{26,18},{28,20},... | collective-permute-start | bytes 1548296 | tf_op jit(solution)/shard_map/ppermute | solution.py:376
  105.4 28.1 %collective-permute-start.10 = (bf16[256,1152]{1,0:T(8,128)(2,1)S(1)}, bf16[256,1152]{1,0:T(8,128)(2,1)S(1)}, u32[]{:S(2)}, u32[]{:S(2)}) collective-permute-start(bf16[256,1152]{1,0:T(8,128)(2,1)S(1)} %collective-permute-done.9.refs_2_), channel_id=1, source_target_pairs={{0,2},{2,0},{1,3},{3,1},{4,6},{6,4},{5,7},{7,5},{8,10},{10,8},{9,1... | collective-permute-start | bytes 1769480 | tf_op jit(solution)/shard_map/ppermute | solution.py:325
  114.9 17.9 %collective-permute-start.34 = (bf16[144,1792]{1,0:T(8,128)(2,1)S(1)}, bf16[144,1792]{1,0:T(8,128)(2,1)S(1)}, u32[]{:S(2)}, u32[]{:S(2)}) collective-permute-start(bf16[144,1792]{1,0:T(8,128)(2,1)S(1)} %collective-permute-done.33), channel_id=1, source_target_pairs={{0,8},{2,6},{8,16},{10,2},{16,24},{18,10},{24,28},{26,18},{28,20},... | collective-permute-start | bytes 1548296 | tf_op jit(solution)/shard_map/ppermute | solution.py:376
  120.4 26.2 %collective-permute-start.21 = (bf16[144,1792]{1,0:T(8,128)(2,1)}, bf16[144,1792]{1,0:T(8,128)(2,1)}, u32[]{:S(2)}, u32[]{:S(2)}) collective-permute-start(bf16[144,1792]{1,0:T(8,128)(2,1)} %collective-permute-done.20), channel_id=1, source_target_pairs={{0,8},{2,6},{8,16},{10,2},{16,24},{18,10},{24,28},{26,18},{28,20},... | collective-permute-start | bytes 1548296 | tf_op jit(solution)/shard_map/ppermute | solution.py:376
  130.1 20.5 %collective-permute-start.27 = (bf16[144,1792]{1,0:T(8,128)(2,1)}, bf16[144,1792]{1,0:T(8,128)(2,1)}, u32[]{:S(2)}, u32[]{:S(2)}) collective-permute-start(bf16[144,1792]{1,0:T(8,128)(2,1)} %collective-permute-done.26), channel_id=1, source_target_pairs={{0,8},{2,6},{8,16},{10,2},{16,24},{18,10},{24,28},{26,18},{28,20},... | collective-permute-start | bytes 1548296 | tf_op jit(solution)/shard_map/ppermute | solution.py:376
  146.1 24.2 %collective-permute-start.14 = (bf16[256,1152]{1,0:T(8,128)(2,1)S(1)}, bf16[256,1152]{1,0:T(8,128)(2,1)S(1)}, u32[]{:S(2)}, u32[]{:S(2)}) collective-permute-start(bf16[256,1152]{1,0:T(8,128)(2,1)S(1)} %get-tuple-element.143), channel_id=1, source_target_pairs={{0,2},{2,0},{1,3},{3,1},{4,6},{6,4},{5,7},{7,5},{8,10},{10,8},{9,1... | collective-permute-start | bytes 1769480 | tf_op jit(solution)/shard_map/ppermute | solution.py:325
  152.9 17.4 %collective-permute-start.13 = (bf16[256,1152]{1,0:T(8,128)(2,1)S(1)}, bf16[256,1152]{1,0:T(8,128)(2,1)S(1)}, u32[]{:S(2)}, u32[]{:S(2)}) collective-permute-start(bf16[256,1152]{1,0:T(8,128)(2,1)S(1)} %add_convert_fusion.3), channel_id=1, source_target_pairs={{0,1},{1,0},{2,3},{3,2},{4,5},{5,4},{6,7},{7,6},{8,9},{9,8},{10,11... | collective-permute-start | bytes 1769480 | tf_op jit(solution)/shard_map/ppermute | solution.py:325
  154.5 12.6 %collective-permute-start.35 = (bf16[144,1792]{1,0:T(8,128)(2,1)S(1)}, bf16[144,1792]{1,0:T(8,128)(2,1)}, u32[]{:S(2)}, u32[]{:S(2)}) collective-permute-start(bf16[144,1792]{1,0:T(8,128)(2,1)S(1)} %copy-done.108), channel_id=1, source_target_pairs={{0,8},{2,6},{8,16},{10,2},{16,24},{18,10},{24,28},{26,18},{28,20},... | collective-permute-start | bytes 1548296 | tf_op jit(solution)/shard_map/ppermute | solution.py:376
  161.6 11.5 %collective-permute-start.29 = (bf16[144,1792]{1,0:T(8,128)(2,1)}, bf16[144,1792]{1,0:T(8,128)(2,1)}, u32[]{:S(2)}, u32[]{:S(2)}) collective-permute-start(bf16[144,1792]{1,0:T(8,128)(2,1)} %collective-permute-done.28), channel_id=1, source_target_pairs={{0,8},{2,6},{8,16},{10,2},{16,24},{18,10},{24,28},{26,18},{28,20},... | collective-permute-start | bytes 1548296 | tf_op jit(solution)/shard_map/ppermute | solution.py:376
  171.0 15.6 %collective-permute-start.16 = (bf16[256,1152]{1,0:T(8,128)(2,1)S(1)}, bf16[256,1152]{1,0:T(8,128)(2,1)S(1)}, u32[]{:S(2)}, u32[]{:S(2)}) collective-permute-start(bf16[256,1152]{1,0:T(8,128)(2,1)S(1)} %get-tuple-element.144.refs_0_), channel_id=1, source_target_pairs={{0,1},{1,0},{2,3},{3,2},{4,5},{5,4},{6,7},{7,6},{8,9},{9,8},{10,11... | collective-permute-start | bytes 1769480 | tf_op jit(solution)/shard_map/ppermute | solution.py:325
  172.6 33.8 %collective-permute-start.15 = (bf16[256,1152]{1,0:T(8,128)(2,1)S(1)}, bf16[256,1152]{1,0:T(8,128)(2,1)S(1)}, u32[]{:S(2)}, u32[]{:S(2)}) collective-permute-start(bf16[256,1152]{1,0:T(8,128)(2,1)S(1)} %get-tuple-element.144.refs_0_), channel_id=1, source_target_pairs={{0,2},{2,0},{1,3},{3,1},{4,6},{6,4},{5,7},{7,5},{8,10},{10,8},{9,1... | collective-permute-start | bytes 1769480 | tf_op jit(solution)/shard_map/ppermute | solution.py:325
  173.0 16.1 %collective-permute-start.30 = (bf16[144,1792]{1,0:T(8,128)(2,1)}, bf16[144,1792]{1,0:T(8,128)(2,1)S(1)}, u32[]{:S(2)}, u32[]{:S(2)}) collective-permute-start(bf16[144,1792]{1,0:T(8,128)(2,1)} %collective-permute-done.29), channel_id=1, source_target_pairs={{0,8},{2,6},{8,16},{10,2},{16,24},{18,10},{24,28},{26,18},{28,20},... | collective-permute-start | bytes 1548296 | tf_op jit(solution)/shard_map/ppermute | solution.py:376
  178.1 16.6 %collective-permute-start.37 = (bf16[144,1792]{1,0:T(8,128)(2,1)S(1)}, bf16[144,1792]{1,0:T(8,128)(2,1)S(1)}, u32[]{:S(2)}, u32[]{:S(2)}) collective-permute-start(bf16[144,1792]{1,0:T(8,128)(2,1)S(1)} %collective-permute-done.36), channel_id=1, source_target_pairs={{0,8},{2,6},{8,16},{10,2},{16,24},{18,10},{24,28},{26,18},{28,20},... | collective-permute-start | bytes 1548296 | tf_op jit(solution)/shard_map/ppermute | solution.py:376
  183.6 16.6 %collective-permute-start.24 = (bf16[144,1792]{1,0:T(8,128)(2,1)S(1)}, bf16[144,1792]{1,0:T(8,128)(2,1)S(1)}, u32[]{:S(2)}, u32[]{:S(2)}) collective-permute-start(bf16[144,1792]{1,0:T(8,128)(2,1)S(1)} %collective-permute-done.23), channel_id=1, source_target_pairs={{0,8},{2,6},{8,16},{10,2},{16,24},{18,10},{24,28},{26,18},{28,20},... | collective-permute-start | bytes 1548296 | tf_op jit(solution)/shard_map/ppermute | solution.py:376
  186.6 19.9 %collective-permute-start.17 = (bf16[256,1152]{1,0:T(8,128)(2,1)S(1)}, bf16[256,1152]{1,0:T(8,128)(2,1)S(1)}, u32[]{:S(2)}, u32[]{:S(2)}) collective-permute-start(bf16[256,1152]{1,0:T(8,128)(2,1)S(1)} %collective-permute-done.16.refs_2_), channel_id=1, source_target_pairs={{0,2},{2,0},{1,3},{3,1},{4,6},{6,4},{5,7},{7,5},{8,10},{10,8},{9,1... | collective-permute-start | bytes 1769480 | tf_op jit(solution)/shard_map/ppermute | solution.py:325
  189.1 16.6 %collective-permute-start.31 = (bf16[144,1792]{1,0:T(8,128)(2,1)S(1)}, bf16[144,1792]{1,0:T(8,128)(2,1)S(1)}, u32[]{:S(2)}, u32[]{:S(2)}) collective-permute-start(bf16[144,1792]{1,0:T(8,128)(2,1)S(1)} %collective-permute-done.30), channel_id=1, source_target_pairs={{0,8},{2,6},{8,16},{10,2},{16,24},{18,10},{24,28},{26,18},{28,20},... | collective-permute-start | bytes 1548296 | tf_op jit(solution)/shard_map/ppermute | solution.py:376
  194.6 30.0 %collective-permute-start.38 = (bf16[144,1792]{1,0:T(8,128)(2,1)S(1)}, bf16[144,1792]{1,0:T(8,128)(2,1)S(1)}, u32[]{:S(2)}, u32[]{:S(2)}) collective-permute-start(bf16[144,1792]{1,0:T(8,128)(2,1)S(1)} %collective-permute-done.37), channel_id=1, source_target_pairs={{0,8},{2,6},{8,16},{10,2},{16,24},{18,10},{24,28},{26,18},{28,20},... | collective-permute-start | bytes 1548296 | tf_op jit(solution)/shard_map/ppermute | solution.py:376
  233.0 21.4 %all-to-all-start.2 = ((bf16[8,32,1152]{2,1,0:T(8,128)(2,1)}), bf16[8,32,1152]{2,1,0:T(8,128)(2,1)S(1)}, u32[]{:S(2)}, u32[]{:S(2)}) async-start(bf16[8,32,1152]{2,1,0:T(8,128)(2,1)} %bitcast.224), calls=%async_computation.2 | async-start | bytes 1179648 | tf_op jit(solution)/shard_map/all_to_all | solution.py:472
  237.8 16.6 %collective-permute-start.41 = (bf16[256,1152]{1,0:T(8,128)(2,1)}, bf16[256,1152]{1,0:T(8,128)(2,1)}, u32[]{:S(2)}, u32[]{:S(2)}) collective-permute-start(bf16[256,1152]{1,0:T(8,128)(2,1)} %copy-done.102), channel_id=1, source_target_pairs={{0,2},{2,0},{1,3},{3,1},{4,6},{6,4},{5,7},{7,5},{8,10},{10,8},{9,1... | collective-permute-start | bytes 1769480 | tf_op jit(solution)/shard_map/ppermute | solution.py:325
  240.1 15.7 %collective-permute-start.40 = (bf16[256,1152]{1,0:T(8,128)(2,1)}, bf16[256,1152]{1,0:T(8,128)(2,1)S(1)}, u32[]{:S(2)}, u32[]{:S(2)}) collective-permute-start(bf16[256,1152]{1,0:T(8,128)(2,1)} %add_convert_fusion.2), channel_id=1, source_target_pairs={{0,1},{1,0},{2,3},{3,2},{4,5},{5,4},{6,7},{7,6},{8,9},{9,8},{10,11... | collective-permute-start | bytes 1769480 | tf_op jit(solution)/shard_map/ppermute | solution.py:325
  262.2 15.0 %collective-permute-start.43 = (bf16[256,1152]{1,0:T(8,128)(2,1)}, bf16[256,1152]{1,0:T(8,128)(2,1)}, u32[]{:S(2)}, u32[]{:S(2)}) collective-permute-start(bf16[256,1152]{1,0:T(8,128)(2,1)} %get-tuple-element.163.refs_0_), channel_id=1, source_target_pairs={{0,1},{1,0},{2,3},{3,2},{4,5},{5,4},{6,7},{7,6},{8,9},{9,8},{10,11... | collective-permute-start | bytes 1769480 | tf_op jit(solution)/shard_map/ppermute | solution.py:325
  263.7 21.5 %all-to-all-start.3 = ((bf16[8,32,1152]{2,1,0:T(8,128)(2,1)}), bf16[8,32,1152]{2,1,0:T(8,128)(2,1)S(1)}, u32[]{:S(2)}, u32[]{:S(2)}) async-start(bf16[8,32,1152]{2,1,0:T(8,128)(2,1)} %bitcast.79), calls=%async_computation.3 | async-start | bytes 1179648 | tf_op jit(solution)/shard_map/all_to_all | solution.py:476
  269.7 15.6 %collective-permute-start.42 = (bf16[256,1152]{1,0:T(8,128)(2,1)}, bf16[256,1152]{1,0:T(8,128)(2,1)}, u32[]{:S(2)}, u32[]{:S(2)}) collective-permute-start(bf16[256,1152]{1,0:T(8,128)(2,1)} %get-tuple-element.163.refs_0_), channel_id=1, source_target_pairs={{0,2},{2,0},{1,3},{3,1},{4,6},{6,4},{5,7},{7,5},{8,10},{10,8},{9,1... | collective-permute-start | bytes 1769480 | tf_op jit(solution)/shard_map/ppermute | solution.py:325
  301.4 24.3 %collective-permute-start.48 = (bf16[144,1792]{1,0:T(8,128)(2,1)S(1)}, bf16[144,1792]{1,0:T(8,128)(2,1)S(1)}, u32[]{:S(2)}, u32[]{:S(2)}) collective-permute-start(bf16[144,1792]{1,0:T(8,128)(2,1)S(1)} %get-tuple-element.162), channel_id=1, source_target_pairs={{0,8},{2,6},{8,16},{10,2},{16,24},{18,10},{24,28},{26,18},{28,20},... | collective-permute-start | bytes 1548296 | tf_op jit(solution)/shard_map/ppermute | solution.py:376
  325.2 31.7 %collective-permute-start.47 = (bf16[256,1152]{1,0:T(8,128)(2,1)}, bf16[256,1152]{1,0:T(8,128)(2,1)}, u32[]{:S(2)}, u32[]{:S(2)}) collective-permute-start(bf16[256,1152]{1,0:T(8,128)(2,1)} %get-tuple-element.172), channel_id=1, source_target_pairs={{0,2},{2,0},{1,3},{3,1},{4,6},{6,4},{5,7},{7,5},{8,10},{10,8},{9,1... | collective-permute-start | bytes 1769480 | tf_op jit(solution)/shard_map/ppermute | solution.py:325
  325.9 11.6 %collective-permute-start.49 = (bf16[144,1792]{1,0:T(8,128)(2,1)S(1)}, bf16[144,1792]{1,0:T(8,128)(2,1)S(1)}, u32[]{:S(2)}, u32[]{:S(2)}) collective-permute-start(bf16[144,1792]{1,0:T(8,128)(2,1)S(1)} %add_convert_fusion.21), channel_id=1, source_target_pairs={{0,8},{2,6},{8,16},{10,2},{16,24},{18,10},{24,28},{26,18},{28,20},... | collective-permute-start | bytes 1548296 | tf_op jit(solution)/shard_map/ppermute | solution.py:376
  334.4 18.8 %collective-permute-start.58 = (bf16[144,1792]{1,0:T(8,128)(2,1)S(1)}, bf16[144,1792]{1,0:T(8,128)(2,1)S(1)}, u32[]{:S(2)}, u32[]{:S(2)}) collective-permute-start(bf16[144,1792]{1,0:T(8,128)(2,1)S(1)} %get-tuple-element.178), channel_id=1, source_target_pairs={{0,8},{2,6},{8,16},{10,2},{16,24},{18,10},{24,28},{26,18},{28,20},... | collective-permute-start | bytes 1548296 | tf_op jit(solution)/shard_map/ppermute | solution.py:376
  337.0 19.9 %collective-permute-start.46 = (bf16[256,1152]{1,0:T(8,128)(2,1)}, bf16[256,1152]{1,0:T(8,128)(2,1)}, u32[]{:S(2)}, u32[]{:S(2)}) collective-permute-start(bf16[256,1152]{1,0:T(8,128)(2,1)} %add_convert_fusion.1), channel_id=1, source_target_pairs={{0,1},{1,0},{2,3},{3,2},{4,5},{5,4},{6,7},{7,6},{8,9},{9,8},{10,11... | collective-permute-start | bytes 1769480 | tf_op jit(solution)/shard_map/ppermute | solution.py:325
  338.5 27.3 %collective-permute-start.59 = (bf16[144,1792]{1,0:T(8,128)(2,1)}, bf16[144,1792]{1,0:T(8,128)(2,1)}, u32[]{:S(2)}, u32[]{:S(2)}) collective-permute-start(bf16[144,1792]{1,0:T(8,128)(2,1)} %add_convert_fusion.20), channel_id=1, source_target_pairs={{0,8},{2,6},{8,16},{10,2},{16,24},{18,10},{24,28},{26,18},{28,20},... | collective-permute-start | bytes 1548296 | tf_op jit(solution)/shard_map/ppermute | solution.py:376
  354.4 15.1 %collective-permute-start.61 = (bf16[144,1792]{1,0:T(8,128)(2,1)}, bf16[144,1792]{1,0:T(8,128)(2,1)}, u32[]{:S(2)}, u32[]{:S(2)}) collective-permute-start(bf16[144,1792]{1,0:T(8,128)(2,1)} %add_convert_fusion.18), channel_id=1, source_target_pairs={{0,8},{2,6},{8,16},{10,2},{16,24},{18,10},{24,28},{26,18},{28,20},... | collective-permute-start | bytes 1548296 | tf_op jit(solution)/shard_map/ppermute | solution.py:376
  356.1 15.7 %collective-permute-start.57 = (bf16[144,1792]{1,0:T(8,128)(2,1)}, bf16[144,1792]{1,0:T(8,128)(2,1)}, u32[]{:S(2)}, u32[]{:S(2)}) collective-permute-start(bf16[144,1792]{1,0:T(8,128)(2,1)} %copy-done.103), channel_id=1, source_target_pairs={{0,8},{2,6},{8,16},{10,2},{16,24},{18,10},{24,28},{26,18},{28,20},... | collective-permute-start | bytes 1548296 | tf_op jit(solution)/shard_map/ppermute | solution.py:376
  362.9 14.5 %collective-permute-start.51 = (bf16[256,1152]{1,0:T(8,128)(2,1)S(1)}, bf16[256,1152]{1,0:T(8,128)(2,1)S(1)}, u32[]{:S(2)}, u32[]{:S(2)}) collective-permute-start(bf16[256,1152]{1,0:T(8,128)(2,1)S(1)} %get-tuple-element.187.refs_0_.refs_5_), channel_id=1, source_target_pairs={{0,1},{1,0},{2,3},{3,2},{4,5},{5,4},{6,7},{7,6},{8,9},{9,8},{10,11... | collective-permute-start | bytes 1769480 | tf_op jit(solution)/shard_map/ppermute | solution.py:325
  364.4 24.0 %collective-permute-start.50 = (bf16[256,1152]{1,0:T(8,128)(2,1)S(1)}, bf16[256,1152]{1,0:T(8,128)(2,1)S(1)}, u32[]{:S(2)}, u32[]{:S(2)}) collective-permute-start(bf16[256,1152]{1,0:T(8,128)(2,1)S(1)} %get-tuple-element.187.refs_0_.refs_5_), channel_id=1, source_target_pairs={{0,2},{2,0},{1,3},{3,1},{4,6},{6,4},{5,7},{7,5},{8,10},{10,8},{9,1... | collective-permute-start | bytes 1769480 | tf_op jit(solution)/shard_map/ppermute | solution.py:325
  373.2 14.3 %collective-permute-start.60 = (bf16[144,1792]{1,0:T(8,128)(2,1)S(1)}, bf16[144,1792]{1,0:T(8,128)(2,1)S(1)}, u32[]{:S(2)}, u32[]{:S(2)}) collective-permute-start(bf16[144,1792]{1,0:T(8,128)(2,1)S(1)} %add_convert_fusion.19), channel_id=1, source_target_pairs={{0,8},{2,6},{8,16},{10,2},{16,24},{18,10},{24,28},{26,18},{28,20},... | collective-permute-start | bytes 1548296 | tf_op jit(solution)/shard_map/ppermute | solution.py:376
  378.4 43.0 %collective-permute-start.65 = (bf16[144,1792]{1,0:T(8,128)(2,1)}, bf16[144,1792]{1,0:T(8,128)(2,1)}, u32[]{:S(2)}, u32[]{:S(2)}) collective-permute-start(bf16[144,1792]{1,0:T(8,128)(2,1)} %add_convert_fusion.14), channel_id=1, source_target_pairs={{0,8},{2,6},{8,16},{10,2},{16,24},{18,10},{24,28},{26,18},{28,20},... | collective-permute-start | bytes 1548296 | tf_op jit(solution)/shard_map/ppermute | solution.py:376
  382.8 40.0 %collective-permute-start.67 = (bf16[144,1792]{1,0:T(8,128)(2,1)}, bf16[144,1792]{1,0:T(8,128)(2,1)}, u32[]{:S(2)}, u32[]{:S(2)}) collective-permute-start(bf16[144,1792]{1,0:T(8,128)(2,1)} %add_convert_fusion.12), channel_id=1, source_target_pairs={{0,8},{2,6},{8,16},{10,2},{16,24},{18,10},{24,28},{26,18},{28,20},... | collective-permute-start | bytes 1548296 | tf_op jit(solution)/shard_map/ppermute | solution.py:376
  401.6 25.9 %collective-permute-start.63 = (bf16[144,1792]{1,0:T(8,128)(2,1)}, bf16[144,1792]{1,0:T(8,128)(2,1)}, u32[]{:S(2)}, u32[]{:S(2)}) collective-permute-start(bf16[144,1792]{1,0:T(8,128)(2,1)} %add_convert_fusion.16), channel_id=1, source_target_pairs={{0,8},{2,6},{8,16},{10,2},{16,24},{18,10},{24,28},{26,18},{28,20},... | collective-permute-start | bytes 1548296 | tf_op jit(solution)/shard_map/ppermute | solution.py:376
  403.8 25.9 %collective-permute-start.53 = (bf16[256,1152]{1,0:T(8,128)(2,1)}, bf16[256,1152]{1,0:T(8,128)(2,1)}, u32[]{:S(2)}, u32[]{:S(2)}) collective-permute-start(bf16[256,1152]{1,0:T(8,128)(2,1)} %get-tuple-element.194), channel_id=1, source_target_pairs={{0,2},{2,0},{1,3},{3,1},{4,6},{6,4},{5,7},{7,5},{8,10},{10,8},{9,1... | collective-permute-start | bytes 1769480 | tf_op jit(solution)/shard_map/ppermute | solution.py:325
  421.4 27.2 %collective-permute-start.55 = (bf16[256,1152]{1,0:T(8,128)(2,1)}, bf16[256,1152]{1,0:T(8,128)(2,1)S(1)}, u32[]{:S(2)}, u32[]{:S(2)}) collective-permute-start(bf16[256,1152]{1,0:T(8,128)(2,1)} %copy-done.101), channel_id=1, source_target_pairs={{0,2},{2,0},{1,3},{3,1},{4,6},{6,4},{5,7},{7,5},{8,10},{10,8},{9,1... | collective-permute-start | bytes 1769480 | tf_op jit(solution)/shard_map/ppermute | solution.py:325
  425.7 11.8 %collective-permute-start.71 = (bf16[144,1792]{1,0:T(8,128)(2,1)S(1)}, bf16[144,1792]{1,0:T(8,128)(2,1)S(1)}, u32[]{:S(2)}, u32[]{:S(2)}) collective-permute-start(bf16[144,1792]{1,0:T(8,128)(2,1)S(1)} %add_convert_fusion.10), channel_id=1, source_target_pairs={{0,8},{2,6},{8,16},{10,2},{16,24},{18,10},{24,28},{26,18},{28,20},... | collective-permute-start | bytes 1548296 | tf_op jit(solution)/shard_map/ppermute | solution.py:376
  430.9 18.5 %collective-permute-start.54 = (bf16[256,1152]{1,0:T(8,128)(2,1)S(1)}, bf16[256,1152]{1,0:T(8,128)(2,1)S(1)}, u32[]{:S(2)}, u32[]{:S(2)}) collective-permute-start(bf16[256,1152]{1,0:T(8,128)(2,1)S(1)} %add_convert_fusion), channel_id=1, source_target_pairs={{0,1},{1,0},{2,3},{3,2},{4,5},{5,4},{6,7},{7,6},{8,9},{9,8},{10,11... | collective-permute-start | bytes 1769480 | tf_op jit(solution)/shard_map/ppermute | solution.py:325
  431.5 19.8 %collective-permute-start.70 = (bf16[144,1792]{1,0:T(8,128)(2,1)}, bf16[144,1792]{1,0:T(8,128)(2,1)}, u32[]{:S(2)}, u32[]{:S(2)}) collective-permute-start(bf16[144,1792]{1,0:T(8,128)(2,1)} %add_convert_fusion.13), channel_id=1, source_target_pairs={{0,8},{2,6},{8,16},{10,2},{16,24},{18,10},{24,28},{26,18},{28,20},... | collective-permute-start | bytes 1548296 | tf_op jit(solution)/shard_map/ppermute | solution.py:376
  432.1 14.0 %collective-permute-start.66 = (bf16[144,1024]{1,0:T(8,128)(2,1)S(1)}, bf16[144,1024]{1,0:T(8,128)(2,1)S(1)}, u32[]{:S(2)}, u32[]{:S(2)}) collective-permute-start(bf16[144,1024]{1,0:T(8,128)(2,1)S(1)} %add_convert_fusion.27), channel_id=1, source_target_pairs={{0,8},{2,6},{8,16},{10,2},{16,24},{18,10},{24,28},{26,18},{28,20},... | collective-permute-start | bytes 884744 | tf_op jit(solution)/shard_map/ppermute | solution.py:376
  437.5 31.4 %collective-permute-start.89 = (bf16[144,1792]{1,0:T(8,128)(2,1)}, bf16[144,1792]{1,0:T(8,128)(2,1)}, u32[]{:S(2)}, u32[]{:S(2)}) collective-permute-start(bf16[144,1792]{1,0:T(8,128)(2,1)} %add_convert_fusion.9), channel_id=1, source_target_pairs={{0,8},{2,6},{8,16},{10,2},{16,24},{18,10},{24,28},{26,18},{28,20},... | collective-permute-start | bytes 1548296 | tf_op jit(solution)/shard_map/ppermute | solution.py:376
  446.2 24.9 %collective-permute-start.74 = (bf16[144,1792]{1,0:T(8,128)(2,1)}, bf16[144,1792]{1,0:T(8,128)(2,1)}, u32[]{:S(2)}, u32[]{:S(2)}) collective-permute-start(bf16[144,1792]{1,0:T(8,128)(2,1)} %add_convert_fusion.7), channel_id=1, source_target_pairs={{0,8},{2,6},{8,16},{10,2},{16,24},{18,10},{24,28},{26,18},{28,20},... | collective-permute-start | bytes 1548296 | tf_op jit(solution)/shard_map/ppermute | solution.py:376
  448.6 11.8 %collective-permute-start.69 = (bf16[144,1024]{1,0:T(8,128)(2,1)}, bf16[144,1024]{1,0:T(8,128)(2,1)}, u32[]{:S(2)}, u32[]{:S(2)}) collective-permute-start(bf16[144,1024]{1,0:T(8,128)(2,1)} %add_convert_fusion.26), channel_id=1, source_target_pairs={{0,8},{2,6},{8,16},{10,2},{16,24},{18,10},{24,28},{26,18},{28,20},... | collective-permute-start | bytes 884744 | tf_op jit(solution)/shard_map/ppermute | solution.py:376
  462.3 20.4 %collective-permute-start.73 = (bf16[144,1792]{1,0:T(8,128)(2,1)}, bf16[144,1792]{1,0:T(8,128)(2,1)}, u32[]{:S(2)}, u32[]{:S(2)}) collective-permute-start(bf16[144,1792]{1,0:T(8,128)(2,1)} %add_convert_fusion.8), channel_id=1, source_target_pairs={{0,8},{2,6},{8,16},{10,2},{16,24},{18,10},{24,28},{26,18},{28,20},... | collective-permute-start | bytes 1548296 | tf_op jit(solution)/shard_map/ppermute | solution.py:376
  463.8 17.9 %collective-permute-start.72 = (bf16[144,1024]{1,0:T(8,128)(2,1)}, bf16[144,1024]{1,0:T(8,128)(2,1)}, u32[]{:S(2)}, u32[]{:S(2)}) collective-permute-start(bf16[144,1024]{1,0:T(8,128)(2,1)} %add_convert_fusion.25), channel_id=1, source_target_pairs={{0,8},{2,6},{8,16},{10,2},{16,24},{18,10},{24,28},{26,18},{28,20},... | collective-permute-start | bytes 884744 | tf_op jit(solution)/shard_map/ppermute | solution.py:376
  473.1 14.4 %collective-permute-start.85 = (bf16[144,1792]{1,0:T(8,128)(2,1)}, bf16[144,1792]{1,0:T(8,128)(2,1)S(1)}, u32[]{:S(2)}, u32[]{:S(2)}) collective-permute-start(bf16[144,1792]{1,0:T(8,128)(2,1)} %add_convert_fusion.5), channel_id=1, source_target_pairs={{0,8},{2,6},{8,16},{10,2},{16,24},{18,10},{24,28},{26,18},{28,20},... | collective-permute-start | bytes 1548296 | tf_op jit(solution)/shard_map/ppermute | solution.py:376
  476.2 33.7 %all-to-all-start.4 = ((bf16[8,32,1152]{2,1,0:T(8,128)(2,1)}), bf16[8,32,1152]{2,1,0:T(8,128)(2,1)S(1)}, u32[]{:S(2)}, u32[]{:S(2)}) async-start(bf16[8,32,1152]{2,1,0:T(8,128)(2,1)} %bitcast.82), calls=%async_computation.4 | async-start | bytes 1179648 | tf_op jit(solution)/shard_map/all_to_all | solution.py:476
  483.9 16.3 %collective-permute-start.76 = (bf16[144,1792]{1,0:T(8,128)(2,1)S(1)}, bf16[144,1792]{1,0:T(8,128)(2,1)S(1)}, u32[]{:S(2)}, u32[]{:S(2)}) collective-permute-start(bf16[144,1792]{1,0:T(8,128)(2,1)S(1)} %add_convert_fusion.6), channel_id=1, source_target_pairs={{0,8},{2,6},{8,16},{10,2},{16,24},{18,10},{24,28},{26,18},{28,20},... | collective-permute-start | bytes 1548296 | tf_op jit(solution)/shard_map/ppermute | solution.py:376
  486.0 14.2 %collective-permute-start.75 = (bf16[144,1024]{1,0:T(8,128)(2,1)S(1)}, bf16[144,1024]{1,0:T(8,128)(2,1)S(1)}, u32[]{:S(2)}, u32[]{:S(2)}) collective-permute-start(bf16[144,1024]{1,0:T(8,128)(2,1)S(1)} %add_convert_fusion.24), channel_id=1, source_target_pairs={{0,8},{2,6},{8,16},{10,2},{16,24},{18,10},{24,28},{26,18},{28,20},... | collective-permute-start | bytes 884744 | tf_op jit(solution)/shard_map/ppermute | solution.py:376
  501.2 23.3 %collective-permute-start.87 = (bf16[144,1792]{1,0:T(8,128)(2,1)}, bf16[144,1792]{1,0:T(8,128)(2,1)}, u32[]{:S(2)}, u32[]{:S(2)}) collective-permute-start(bf16[144,1792]{1,0:T(8,128)(2,1)} %add_convert_fusion.4), channel_id=1, source_target_pairs={{0,8},{2,6},{8,16},{10,2},{16,24},{18,10},{24,28},{26,18},{28,20},... | collective-permute-start | bytes 1548296 | tf_op jit(solution)/shard_map/ppermute | solution.py:376
  509.4 12.6 %collective-permute-start.86 = (f32[72,1728]{1,0:T(8,128)}, f32[72,1728]{1,0:T(8,128)}, u32[]{:S(2)}, u32[]{:S(2)}) collective-permute-start(f32[72,1728]{1,0:T(8,128)} %get-tuple-element.275), channel_id=1, source_target_pairs={{0,2},{2,0},{1,3},{3,1},{4,6},{6,4},{5,7},{7,5},{8,10},{10,8},{9,1... | collective-permute-start | bytes 1493000 | tf_op jit(solution)/shard_map/ppermute | solution.py:325
  (150 other events, 1903.6 us)

commit v5 on v4

--- a/solution.py
+++ b/solution.py
@@ -630,7 +630,7 @@
         [struct((size, width), F32), block, vector, vector],
         (*together(shares, ups.blocks[0]), middle, cotangent, branch, g_fi, g_ao),
     )
-    meet(rings, dr_own)
+    meet([downs, ups, gates], dr_own)
 
     dr_all = flat(gather_rows(dr_own))
     dr_used = [dr_all[i] for i in q_blocks]
@@ -644,12 +644,12 @@
         ),
         scratch=[pltpu.VMEM((rows, HD), F32)] * 2,
     )
-    meet(rings, grads)
+    meet([downs, ups, gates], grads)
     shares, sent = scatter_rows(by_tensor(da_parts))
     stage()
     smalls = RingSum(outer([(a_all, [grads]), (dr_used, [o])], spot_line))
     smalls.step()
-    meet(rings, *sent)
+    meet([downs, ups, gates], *sent)
     smalls.wait(ups.sum)
     stage()
     smalls.step()

time: 548 us -> 552 us (level)
    unnamed x238 -> x252, local copies, waits for them, and re-layouts: 42.2 us -> 40.5 us
  transfers between devices with their start and end apart: 97 -> 97, of which waited for: 36 -> 37; matrix products, arithmetic and copies ran while one was open for 25% -> 25% of each run, Pallas kernels for 15% -> 15%
where the time goes in v5:
time: 552 us; the launch traced here: 542 us
  waiting for transfers between devices  138 us (25%)
  local copies, waits for them, and re-layouts  122 us (22%)
  starting transfers between devices  118 us (21%)
  Pallas kernels  99.8 us (18%)
  other arithmetic  61.7 us (11%)
    pallas_call x14, Pallas kernels, call(): pl.pallas_call(kernel, out_shape=outs, scratch_shapes=list(scratch), comp...  99.8 us
    ppermute x56, waiting for transfers between devices, hop(): return lax.ppermute(values, ('seq', 'core'), pairs)  96.1 us
    ppermute x56, starting transfers between devices, hop(): return lax.ppermute(values, ('seq', 'core'), pairs)  73.6 us
    dynamic_update_slice x39, local copies, waits for them, and re-layouts, put(): lax.dynamic_update_slice(full, block[None], (spot, row, 0), allow_negativ...  53.3 us
    unnamed x252, local copies, waits for them, and re-layouts  40.5 us
    convert_element_type x24, other arithmetic, step(): self.sum = total if self.left() == 0 else total.astype(BF16)  27.9 us
    ppermute x33, waiting for transfers between devices, shift(): lax.ppermute(values, axis, [(i, (i + step) % size) for i in range(size)])  23.1 us
    ppermute x33, starting transfers between devices, shift(): lax.ppermute(values, axis, [(i, (i + step) % size) for i in range(size)])  16.5 us
  transfers between devices with their start and end apart: 97, of which 37 were waited for; matrix products, arithmetic and copies ran while one was open for 25% of the time, Pallas kernels for 15%

profile of v5, /device:TPU:0, one launch (start us, length us, event | category | flops | bytes accessed | tf_op | source)
XLA Modules:
  0.0 541.6 jit_solution(14118322041761024947)
XLA Ops:
  3.2 3.1 collective-permute-start
  13.8 3.7 all-to-all-start.1
  19.9 4.8 all-to-all-start
  37.6 3.1 collective-permute-done.1
  44.2 3.5 collective-permute-done.2
  50.4 3.8 collective-permute-done.3
  56.6 3.8 collective-permute-done.4
  62.8 3.8 collective-permute-done.5
  69.0 3.8 collective-permute-done.6
  82.3 2.6 broadcast.201.clone
  85.0 2.5 bitcast_dynamic-update-slice_fusion.23
  90.7 2.5 bitcast_dynamic-update-slice_fusion.22
  94.8 2.6 bitcast_dynamic-update-slice_fusion.6
  97.4 2.4 collective-permute-start.33
  99.8 2.5 bitcast_dynamic-update-slice_fusion.14
  106.9 2.4 collective-permute-done.33
  111.2 3.7 collective-permute-done.26
  115.3 2.5 bitcast_dynamic-update-slice_fusion.13
  117.8 2.6 collective-permute-done.20
  120.8 2.5 bitcast_dynamic-update-slice_fusion.20
  123.3 4.4 maximum_select_fusion
  130.2 2.6 collective-permute-start.27
  134.5 10.8 %shard_map.290 = (bf16[1024,256]{1,0:T(8,128)(2,1)S(1)}, bf16[1024,1024]{1,0:T(8,128)(2,1)}, bf16[1024,512]{1,0:T(8,128)(2,1)}, bf16[1024,256]{1,0:T(8,128)(2,1)...) custom-call(bf16[256,1152]{1,0:T(8,128)(2,1)} %copy-done.9, ...), custom_call_target="tpu_custom_call" | custom-call | bytes 1 | tf_op jit(solution)/shard_map/pallas_call | solution.py:66
  148.1 2.5 bitcast_dynamic-update-slice_fusion.19
  157.4 4.2 collective-permute-done.28
  164.8 2.3 collective-permute-done.35
  180.3 3.3 collective-permute-done.23
  186.6 2.5 collective-permute-done.30
  191.3 3.3 collective-permute-done.37
  197.2 3.0 collective-permute-done.24
  201.7 4.0 collective-permute-done.31
  206.4 14.5 %shard_map.292 = (bf16[1024,1792]{1,0:T(8,128)(2,1)S(1)}, bf16[1024,1792]{1,0:T(8,128)(2,1)S(1)}, bf16[1024,1792]{1,0:T(8,128)(2,1)S(1)}) custom-call(bf16[256,1152]{1,0:T(8,128)(2,1)S(1)} %get-tuple-element.144.refs_0_, bf16[256,1152]{1,0:T(8,128)(2,1)S(1)} %collective-permute-done.15.refs_1_, bf16[256,1152]{1,0:T(8,128)(2,1)S(1)} %collective-permute-done.16.refs_2_, ...), custom_call_target="tpu_custom_call" | custom-call | bytes 1 | tf_op jit(solution)/shard_map/pallas_call | solution.py:66
  225.4 5.9 %shard_map.293 = (bf16[256,1152]{1,0:T(8,128)(2,1)S(1)}, bf16[256,1152]{1,0:T(8,128)(2,1)S(1)}, bf16[256,1152]{1,0:T(8,128)(2,1)S(1)}, bf16[256,1152]{1,0:T(8,128)(2,1)}) custom-call(bf16[1024,1792]{1,0:T(8,128)(2,1)S(1)} %get-tuple-element.161.hid_ref.refs_4_, bf16[1152,1792]{1,0:T(8,128)(2,1)S(1)} %bitcast.198), custom_call_target="tpu_custom_call" | custom-call | bytes 1 | tf_op jit(solution)/shard_map/pallas_call | solution.py:66
  233.0 4.8 all-to-all-start.2
  244.3 10.1 %all-to-all-done.2 = bf16[8,32,1152]{2,1,0:T(8,128)(2,1)S(1)} async-done(((bf16[8,32,1152]{2,1,0:T(8,128)(2,1)}), bf16[8,32,1152]{2,1,0:T(8,128)(2,1)S(1)}, u32[]{:S(2)}, u32[]{:S(2)}) %all-to-all-start.2) | async-done | bytes 589856 | tf_op jit(solution)/shard_map/all_to_all | solution.py:472
  258.9 2.9 shard_map.294
  263.9 6.0 %all-to-all-start.3 = ((bf16[8,32,1152]{2,1,0:T(8,128)(2,1)}), bf16[8,32,1152]{2,1,0:T(8,128)(2,1)S(1)}, u32[]{:S(2)}, u32[]{:S(2)}) async-start(bf16[8,32,1152]{2,1,0:T(8,128)(2,1)} %bitcast.79), calls=%async_computation.3 | async-start | bytes 1179648 | tf_op jit(solution)/shard_map/all_to_all | solution.py:476
  269.9 7.5 %collective-permute-done.43.refs_2_ = bf16[256,1152]{1,0:T(8,128)(2,1)} collective-permute-done((bf16[256,1152]{1,0:T(8,128)(2,1)}, bf16[256,1152]{1,0:T(8,128)(2,1)}, u32[]{:S(2)}, u32[]{:S(2)}) %collective-permute-start.43) | collective-permute-done | bytes 589856 | tf_op jit(solution)/shard_map/ppermute | solution.py:325
  277.4 8.0 %all-to-all-done.3 = bf16[8,32,1152]{2,1,0:T(8,128)(2,1)S(1)} async-done(((bf16[8,32,1152]{2,1,0:T(8,128)(2,1)}), bf16[8,32,1152]{2,1,0:T(8,128)(2,1)S(1)}, u32[]{:S(2)}, u32[]{:S(2)}) %all-to-all-start.3) | async-done | bytes 589856 | tf_op jit(solution)/shard_map/all_to_all | solution.py:476
  286.3 2.6 copy-done.8
  289.6 9.0 %shard_map.295 = (bf16[144,1792]{1,0:T(8,128)(2,1)S(1)}, bf16[144,1792]{1,0:T(8,128)(2,1)S(1)}, bf16[144,1792]{1,0:T(8,128)(2,1)S(1)}, bf16[144,1792]{1,0:T(8,12...) custom-call(s32[8]{0:T(128)S(1)} %copy-done.100, ...), custom_call_target="tpu_custom_call" | custom-call | bytes 1 | tf_op jit(solution)/shard_map/pallas_call | solution.py:66
  307.3 19.0 %shard_map.296 = (bf16[1024,1792]{1,0:T(8,128)(2,1)S(1)}, bf16[1024,1792]{1,0:T(8,128)(2,1)S(1)}, bf16[256,1152]{1,0:T(8,128)(2,1)S(1)}, bf16[256,1152]{1,0:T(8,...) custom-call(bf16[256,1152]{1,0:T(8,128)(2,1)} %get-tuple-element.163.refs_0_, ...), custom_call_target="tpu_custom_call" | custom-call | bytes 1 | tf_op jit(solution)/shard_map/pallas_call | solution.py:66
  327.6 7.6 %shard_map.297 = (bf16[144,1792]{1,0:T(8,128)(2,1)}, bf16[144,1792]{1,0:T(8,128)(2,1)S(1)}, bf16[144,1792]{1,0:T(8,128)(2,1)S(1)}, bf16[144,1792]{1,0:T(8,128)(2...) custom-call(s32[8]{0:T(128)S(1)} %copy-done.101, ...), custom_call_target="tpu_custom_call" | custom-call | bytes 1 | tf_op jit(solution)/shard_map/pallas_call | solution.py:66
  348.0 7.6 %shard_map.298 = (bf16[144,1792]{1,0:T(8,128)(2,1)}, bf16[144,1792]{1,0:T(8,128)(2,1)S(1)}, bf16[144,1792]{1,0:T(8,128)(2,1)S(1)}, bf16[144,1792]{1,0:T(8,128)(2...) custom-call(s32[8]{0:T(128)S(1)} %copy-done.102, ...), custom_call_target="tpu_custom_call" | custom-call | bytes 1 | tf_op jit(solution)/shard_map/pallas_call | solution.py:66
  356.1 2.5 add_convert_fusion.17
  359.4 3.0 shard_map.299
  374.3 3.2 collective-permute-done.51.refs_2_.refs_7_
  379.7 2.6 collective-permute-done.60
  385.2 2.7 collective-permute-done.65
  391.8 11.4 %shard_map.300 = (bf16[1024,768]{1,0:T(8,128)(2,1)}, f32[1,256]{1,0:T(1,128)S(1)}, f32[1,256]{1,0:T(1,128)S(1)}, bf16[256,1152]{1,0:T(8,128)(2,1)S(1)}, bf16[256...) custom-call(bf16[256,1152]{1,0:T(8,128)(2,1)S(1)} %get-tuple-element.187.refs_0_.refs_5_, ...), custom_call_target="tpu_custom_call" | custom-call | bytes 1 | tf_op jit(solution)/shard_map/pallas_call | solution.py:66
  407.6 5.6 %shard_map.302 = (bf16[144,1024]{1,0:T(8,128)(2,1)}, bf16[144,1024]{1,0:T(8,128)(2,1)S(1)}, bf16[144,1024]{1,0:T(8,128)(2,1)S(1)}, bf16[144,1024]{1,0:T(8,128)(2...) custom-call(s32[8]{0:T(128)S(1)} %copy-done.103, ...), custom_call_target="tpu_custom_call" | custom-call | bytes 1 | tf_op jit(solution)/shard_map/pallas_call | solution.py:66
  431.0 10.4 %collective-permute-done.66 = bf16[144,1024]{1,0:T(8,128)(2,1)S(1)} collective-permute-done((bf16[144,1024]{1,0:T(8,128)(2,1)S(1)}, bf16[144,1024]{1,0:T(8,128)(2,1)S(1)}, u32[]{:S(2)}, u32[]{:S(2)}) %collective-permute-start.66) | collective-permute-done | bytes 294944 | tf_op jit(solution)/shard_map/ppermute | solution.py:376
  447.1 3.3 collective-permute-done.71
  453.7 5.1 collective-permute-done.54.refs_0_
  469.2 3.5 all-to-all-start.5
  479.8 4.2 all-to-all-start.4
  491.2 12.8 %collective-permute-done.75 = bf16[144,1024]{1,0:T(8,128)(2,1)S(1)} collective-permute-done((bf16[144,1024]{1,0:T(8,128)(2,1)S(1)}, bf16[144,1024]{1,0:T(8,128)(2,1)S(1)}, u32[]{:S(2)}, u32[]{:S(2)}) %collective-permute-start.75) | collective-permute-done | bytes 294944 | tf_op jit(solution)/shard_map/ppermute | solution.py:376
  505.0 4.6 collective-permute-start.87
  509.6 2.5 collective-permute-start.79
  513.7 5.9 %collective-permute-done.79 = bf16[144,1024]{1,0:T(8,128)(2,1)} collective-permute-done((bf16[144,1024]{1,0:T(8,128)(2,1)S(1)}, bf16[144,1024]{1,0:T(8,128)(2,1)}, u32[]{:S(2)}, u32[]{:S(2)}) %collective-permute-start.79) | collective-permute-done | bytes 294944 | tf_op jit(solution)/shard_map/ppermute | solution.py:376
  520.6 2.6 collective-permute-start.80
  523.3 2.5 maximum_select_fusion.3
  525.8 2.5 maximum_select_fusion.1
  534.0 3.7 collective-permute-done.83
  (566 shorter events, 233.4 us)
Async XLA Ops:
  3.2 30.3 %collective-permute-start = (bf16[80,1536]{1,0:T(8,128)(2,1)S(1)}, bf16[80,1536]{1,0:T(8,128)(2,1)S(1)}, u32[]{:S(2)}, u32[]{:S(2)}) collective-permute-start(bf16[80,1536]{1,0:T(8,128)(2,1)S(1)} %pad_maximum_fusion.2), channel_id=1, source_target_pairs={{0,8},{2,6},{8,16},{10,2},{16,24},{18,10},{24,28},{26,18},{28,20},... | collective-permute-start | bytes 737288 | tf_op jit(solution)/shard_map/ppermute | solution.py:376
  19.9 34.3 %all-to-all-start = ((bf16[8,32,1152]{2,1,0:T(8,128)(2,1)}), bf16[8,32,1152]{2,1,0:T(8,128)(2,1)S(1)}, u32[]{:S(2)}, u32[]{:S(2)}) async-start(bf16[8,32,1152]{2,1,0:T(8,128)(2,1)} %bitcast), calls=%async_computation | async-start | bytes 1179648 | tf_op jit(solution)/shard_map/all_to_all | solution.py:472
  74.1 49.2 %collective-permute-start.11 = (bf16[8,80,1536]{2,1,0:T(8,128)(2,1)}, bf16[8,80,1536]{2,1,0:T(8,128)(2,1)}, u32[]{:S(2)}, u32[]{:S(2)}) collective-permute-start(bf16[8,80,1536]{2,1,0:T(8,128)(2,1)} %bitcast_dynamic-update-slice_fusion.24), channel_id=1, source_target_pairs={{0,2},{2,0},{1,3},{3,1},{4,6},{6,4},{5,7},{7,5},{8,10},{10,8},{9,1... | collective-permute-start | bytes 5898248 | tf_op jit(solution)/shard_map/ppermute | solution.py:325
  74.2 23.2 %collective-permute-start.25 = (bf16[144,1792]{1,0:T(8,128)(2,1)S(1)}, bf16[144,1792]{1,0:T(8,128)(2,1)}, u32[]{:S(2)}, u32[]{:S(2)}) collective-permute-start(bf16[144,1792]{1,0:T(8,128)(2,1)S(1)} %get-tuple-element.148), channel_id=1, source_target_pairs={{0,8},{2,6},{8,16},{10,2},{16,24},{18,10},{24,28},{26,18},{28,20},... | collective-permute-start | bytes 1548296 | tf_op jit(solution)/shard_map/ppermute | solution.py:376
  75.2 12.3 %collective-permute-start.7 = (bf16[8,8,512]{2,1,0:T(8,128)(2,1)S(1)}, bf16[8,8,512]{2,1,0:T(8,128)(2,1)S(1)}, u32[]{:S(2)}, u32[]{:S(2)}) collective-permute-start(bf16[8,8,512]{2,1,0:T(8,128)(2,1)S(1)} %constant_dynamic-update-slice_fusion), channel_id=1, source_target_pairs={{0,2},{2,0},{1,3},{3,1},{4,6},{6,4},{5,7},{7,5},{8,10},{10,8},{9,1... | collective-permute-start | bytes 196616 | tf_op jit(solution)/shard_map/ppermute | solution.py:325
  77.1 13.5 %collective-permute-start.18 = (bf16[144,1792]{1,0:T(8,128)(2,1)}, bf16[144,1792]{1,0:T(8,128)(2,1)}, u32[]{:S(2)}, u32[]{:S(2)}) collective-permute-start(bf16[144,1792]{1,0:T(8,128)(2,1)} %get-tuple-element.145), channel_id=1, source_target_pairs={{0,8},{2,6},{8,16},{10,2},{16,24},{18,10},{24,28},{26,18},{28,20},... | collective-permute-start | bytes 1548296 | tf_op jit(solution)/shard_map/ppermute | solution.py:376
  77.8 16.6 %collective-permute-start.32 = (bf16[144,1792]{1,0:T(8,128)(2,1)}, bf16[144,1792]{1,0:T(8,128)(2,1)}, u32[]{:S(2)}, u32[]{:S(2)}) collective-permute-start(bf16[144,1792]{1,0:T(8,128)(2,1)} %get-tuple-element.151), channel_id=1, source_target_pairs={{0,8},{2,6},{8,16},{10,2},{16,24},{18,10},{24,28},{26,18},{28,20},... | collective-permute-start | bytes 1548296 | tf_op jit(solution)/shard_map/ppermute | solution.py:376
  88.6 15.0 %collective-permute-start.9 = (bf16[256,1152]{1,0:T(8,128)(2,1)S(1)}, bf16[256,1152]{1,0:T(8,128)(2,1)S(1)}, u32[]{:S(2)}, u32[]{:S(2)}) collective-permute-start(bf16[256,1152]{1,0:T(8,128)(2,1)S(1)} %shard_map.289.refs_0_), channel_id=1, source_target_pairs={{0,1},{1,0},{2,3},{3,2},{4,5},{5,4},{6,7},{7,6},{8,9},{9,8},{10,11... | collective-permute-start | bytes 1769480 | tf_op jit(solution)/shard_map/ppermute | solution.py:325
  90.7 42.8 %collective-permute-start.8 = (bf16[256,1152]{1,0:T(8,128)(2,1)S(1)}, bf16[256,1152]{1,0:T(8,128)(2,1)S(1)}, u32[]{:S(2)}, u32[]{:S(2)}) collective-permute-start(bf16[256,1152]{1,0:T(8,128)(2,1)S(1)} %shard_map.289.refs_0_), channel_id=1, source_target_pairs={{0,2},{2,0},{1,3},{3,1},{4,6},{6,4},{5,7},{7,5},{8,10},{10,8},{9,1... | collective-permute-start | bytes 1769480 | tf_op jit(solution)/shard_map/ppermute | solution.py:325
  97.4 11.9 %collective-permute-start.33 = (bf16[144,1792]{1,0:T(8,128)(2,1)}, bf16[144,1792]{1,0:T(8,128)(2,1)S(1)}, u32[]{:S(2)}, u32[]{:S(2)}) collective-permute-start(bf16[144,1792]{1,0:T(8,128)(2,1)} %collective-permute-done.32), channel_id=1, source_target_pairs={{0,8},{2,6},{8,16},{10,2},{16,24},{18,10},{24,28},{26,18},{28,20},... | collective-permute-start | bytes 1548296 | tf_op jit(solution)/shard_map/ppermute | solution.py:376
  105.4 28.1 %collective-permute-start.10 = (bf16[256,1152]{1,0:T(8,128)(2,1)S(1)}, bf16[256,1152]{1,0:T(8,128)(2,1)S(1)}, u32[]{:S(2)}, u32[]{:S(2)}) collective-permute-start(bf16[256,1152]{1,0:T(8,128)(2,1)S(1)} %collective-permute-done.9.refs_2_), channel_id=1, source_target_pairs={{0,2},{2,0},{1,3},{3,1},{4,6},{6,4},{5,7},{7,5},{8,10},{10,8},{9,1... | collective-permute-start | bytes 1769480 | tf_op jit(solution)/shard_map/ppermute | solution.py:325
  114.9 17.9 %collective-permute-start.34 = (bf16[144,1792]{1,0:T(8,128)(2,1)S(1)}, bf16[144,1792]{1,0:T(8,128)(2,1)S(1)}, u32[]{:S(2)}, u32[]{:S(2)}) collective-permute-start(bf16[144,1792]{1,0:T(8,128)(2,1)S(1)} %collective-permute-done.33), channel_id=1, source_target_pairs={{0,8},{2,6},{8,16},{10,2},{16,24},{18,10},{24,28},{26,18},{28,20},... | collective-permute-start | bytes 1548296 | tf_op jit(solution)/shard_map/ppermute | solution.py:376
  120.4 26.2 %collective-permute-start.21 = (bf16[144,1792]{1,0:T(8,128)(2,1)}, bf16[144,1792]{1,0:T(8,128)(2,1)}, u32[]{:S(2)}, u32[]{:S(2)}) collective-permute-start(bf16[144,1792]{1,0:T(8,128)(2,1)} %collective-permute-done.20), channel_id=1, source_target_pairs={{0,8},{2,6},{8,16},{10,2},{16,24},{18,10},{24,28},{26,18},{28,20},... | collective-permute-start | bytes 1548296 | tf_op jit(solution)/shard_map/ppermute | solution.py:376
  130.2 20.5 %collective-permute-start.27 = (bf16[144,1792]{1,0:T(8,128)(2,1)}, bf16[144,1792]{1,0:T(8,128)(2,1)}, u32[]{:S(2)}, u32[]{:S(2)}) collective-permute-start(bf16[144,1792]{1,0:T(8,128)(2,1)} %collective-permute-done.26), channel_id=1, source_target_pairs={{0,8},{2,6},{8,16},{10,2},{16,24},{18,10},{24,28},{26,18},{28,20},... | collective-permute-start | bytes 1548296 | tf_op jit(solution)/shard_map/ppermute | solution.py:376
  146.1 24.2 %collective-permute-start.14 = (bf16[256,1152]{1,0:T(8,128)(2,1)S(1)}, bf16[256,1152]{1,0:T(8,128)(2,1)S(1)}, u32[]{:S(2)}, u32[]{:S(2)}) collective-permute-start(bf16[256,1152]{1,0:T(8,128)(2,1)S(1)} %get-tuple-element.143), channel_id=1, source_target_pairs={{0,2},{2,0},{1,3},{3,1},{4,6},{6,4},{5,7},{7,5},{8,10},{10,8},{9,1... | collective-permute-start | bytes 1769480 | tf_op jit(solution)/shard_map/ppermute | solution.py:325
  153.0 17.3 %collective-permute-start.13 = (bf16[256,1152]{1,0:T(8,128)(2,1)S(1)}, bf16[256,1152]{1,0:T(8,128)(2,1)S(1)}, u32[]{:S(2)}, u32[]{:S(2)}) collective-permute-start(bf16[256,1152]{1,0:T(8,128)(2,1)S(1)} %add_convert_fusion.3), channel_id=1, source_target_pairs={{0,1},{1,0},{2,3},{3,2},{4,5},{5,4},{6,7},{7,6},{8,9},{9,8},{10,11... | collective-permute-start | bytes 1769480 | tf_op jit(solution)/shard_map/ppermute | solution.py:325
  154.6 12.5 %collective-permute-start.35 = (bf16[144,1792]{1,0:T(8,128)(2,1)S(1)}, bf16[144,1792]{1,0:T(8,128)(2,1)}, u32[]{:S(2)}, u32[]{:S(2)}) collective-permute-start(bf16[144,1792]{1,0:T(8,128)(2,1)S(1)} %copy-done.115), channel_id=1, source_target_pairs={{0,8},{2,6},{8,16},{10,2},{16,24},{18,10},{24,28},{26,18},{28,20},... | collective-permute-start | bytes 1548296 | tf_op jit(solution)/shard_map/ppermute | solution.py:376
  171.0 15.5 %collective-permute-start.16 = (bf16[256,1152]{1,0:T(8,128)(2,1)S(1)}, bf16[256,1152]{1,0:T(8,128)(2,1)S(1)}, u32[]{:S(2)}, u32[]{:S(2)}) collective-permute-start(bf16[256,1152]{1,0:T(8,128)(2,1)S(1)} %get-tuple-element.144.refs_0_), channel_id=1, source_target_pairs={{0,1},{1,0},{2,3},{3,2},{4,5},{5,4},{6,7},{7,6},{8,9},{9,8},{10,11... | collective-permute-start | bytes 1769480 | tf_op jit(solution)/shard_map/ppermute | solution.py:325
  172.6 33.8 %collective-permute-start.15 = (bf16[256,1152]{1,0:T(8,128)(2,1)S(1)}, bf16[256,1152]{1,0:T(8,128)(2,1)S(1)}, u32[]{:S(2)}, u32[]{:S(2)}) collective-permute-start(bf16[256,1152]{1,0:T(8,128)(2,1)S(1)} %get-tuple-element.144.refs_0_), channel_id=1, source_target_pairs={{0,2},{2,0},{1,3},{3,1},{4,6},{6,4},{5,7},{7,5},{8,10},{10,8},{9,1... | collective-permute-start | bytes 1769480 | tf_op jit(solution)/shard_map/ppermute | solution.py:325
  173.1 16.0 %collective-permute-start.30 = (bf16[144,1792]{1,0:T(8,128)(2,1)}, bf16[144,1792]{1,0:T(8,128)(2,1)S(1)}, u32[]{:S(2)}, u32[]{:S(2)}) collective-permute-start(bf16[144,1792]{1,0:T(8,128)(2,1)} %collective-permute-done.29), channel_id=1, source_target_pairs={{0,8},{2,6},{8,16},{10,2},{16,24},{18,10},{24,28},{26,18},{28,20},... | collective-permute-start | bytes 1548296 | tf_op jit(solution)/shard_map/ppermute | solution.py:376
  178.1 16.6 %collective-permute-start.37 = (bf16[144,1792]{1,0:T(8,128)(2,1)S(1)}, bf16[144,1792]{1,0:T(8,128)(2,1)S(1)}, u32[]{:S(2)}, u32[]{:S(2)}) collective-permute-start(bf16[144,1792]{1,0:T(8,128)(2,1)S(1)} %collective-permute-done.36), channel_id=1, source_target_pairs={{0,8},{2,6},{8,16},{10,2},{16,24},{18,10},{24,28},{26,18},{28,20},... | collective-permute-start | bytes 1548296 | tf_op jit(solution)/shard_map/ppermute | solution.py:376
  183.6 16.6 %collective-permute-start.24 = (bf16[144,1792]{1,0:T(8,128)(2,1)S(1)}, bf16[144,1792]{1,0:T(8,128)(2,1)S(1)}, u32[]{:S(2)}, u32[]{:S(2)}) collective-permute-start(bf16[144,1792]{1,0:T(8,128)(2,1)S(1)} %collective-permute-done.23), channel_id=1, source_target_pairs={{0,8},{2,6},{8,16},{10,2},{16,24},{18,10},{24,28},{26,18},{28,20},... | collective-permute-start | bytes 1548296 | tf_op jit(solution)/shard_map/ppermute | solution.py:376
  186.6 19.8 %collective-permute-start.17 = (bf16[256,1152]{1,0:T(8,128)(2,1)S(1)}, bf16[256,1152]{1,0:T(8,128)(2,1)S(1)}, u32[]{:S(2)}, u32[]{:S(2)}) collective-permute-start(bf16[256,1152]{1,0:T(8,128)(2,1)S(1)} %collective-permute-done.16.refs_2_), channel_id=1, source_target_pairs={{0,2},{2,0},{1,3},{3,1},{4,6},{6,4},{5,7},{7,5},{8,10},{10,8},{9,1... | collective-permute-start | bytes 1769480 | tf_op jit(solution)/shard_map/ppermute | solution.py:325
  189.1 16.6 %collective-permute-start.31 = (bf16[144,1792]{1,0:T(8,128)(2,1)S(1)}, bf16[144,1792]{1,0:T(8,128)(2,1)S(1)}, u32[]{:S(2)}, u32[]{:S(2)}) collective-permute-start(bf16[144,1792]{1,0:T(8,128)(2,1)S(1)} %collective-permute-done.30), channel_id=1, source_target_pairs={{0,8},{2,6},{8,16},{10,2},{16,24},{18,10},{24,28},{26,18},{28,20},... | collective-permute-start | bytes 1548296 | tf_op jit(solution)/shard_map/ppermute | solution.py:376
  194.7 30.0 %collective-permute-start.38 = (bf16[144,1792]{1,0:T(8,128)(2,1)S(1)}, bf16[144,1792]{1,0:T(8,128)(2,1)S(1)}, u32[]{:S(2)}, u32[]{:S(2)}) collective-permute-start(bf16[144,1792]{1,0:T(8,128)(2,1)S(1)} %collective-permute-done.37), channel_id=1, source_target_pairs={{0,8},{2,6},{8,16},{10,2},{16,24},{18,10},{24,28},{26,18},{28,20},... | collective-permute-start | bytes 1548296 | tf_op jit(solution)/shard_map/ppermute | solution.py:376
  233.0 21.4 %all-to-all-start.2 = ((bf16[8,32,1152]{2,1,0:T(8,128)(2,1)}), bf16[8,32,1152]{2,1,0:T(8,128)(2,1)S(1)}, u32[]{:S(2)}, u32[]{:S(2)}) async-start(bf16[8,32,1152]{2,1,0:T(8,128)(2,1)} %bitcast.224), calls=%async_computation.2 | async-start | bytes 1179648 | tf_op jit(solution)/shard_map/all_to_all | solution.py:472
  237.9 16.6 %collective-permute-start.41 = (bf16[256,1152]{1,0:T(8,128)(2,1)}, bf16[256,1152]{1,0:T(8,128)(2,1)}, u32[]{:S(2)}, u32[]{:S(2)}) collective-permute-start(bf16[256,1152]{1,0:T(8,128)(2,1)} %copy-done.110), channel_id=1, source_target_pairs={{0,2},{2,0},{1,3},{3,1},{4,6},{6,4},{5,7},{7,5},{8,10},{10,8},{9,1... | collective-permute-start | bytes 1769480 | tf_op jit(solution)/shard_map/ppermute | solution.py:325
  240.1 15.7 %collective-permute-start.40 = (bf16[256,1152]{1,0:T(8,128)(2,1)}, bf16[256,1152]{1,0:T(8,128)(2,1)S(1)}, u32[]{:S(2)}, u32[]{:S(2)}) collective-permute-start(bf16[256,1152]{1,0:T(8,128)(2,1)} %add_convert_fusion.2), channel_id=1, source_target_pairs={{0,1},{1,0},{2,3},{3,2},{4,5},{5,4},{6,7},{7,6},{8,9},{9,8},{10,11... | collective-permute-start | bytes 1769480 | tf_op jit(solution)/shard_map/ppermute | solution.py:325
  262.4 15.0 %collective-permute-start.43 = (bf16[256,1152]{1,0:T(8,128)(2,1)}, bf16[256,1152]{1,0:T(8,128)(2,1)}, u32[]{:S(2)}, u32[]{:S(2)}) collective-permute-start(bf16[256,1152]{1,0:T(8,128)(2,1)} %get-tuple-element.163.refs_0_), channel_id=1, source_target_pairs={{0,1},{1,0},{2,3},{3,2},{4,5},{5,4},{6,7},{7,6},{8,9},{9,8},{10,11... | collective-permute-start | bytes 1769480 | tf_op jit(solution)/shard_map/ppermute | solution.py:325
  263.9 21.5 %all-to-all-start.3 = ((bf16[8,32,1152]{2,1,0:T(8,128)(2,1)}), bf16[8,32,1152]{2,1,0:T(8,128)(2,1)S(1)}, u32[]{:S(2)}, u32[]{:S(2)}) async-start(bf16[8,32,1152]{2,1,0:T(8,128)(2,1)} %bitcast.79), calls=%async_computation.3 | async-start | bytes 1179648 | tf_op jit(solution)/shard_map/all_to_all | solution.py:476
  269.9 15.6 %collective-permute-start.42 = (bf16[256,1152]{1,0:T(8,128)(2,1)}, bf16[256,1152]{1,0:T(8,128)(2,1)}, u32[]{:S(2)}, u32[]{:S(2)}) collective-permute-start(bf16[256,1152]{1,0:T(8,128)(2,1)} %get-tuple-element.163.refs_0_), channel_id=1, source_target_pairs={{0,2},{2,0},{1,3},{3,1},{4,6},{6,4},{5,7},{7,5},{8,10},{10,8},{9,1... | collective-permute-start | bytes 1769480 | tf_op jit(solution)/shard_map/ppermute | solution.py:325
  302.6 24.3 %collective-permute-start.48 = (bf16[144,1792]{1,0:T(8,128)(2,1)S(1)}, bf16[144,1792]{1,0:T(8,128)(2,1)S(1)}, u32[]{:S(2)}, u32[]{:S(2)}) collective-permute-start(bf16[144,1792]{1,0:T(8,128)(2,1)S(1)} %get-tuple-element.162), channel_id=1, source_target_pairs={{0,8},{2,6},{8,16},{10,2},{16,24},{18,10},{24,28},{26,18},{28,20},... | collective-permute-start | bytes 1548296 | tf_op jit(solution)/shard_map/ppermute | solution.py:376
  326.3 12.1 %collective-permute-start.45 = (bf16[256,1152]{1,0:T(8,128)(2,1)S(1)}, bf16[256,1152]{1,0:T(8,128)(2,1)S(1)}, u32[]{:S(2)}, u32[]{:S(2)}) collective-permute-start(bf16[256,1152]{1,0:T(8,128)(2,1)S(1)} %get-tuple-element.170), channel_id=1, source_target_pairs={{0,2},{2,0},{1,3},{3,1},{4,6},{6,4},{5,7},{7,5},{8,10},{10,8},{9,1... | collective-permute-start | bytes 1769480 | tf_op jit(solution)/shard_map/ppermute | solution.py:325
  326.4 32.9 %collective-permute-start.47 = (bf16[256,1152]{1,0:T(8,128)(2,1)}, bf16[256,1152]{1,0:T(8,128)(2,1)}, u32[]{:S(2)}, u32[]{:S(2)}) collective-permute-start(bf16[256,1152]{1,0:T(8,128)(2,1)} %get-tuple-element.172), channel_id=1, source_target_pairs={{0,2},{2,0},{1,3},{3,1},{4,6},{6,4},{5,7},{7,5},{8,10},{10,8},{9,1... | collective-permute-start | bytes 1769480 | tf_op jit(solution)/shard_map/ppermute | solution.py:325
  327.0 12.9 %collective-permute-start.49 = (bf16[144,1792]{1,0:T(8,128)(2,1)S(1)}, bf16[144,1792]{1,0:T(8,128)(2,1)S(1)}, u32[]{:S(2)}, u32[]{:S(2)}) collective-permute-start(bf16[144,1792]{1,0:T(8,128)(2,1)S(1)} %add_convert_fusion.21), channel_id=1, source_target_pairs={{0,8},{2,6},{8,16},{10,2},{16,24},{18,10},{24,28},{26,18},{28,20},... | collective-permute-start | bytes 1548296 | tf_op jit(solution)/shard_map/ppermute | solution.py:376
  336.8 19.3 %collective-permute-start.59 = (bf16[144,1792]{1,0:T(8,128)(2,1)}, bf16[144,1792]{1,0:T(8,128)(2,1)}, u32[]{:S(2)}, u32[]{:S(2)}) collective-permute-start(bf16[144,1792]{1,0:T(8,128)(2,1)} %get-tuple-element.178), channel_id=1, source_target_pairs={{0,8},{2,6},{8,16},{10,2},{16,24},{18,10},{24,28},{26,18},{28,20},... | collective-permute-start | bytes 1548296 | tf_op jit(solution)/shard_map/ppermute | solution.py:376
  339.4 19.9 %collective-permute-start.46 = (bf16[256,1152]{1,0:T(8,128)(2,1)}, bf16[256,1152]{1,0:T(8,128)(2,1)}, u32[]{:S(2)}, u32[]{:S(2)}) collective-permute-start(bf16[256,1152]{1,0:T(8,128)(2,1)} %add_convert_fusion.1), channel_id=1, source_target_pairs={{0,1},{1,0},{2,3},{3,2},{4,5},{5,4},{6,7},{7,6},{8,9},{9,8},{10,11... | collective-permute-start | bytes 1769480 | tf_op jit(solution)/shard_map/ppermute | solution.py:325
  340.8 25.6 %collective-permute-start.58 = (bf16[144,1792]{1,0:T(8,128)(2,1)}, bf16[144,1792]{1,0:T(8,128)(2,1)}, u32[]{:S(2)}, u32[]{:S(2)}) collective-permute-start(bf16[144,1792]{1,0:T(8,128)(2,1)} %add_convert_fusion.20), channel_id=1, source_target_pairs={{0,8},{2,6},{8,16},{10,2},{16,24},{18,10},{24,28},{26,18},{28,20},... | collective-permute-start | bytes 1548296 | tf_op jit(solution)/shard_map/ppermute | solution.py:376
  355.7 13.9 %collective-permute-start.57 = (bf16[144,1792]{1,0:T(8,128)(2,1)}, bf16[144,1792]{1,0:T(8,128)(2,1)}, u32[]{:S(2)}, u32[]{:S(2)}) collective-permute-start(bf16[144,1792]{1,0:T(8,128)(2,1)} %get-tuple-element.203), channel_id=1, source_target_pairs={{0,8},{2,6},{8,16},{10,2},{16,24},{18,10},{24,28},{26,18},{28,20},... | collective-permute-start | bytes 1548296 | tf_op jit(solution)/shard_map/ppermute | solution.py:376
  358.6 13.8 %collective-permute-start.62 = (bf16[144,1792]{1,0:T(8,128)(2,1)}, bf16[144,1792]{1,0:T(8,128)(2,1)}, u32[]{:S(2)}, u32[]{:S(2)}) collective-permute-start(bf16[144,1792]{1,0:T(8,128)(2,1)} %add_convert_fusion.17), channel_id=1, source_target_pairs={{0,8},{2,6},{8,16},{10,2},{16,24},{18,10},{24,28},{26,18},{28,20},... | collective-permute-start | bytes 1548296 | tf_op jit(solution)/shard_map/ppermute | solution.py:376
  363.4 14.1 %collective-permute-start.51 = (bf16[256,1152]{1,0:T(8,128)(2,1)S(1)}, bf16[256,1152]{1,0:T(8,128)(2,1)S(1)}, u32[]{:S(2)}, u32[]{:S(2)}) collective-permute-start(bf16[256,1152]{1,0:T(8,128)(2,1)S(1)} %get-tuple-element.187.refs_0_.refs_5_), channel_id=1, source_target_pairs={{0,1},{1,0},{2,3},{3,2},{4,5},{5,4},{6,7},{7,6},{8,9},{9,8},{10,11... | collective-permute-start | bytes 1769480 | tf_op jit(solution)/shard_map/ppermute | solution.py:325
  365.0 25.9 %collective-permute-start.50 = (bf16[256,1152]{1,0:T(8,128)(2,1)S(1)}, bf16[256,1152]{1,0:T(8,128)(2,1)S(1)}, u32[]{:S(2)}, u32[]{:S(2)}) collective-permute-start(bf16[256,1152]{1,0:T(8,128)(2,1)S(1)} %get-tuple-element.187.refs_0_.refs_5_), channel_id=1, source_target_pairs={{0,2},{2,0},{1,3},{3,1},{4,6},{6,4},{5,7},{7,5},{8,10},{10,8},{9,1... | collective-permute-start | bytes 1769480 | tf_op jit(solution)/shard_map/ppermute | solution.py:325
  373.7 14.2 %collective-permute-start.65 = (bf16[144,1792]{1,0:T(8,128)(2,1)S(1)}, bf16[144,1792]{1,0:T(8,128)(2,1)S(1)}, u32[]{:S(2)}, u32[]{:S(2)}) collective-permute-start(bf16[144,1792]{1,0:T(8,128)(2,1)S(1)} %add_convert_fusion.14), channel_id=1, source_target_pairs={{0,8},{2,6},{8,16},{10,2},{16,24},{18,10},{24,28},{26,18},{28,20},... | collective-permute-start | bytes 1548296 | tf_op jit(solution)/shard_map/ppermute | solution.py:376
  377.5 13.3 %collective-permute-start.52 = (bf16[256,1152]{1,0:T(8,128)(2,1)S(1)}, bf16[256,1152]{1,0:T(8,128)(2,1)S(1)}, u32[]{:S(2)}, u32[]{:S(2)}) collective-permute-start(bf16[256,1152]{1,0:T(8,128)(2,1)S(1)} %collective-permute-done.51.refs_2_.refs_7_), channel_id=1, source_target_pairs={{0,2},{2,0},{1,3},{3,1},{4,6},{6,4},{5,7},{7,5},{8,10},{10,8},{9,1... | collective-permute-start | bytes 1769480 | tf_op jit(solution)/shard_map/ppermute | solution.py:325
  378.6 43.5 %collective-permute-start.64 = (bf16[144,1792]{1,0:T(8,128)(2,1)}, bf16[144,1792]{1,0:T(8,128)(2,1)}, u32[]{:S(2)}, u32[]{:S(2)}) collective-permute-start(bf16[144,1792]{1,0:T(8,128)(2,1)} %add_convert_fusion.15), channel_id=1, source_target_pairs={{0,8},{2,6},{8,16},{10,2},{16,24},{18,10},{24,28},{26,18},{28,20},... | collective-permute-start | bytes 1548296 | tf_op jit(solution)/shard_map/ppermute | solution.py:376
  383.3 40.2 %collective-permute-start.63 = (bf16[144,1792]{1,0:T(8,128)(2,1)}, bf16[144,1792]{1,0:T(8,128)(2,1)}, u32[]{:S(2)}, u32[]{:S(2)}) collective-permute-start(bf16[144,1792]{1,0:T(8,128)(2,1)} %add_convert_fusion.16), channel_id=1, source_target_pairs={{0,8},{2,6},{8,16},{10,2},{16,24},{18,10},{24,28},{26,18},{28,20},... | collective-permute-start | bytes 1548296 | tf_op jit(solution)/shard_map/ppermute | solution.py:376
  388.8 40.2 %collective-permute-start.67 = (bf16[144,1792]{1,0:T(8,128)(2,1)}, bf16[144,1792]{1,0:T(8,128)(2,1)}, u32[]{:S(2)}, u32[]{:S(2)}) collective-permute-start(bf16[144,1792]{1,0:T(8,128)(2,1)} %add_convert_fusion.11), channel_id=1, source_target_pairs={{0,8},{2,6},{8,16},{10,2},{16,24},{18,10},{24,28},{26,18},{28,20},... | collective-permute-start | bytes 1548296 | tf_op jit(solution)/shard_map/ppermute | solution.py:376
  404.0 39.1 %collective-permute-start.53 = (bf16[256,1152]{1,0:T(8,128)(2,1)}, bf16[256,1152]{1,0:T(8,128)(2,1)}, u32[]{:S(2)}, u32[]{:S(2)}) collective-permute-start(bf16[256,1152]{1,0:T(8,128)(2,1)} %get-tuple-element.194), channel_id=1, source_target_pairs={{0,2},{2,0},{1,3},{3,1},{4,6},{6,4},{5,7},{7,5},{8,10},{10,8},{9,1... | collective-permute-start | bytes 1769480 | tf_op jit(solution)/shard_map/ppermute | solution.py:325
  422.1 30.3 %collective-permute-start.55 = (bf16[256,1152]{1,0:T(8,128)(2,1)}, bf16[256,1152]{1,0:T(8,128)(2,1)S(1)}, u32[]{:S(2)}, u32[]{:S(2)}) collective-permute-start(bf16[256,1152]{1,0:T(8,128)(2,1)} %copy-done.109), channel_id=1, source_target_pairs={{0,2},{2,0},{1,3},{3,1},{4,6},{6,4},{5,7},{7,5},{8,10},{10,8},{9,1... | collective-permute-start | bytes 1769480 | tf_op jit(solution)/shard_map/ppermute | solution.py:325
  423.5 21.5 %collective-permute-start.68 = (bf16[144,1792]{1,0:T(8,128)(2,1)S(1)}, bf16[144,1792]{1,0:T(8,128)(2,1)S(1)}, u32[]{:S(2)}, u32[]{:S(2)}) collective-permute-start(bf16[144,1792]{1,0:T(8,128)(2,1)S(1)} %add_convert_fusion.12), channel_id=1, source_target_pairs={{0,8},{2,6},{8,16},{10,2},{16,24},{18,10},{24,28},{26,18},{28,20},... | collective-permute-start | bytes 1548296 | tf_op jit(solution)/shard_map/ppermute | solution.py:376
  426.7 34.1 %collective-permute-start.70 = (bf16[144,1792]{1,0:T(8,128)(2,1)}, bf16[144,1792]{1,0:T(8,128)(2,1)}, u32[]{:S(2)}, u32[]{:S(2)}) collective-permute-start(bf16[144,1792]{1,0:T(8,128)(2,1)} %add_convert_fusion.13), channel_id=1, source_target_pairs={{0,8},{2,6},{8,16},{10,2},{16,24},{18,10},{24,28},{26,18},{28,20},... | collective-permute-start | bytes 1548296 | tf_op jit(solution)/shard_map/ppermute | solution.py:376
  429.0 12.3 %collective-permute-start.66 = (bf16[144,1024]{1,0:T(8,128)(2,1)S(1)}, bf16[144,1024]{1,0:T(8,128)(2,1)S(1)}, u32[]{:S(2)}, u32[]{:S(2)}) collective-permute-start(bf16[144,1024]{1,0:T(8,128)(2,1)S(1)} %add_convert_fusion.27), channel_id=1, source_target_pairs={{0,8},{2,6},{8,16},{10,2},{16,24},{18,10},{24,28},{26,18},{28,20},... | collective-permute-start | bytes 884744 | tf_op jit(solution)/shard_map/ppermute | solution.py:376
  444.4 14.5 %collective-permute-start.54 = (bf16[256,1152]{1,0:T(8,128)(2,1)S(1)}, bf16[256,1152]{1,0:T(8,128)(2,1)S(1)}, u32[]{:S(2)}, u32[]{:S(2)}) collective-permute-start(bf16[256,1152]{1,0:T(8,128)(2,1)S(1)} %add_convert_fusion), channel_id=1, source_target_pairs={{0,1},{1,0},{2,3},{3,2},{4,5},{5,4},{6,7},{7,6},{8,9},{9,8},{10,11... | collective-permute-start | bytes 1769480 | tf_op jit(solution)/shard_map/ppermute | solution.py:325
  445.9 26.8 %collective-permute-start.89 = (bf16[144,1792]{1,0:T(8,128)(2,1)}, bf16[144,1792]{1,0:T(8,128)(2,1)}, u32[]{:S(2)}, u32[]{:S(2)}) collective-permute-start(bf16[144,1792]{1,0:T(8,128)(2,1)} %add_convert_fusion.9), channel_id=1, source_target_pairs={{0,8},{2,6},{8,16},{10,2},{16,24},{18,10},{24,28},{26,18},{28,20},... | collective-permute-start | bytes 1548296 | tf_op jit(solution)/shard_map/ppermute | solution.py:376
  451.3 23.7 %collective-permute-start.74 = (bf16[144,1792]{1,0:T(8,128)(2,1)}, bf16[144,1792]{1,0:T(8,128)(2,1)}, u32[]{:S(2)}, u32[]{:S(2)}) collective-permute-start(bf16[144,1792]{1,0:T(8,128)(2,1)} %add_convert_fusion.7), channel_id=1, source_target_pairs={{0,8},{2,6},{8,16},{10,2},{16,24},{18,10},{24,28},{26,18},{28,20},... | collective-permute-start | bytes 1548296 | tf_op jit(solution)/shard_map/ppermute | solution.py:376
  452.4 12.3 %collective-permute-start.69 = (bf16[144,1024]{1,0:T(8,128)(2,1)}, bf16[144,1024]{1,0:T(8,128)(2,1)S(1)}, u32[]{:S(2)}, u32[]{:S(2)}) collective-permute-start(bf16[144,1024]{1,0:T(8,128)(2,1)} %add_convert_fusion.26), channel_id=1, source_target_pairs={{0,8},{2,6},{8,16},{10,2},{16,24},{18,10},{24,28},{26,18},{28,20},... | collective-permute-start | bytes 884744 | tf_op jit(solution)/shard_map/ppermute | solution.py:376
  466.4 19.9 %collective-permute-start.73 = (bf16[144,1792]{1,0:T(8,128)(2,1)}, bf16[144,1792]{1,0:T(8,128)(2,1)S(1)}, u32[]{:S(2)}, u32[]{:S(2)}) collective-permute-start(bf16[144,1792]{1,0:T(8,128)(2,1)} %add_convert_fusion.8), channel_id=1, source_target_pairs={{0,8},{2,6},{8,16},{10,2},{16,24},{18,10},{24,28},{26,18},{28,20},... | collective-permute-start | bytes 1548296 | tf_op jit(solution)/shard_map/ppermute | solution.py:376
  467.4 17.9 %collective-permute-start.72 = (bf16[144,1024]{1,0:T(8,128)(2,1)}, bf16[144,1024]{1,0:T(8,128)(2,1)}, u32[]{:S(2)}, u32[]{:S(2)}) collective-permute-start(bf16[144,1024]{1,0:T(8,128)(2,1)} %add_convert_fusion.25), channel_id=1, source_target_pairs={{0,8},{2,6},{8,16},{10,2},{16,24},{18,10},{24,28},{26,18},{28,20},... | collective-permute-start | bytes 884744 | tf_op jit(solution)/shard_map/ppermute | solution.py:376
  477.0 13.1 %collective-permute-start.85 = (bf16[144,1792]{1,0:T(8,128)(2,1)}, bf16[144,1792]{1,0:T(8,128)(2,1)}, u32[]{:S(2)}, u32[]{:S(2)}) collective-permute-start(bf16[144,1792]{1,0:T(8,128)(2,1)} %add_convert_fusion.5), channel_id=1, source_target_pairs={{0,8},{2,6},{8,16},{10,2},{16,24},{18,10},{24,28},{26,18},{28,20},... | collective-permute-start | bytes 1548296 | tf_op jit(solution)/shard_map/ppermute | solution.py:376
  479.8 33.9 %all-to-all-start.4 = ((bf16[8,32,1152]{2,1,0:T(8,128)(2,1)}), bf16[8,32,1152]{2,1,0:T(8,128)(2,1)S(1)}, u32[]{:S(2)}, u32[]{:S(2)}) async-start(bf16[8,32,1152]{2,1,0:T(8,128)(2,1)} %bitcast.82), calls=%async_computation.4 | async-start | bytes 1179648 | tf_op jit(solution)/shard_map/all_to_all | solution.py:476
  486.5 17.6 %collective-permute-start.76 = (bf16[144,1792]{1,0:T(8,128)(2,1)S(1)}, bf16[144,1792]{1,0:T(8,128)(2,1)S(1)}, u32[]{:S(2)}, u32[]{:S(2)}) collective-permute-start(bf16[144,1792]{1,0:T(8,128)(2,1)S(1)} %add_convert_fusion.6), channel_id=1, source_target_pairs={{0,8},{2,6},{8,16},{10,2},{16,24},{18,10},{24,28},{26,18},{28,20},... | collective-permute-start | bytes 1548296 | tf_op jit(solution)/shard_map/ppermute | solution.py:376
  488.6 15.4 %collective-permute-start.75 = (bf16[144,1024]{1,0:T(8,128)(2,1)S(1)}, bf16[144,1024]{1,0:T(8,128)(2,1)S(1)}, u32[]{:S(2)}, u32[]{:S(2)}) collective-permute-start(bf16[144,1024]{1,0:T(8,128)(2,1)S(1)} %add_convert_fusion.24), channel_id=1, source_target_pairs={{0,8},{2,6},{8,16},{10,2},{16,24},{18,10},{24,28},{26,18},{28,20},... | collective-permute-start | bytes 884744 | tf_op jit(solution)/shard_map/ppermute | solution.py:376
  505.0 23.3 %collective-permute-start.87 = (bf16[144,1792]{1,0:T(8,128)(2,1)}, bf16[144,1792]{1,0:T(8,128)(2,1)}, u32[]{:S(2)}, u32[]{:S(2)}) collective-permute-start(bf16[144,1792]{1,0:T(8,128)(2,1)} %add_convert_fusion.4), channel_id=1, source_target_pairs={{0,8},{2,6},{8,16},{10,2},{16,24},{18,10},{24,28},{26,18},{28,20},... | collective-permute-start | bytes 1548296 | tf_op jit(solution)/shard_map/ppermute | solution.py:376
  513.2 12.6 %collective-permute-start.86 = (f32[72,1728]{1,0:T(8,128)}, f32[72,1728]{1,0:T(8,128)}, u32[]{:S(2)}, u32[]{:S(2)}) collective-permute-start(f32[72,1728]{1,0:T(8,128)} %get-tuple-element.275), channel_id=1, source_target_pairs={{0,2},{2,0},{1,3},{3,1},{4,6},{6,4},{5,7},{7,5},{8,10},{10,8},{9,1... | collective-permute-start | bytes 1493000 | tf_op jit(solution)/shard_map/ppermute | solution.py:325
  (157 other events, 1978.6 us)
